TPU v7x, 32 devices: a whole 2x2x4 slice. The times are simulated.
32 devices in a mesh: dp: 4 (over x, core), fsdp: 4 (over z), ctx: 2 (over y).
Axes of the slice: x: 2, y: 2, z: 4, core: 2. Of those that a mesh axis runs over, the one named last changes fastest.
Arguments:
- x_in: bfloat16 [16, 1024, 2048], P(('dp', 'fsdp'), 'ctx'), may hold values from -6 to 6
- span_order: int32 [16, 2], P(('dp', 'fsdp')), may hold values from 0 to 1, each once within a row
- attn_gain: bfloat16 [2048], P(('fsdp', 'ctx')), may hold values from 0.25 to 1.75
- w_qkv: bfloat16 [2048, 3072], P(('fsdp', 'ctx')), may hold values from -0.125 to 0.125
- w_out: bfloat16 [2048, 2048], P(('fsdp', 'ctx')), may hold values from -1 to 1
- ffn_gain: bfloat16 [2048], P(('fsdp', 'ctx')), may hold values from 0.25 to 1.75
- w_gate_up: bfloat16 [2048, 16384], P(('fsdp', 'ctx')), may hold values from -0.125 to 0.125
- w_down: bfloat16 [2048, 8192], P(('fsdp', 'ctx')), may hold values from -0.0625 to 0.0625
- cotangent: bfloat16 [16, 1024, 2048], P(('dp', 'fsdp'), 'ctx'), may hold values from -6 to 6
Outputs:
- y_out: bfloat16 [16, 1024, 2048], P(('dp', 'fsdp'), 'ctx')
- grad_input: float32 [16, 1024, 2048], P(('dp', 'fsdp'), 'ctx')
- grad_attn_gain: float32 [2048], P(('fsdp', 'ctx'))
- grad_qkv: float32 [2048, 3072], P(('fsdp', 'ctx'))
- grad_out: float32 [2048, 2048], P(('fsdp', 'ctx'))
- grad_ffn_gain: float32 [2048], P(('fsdp', 'ctx'))
- grad_gate_up: float32 [2048, 16384], P(('fsdp', 'ctx'))
- grad_down: float32 [2048, 8192], P(('fsdp', 'ctx'))
Inputs may be any that keep to these rules, and one draw needn't show every extreme that they name: Each row is a permutation; device c of ctx holds positions span_order[s, c] * 512 to span_order[s, c] * 512 + 511 of sequence s.
All inputs are finite; a program needn't handle non-finite values.
Results may differ from a plain program's by a relative error of at most 0.02.
Values may be sent and summed in bfloat16 or wider, within the bound.
A program may use at most 832 MiB of HBM per device.

v0:
```python
import math

import jax
import jax.numpy as jnp
from jax import lax
from jax.sharding import PartitionSpec as P

HEADS = 32
KV_HEADS = 8
HD = 64


EPS = 1e-05


def rotate(tensor, positions):
    half = tensor.shape[-1] // 2
    freq = jnp.exp(jnp.arange(half, dtype=jnp.float32) * (-math.log(500000.0) / half))
    angle = positions[:, None] * freq[None, :]
    cosine = jnp.concatenate([jnp.cos(angle), jnp.cos(angle)], -1)[:, None, :]
    sine = jnp.concatenate([jnp.sin(angle), jnp.sin(angle)], -1)[:, None, :]
    turned = jnp.concatenate([-tensor[..., half:], tensor[..., :half]], -1)
    return tensor * cosine + turned * sine


def normalize(rows, gain):
    return rows * lax.rsqrt(jnp.mean(rows * rows, -1, keepdims=True) + EPS) * gain


def matmul(left, right):
    return jnp.dot(left, right, preferred_element_type=jnp.float32)


def matmul_rows(left, right):
    return lax.dot_general(
        left, right, (((1,), (1,)), ((), ())), preferred_element_type=jnp.float32
    )


def matmul_tokens(left, right):
    return lax.dot_general(
        left, right, (((0,), (0,)), ((), ())), preferred_element_type=jnp.float32
    )


def norm_fold_step(unit, pieces):
    piece_gain = pieces[1].astype(jnp.float32)
    low_part = (unit * piece_gain[None, :]).astype(jnp.bfloat16)
    total = matmul(low_part, pieces[0])
    return (total, low_part, piece_gain)


def left_fold_step(left, piece):
    return matmul(left, piece)


def shards(x_in, span_order, attn_gain, w_qkv, w_out, ffn_gain, w_gate_up, w_down, cotangent):
    width = x_in.shape[-1]
    tokens = x_in.reshape(-1, width)
    span = tokens.shape[0]
    rank = lax.axis_index("ctx")
    qwidth = HEADS * HD
    kvwidth = KV_HEADS * HD
    ratio = HEADS // KV_HEADS
    ffwidth = w_down.shape[1]
    scale = HD ** (-0.5)
    order = span_order.reshape(-1)
    offsets = jnp.arange(span, dtype=jnp.int32)
    key_pos = (order[:, None] * span + offsets[None, :]).reshape(-1)
    query_pos = lax.dynamic_slice_in_dim(key_pos, rank * span, span)
    causal = query_pos[:, None] >= key_pos[None, :]
    query_angle = query_pos.astype(jnp.float32)
    inputs = tokens.astype(jnp.float32)
    unit_one = inputs * lax.rsqrt(jnp.mean(inputs * inputs, -1, keepdims=True) + EPS)
    qkv, normed_one, gain_one = norm_fold_step(
        unit_one,
        (
            lax.all_gather(w_qkv, ("fsdp", "ctx"), axis=0, tiled=True),
            lax.all_gather(attn_gain, ("fsdp", "ctx"), axis=0, tiled=True),
        ),
    )
    query_raw = qkv[:, :qwidth].reshape(span, HEADS, HD)
    key_raw = qkv[:, qwidth : qwidth + kvwidth].reshape(span, KV_HEADS, HD)
    query = rotate(query_raw, query_angle).astype(jnp.bfloat16)
    keys = rotate(key_raw, query_angle).astype(jnp.bfloat16).reshape(span, kvwidth)
    values = qkv[:, qwidth + kvwidth :].astype(jnp.bfloat16)
    all_keys, all_values = (
        lax.all_gather(keys, "ctx", axis=0, tiled=True),
        lax.all_gather(values, "ctx", axis=0, tiled=True),
    )
    length = all_keys.shape[0]
    grouped = jnp.transpose(query.reshape(span, KV_HEADS, ratio, HD), (1, 0, 2, 3))
    key_heads = jnp.transpose(all_keys.reshape(length, KV_HEADS, HD), (1, 0, 2))
    value_heads = jnp.transpose(all_values.reshape(length, KV_HEADS, HD), (1, 0, 2))

    def head_forward(operands):
        qhead, khead, vhead = operands
        scores = jnp.einsum("crd,ld->rcl", qhead, khead, preferred_element_type=jnp.float32) * scale
        scores = jnp.where(causal[None], scores, -1e30)
        peak = jnp.max(scores, -1, keepdims=True)
        expd = jnp.exp(scores - peak)
        total = jnp.sum(expd, -1, keepdims=True)
        probs = (expd / total).astype(jnp.bfloat16)
        result = jnp.einsum("rcl,ld->crd", probs, vhead, preferred_element_type=jnp.float32)
        return (result.astype(jnp.bfloat16), (peak + jnp.log(total))[..., 0])

    head_outs, logsum = lax.map(head_forward, (grouped, key_heads, value_heads))
    attn_low = jnp.transpose(head_outs, (1, 0, 2, 3)).reshape(span, qwidth)
    proj = left_fold_step(attn_low, lax.all_gather(w_out, ("fsdp", "ctx"), axis=0, tiled=True))
    hidden_one = inputs + proj
    unit_two = hidden_one * lax.rsqrt(jnp.mean(hidden_one * hidden_one, -1, keepdims=True) + EPS)
    gate_up, normed_two, gain_two = norm_fold_step(
        unit_two,
        (
            lax.all_gather(w_gate_up, ("fsdp", "ctx"), axis=0, tiled=True),
            lax.all_gather(ffn_gain, ("fsdp", "ctx"), axis=0, tiled=True),
        ),
    )
    gate = gate_up[:, :ffwidth]
    up = gate_up[:, ffwidth:]
    inner = (jax.nn.silu(gate) * up).astype(jnp.bfloat16)
    ffn_result = matmul_rows(inner, lax.all_gather(w_down, ("fsdp", "ctx"), axis=0, tiled=True))
    y_out = (hidden_one + ffn_result).astype(jnp.bfloat16)
    grad_y = cotangent.reshape(span, width)
    d_inner = left_fold_step(grad_y, lax.all_gather(w_down, ("fsdp", "ctx"), axis=0, tiled=True))
    _, pull_inner = jax.vjp(lambda first, second: jax.nn.silu(first) * second, gate, up)
    d_gate, d_up = pull_inner(d_inner)
    d_gate_up = jnp.concatenate([d_gate, d_up], 1).astype(jnp.bfloat16)
    d_normed_two = matmul_rows(
        d_gate_up, lax.all_gather(w_gate_up, ("fsdp", "ctx"), axis=0, tiled=True)
    )
    _, pull_two = jax.vjp(normalize, hidden_one, gain_two)
    d_hidden_norm, d_gain_two = pull_two(d_normed_two)
    d_hidden = grad_y.astype(jnp.float32) + d_hidden_norm
    d_proj = d_hidden.astype(jnp.bfloat16)
    d_attn = matmul_rows(d_proj, lax.all_gather(w_out, ("fsdp", "ctx"), axis=0, tiled=True))
    d_attn_heads = jnp.transpose(
        d_attn.astype(jnp.bfloat16).reshape(span, KV_HEADS, ratio, HD), (1, 0, 2, 3)
    )

    def head_backward(operands):
        qhead, khead, vhead, dhead, lse_head = operands
        scores = jnp.einsum("crd,ld->rcl", qhead, khead, preferred_element_type=jnp.float32) * scale
        scores = jnp.where(causal[None], scores, -1e30)
        probs = jnp.exp(scores - lse_head[..., None])
        d_probs = jnp.einsum("crd,ld->rcl", dhead, vhead, preferred_element_type=jnp.float32)
        delta = jnp.sum(probs * d_probs, -1, keepdims=True)
        d_scores = (probs * (d_probs - delta)).astype(jnp.bfloat16)
        d_query = (
            jnp.einsum("rcl,ld->crd", d_scores, khead, preferred_element_type=jnp.float32) * scale
        )
        d_key = (
            jnp.einsum("rcl,crd->ld", d_scores, qhead, preferred_element_type=jnp.float32) * scale
        )
        d_value = jnp.einsum(
            "rcl,crd->ld", probs.astype(jnp.bfloat16), dhead, preferred_element_type=jnp.float32
        )
        return (d_query, d_key, d_value)

    d_query, d_key, d_value = lax.map(
        head_backward, (grouped, key_heads, value_heads, d_attn_heads, logsum)
    )
    d_key = jnp.transpose(d_key, (1, 0, 2)).reshape(length, kvwidth)
    d_value = jnp.transpose(d_value, (1, 0, 2)).reshape(length, kvwidth)
    d_key_mine, d_value_mine = (
        lax.psum_scatter(d_key.astype(jnp.bfloat16), "ctx", scatter_dimension=0, tiled=True).astype(
            jnp.float32
        ),
        lax.psum_scatter(
            d_value.astype(jnp.bfloat16), "ctx", scatter_dimension=0, tiled=True
        ).astype(jnp.float32),
    )
    d_query = jnp.transpose(d_query, (1, 0, 2, 3)).reshape(span, HEADS, HD)
    _, pull_query = jax.vjp(lambda tensor: rotate(tensor, query_angle), query_raw)
    _, pull_key = jax.vjp(lambda tensor: rotate(tensor, query_angle), key_raw)
    d_query_raw = pull_query(d_query)[0].reshape(span, qwidth)
    d_key_raw = pull_key(d_key_mine.reshape(span, KV_HEADS, HD))[0].reshape(span, kvwidth)
    d_qkv = jnp.concatenate([d_query_raw, d_key_raw, d_value_mine], 1).astype(jnp.bfloat16)
    d_normed_one = matmul_rows(d_qkv, lax.all_gather(w_qkv, ("fsdp", "ctx"), axis=0, tiled=True))
    _, pull_one = jax.vjp(normalize, inputs, gain_one)
    d_input_norm, d_gain_one = pull_one(d_normed_one)
    grad_input = d_hidden + d_input_norm
    lefts = (normed_one, attn_low, normed_two, grad_y)

    def outer(left, right):
        return matmul_tokens(left, right)

    shard_grads = lax.psum_scatter(
        jnp.concatenate(
            [
                outer(lefts[0], d_qkv),
                outer(lefts[1], d_proj),
                outer(lefts[2], d_gate_up),
                outer(lefts[3], inner),
            ],
            1,
        ).astype(jnp.bfloat16),
        ("fsdp", "ctx"),
        scatter_dimension=0,
        tiled=True,
    ).astype(jnp.float32)
    gain_one_part, gain_two_part = (
        lax.psum_scatter(d_gain_one, ("fsdp", "ctx"), scatter_dimension=0, tiled=True),
        lax.psum_scatter(d_gain_two, ("fsdp", "ctx"), scatter_dimension=0, tiled=True),
    )
    shard_grads, gain_one_part, gain_two_part = (
        lax.psum(shard_grads.astype(jnp.bfloat16), "dp").astype(jnp.float32),
        lax.psum(gain_one_part.astype(jnp.bfloat16), "dp").astype(jnp.float32),
        lax.psum(gain_two_part.astype(jnp.bfloat16), "dp").astype(jnp.float32),
    )
    qkv_cols = w_qkv.shape[1]
    grad_qkv = shard_grads[:, :qkv_cols]
    grad_out = shard_grads[:, qkv_cols : qkv_cols + width]
    grad_gate_up = shard_grads[:, qkv_cols + width : qkv_cols + width + 2 * ffwidth]
    grad_down = shard_grads[:, qkv_cols + width + 2 * ffwidth :]
    return (
        y_out.reshape(x_in.shape),
        grad_input.reshape(x_in.shape),
        gain_one_part,
        grad_qkv,
        grad_out,
        gain_two_part,
        grad_gate_up,
        grad_down,
    )


def solution(mesh):
    in_specs = (
        P(("dp", "fsdp"), "ctx", None),
        P(("dp", "fsdp"), None),
        P(("fsdp", "ctx")),
        P(("fsdp", "ctx"), None),
        P(("fsdp", "ctx"), None),
        P(("fsdp", "ctx")),
        P(("fsdp", "ctx"), None),
        P(("fsdp", "ctx"), None),
        P(("dp", "fsdp"), "ctx", None),
    )
    out_specs = (
        P(("dp", "fsdp"), "ctx", None),
        P(("dp", "fsdp"), "ctx", None),
        P(("fsdp", "ctx")),
        P(("fsdp", "ctx"), None),
        P(("fsdp", "ctx"), None),
        P(("fsdp", "ctx")),
        P(("fsdp", "ctx"), None),
        P(("fsdp", "ctx"), None),
    )
    return jax.shard_map(shards, mesh=mesh, in_specs=in_specs, out_specs=out_specs, check_vma=False)
```

profile of v0, /device:TPU:1, one launch (start us, length us, event | category | flops | bytes accessed | tf_op | source)
XLA Modules:
  0.0 4859.3 jit_solution(16872591110406162582)
XLA Ops:
  8.6 17.9 all-gather
  29.4 158.9 %all-gather.9.cloned.1.call-done = bf16[2048,3072]{1,0:T(8,128)(2,1)} async-done(((bf16[256,3072]{1,0:T(8,128)(2,1)}), bf16[2048,3072]{1,0:T(8,128)(2,1)}) %all-gather.9.cloned.1.call-update) | async-done | bytes 12582928 | tf_op jit(solution)/shard_map/all_gather | solution.py:78
  208.4 14.7 all-gather.1
  247.2 67.6 %while.28 = (s32[]{:T(128)}, bf16[8,512,4,64]{1,3,2,0:T(8,128)(2,1)}, f32[8,4,512]{2,1,0:T(4,128)}, bf16[8,1024,64]{1,2,0:T(8,128)(2,1)}, bf16[8,1024,64]{1,2,0:...) while((s32[]{:T(128)}, ...), condition=%wide.region_4.5_spmd.clone, body=%wide.region_1.4_spmd.clone.sunk | while | flops 562690048 | bytes 28123240 | solution.py:107
  314.8 57.5 %all-gather.15.cloned.1.call-done = bf16[2048,2048]{1,0:T(8,128)(2,1)} async-done(((bf16[256,2048]{1,0:T(8,128)(2,1)}), bf16[2048,2048]{1,0:T(8,128)(2,1)}) %all-gather.15.cloned.1.call-update) | async-done | bytes 8388624 | tf_op jit(solution)/shard_map/all_gather | solution.py:109
  372.3 11.4 multiply_reduce_fusion.2
  383.7 1255.5 %all-gather.17.cloned.1.call-done = bf16[2048,16384]{1,0:T(8,128)(2,1)} async-done(((bf16[256,16384]{1,0:T(8,128)(2,1)}), bf16[2048,16384]{1,0:T(8,128)(2,1)}) %all-gather.17.cloned.1.call-update) | async-done | bytes 67108880 | tf_op jit(solution)/shard_map/all_gather | solution.py:115
  1639.2 46.1 fusion.103
  1685.3 593.0 %all-gather.19.cloned.1.call-done = bf16[2048,8192]{1,0:T(8,128)(2,1)} async-done(((bf16[256,8192]{1,0:T(8,128)(2,1)}), bf16[2048,8192]{1,0:T(8,128)(2,1)}) %all-gather.19.cloned.1.call-update) | async-done | bytes 33554448 | tf_op jit(solution)/shard_map/all_gather | solution.py:122
  2278.3 36.5 fusion.66
  2314.8 44.5 convolution_convert_fusion
  2359.3 48.8 %multiply_reduce_fusion = (f32[2048]{0:T(1024)}, f32[512]{0:T(512)S(1)}, f32[512,2048]{1,0:T(8,128)}) fusion(f32[512,2048]{1,0:T(8,128)} %get-tuple-element.217, f32[512]{0:T(512)S(1)} %fusion.98, f32[2048]{0:T(1024)S(1)} %bitcast.282, bf16[2048,16384]{1,0:T(8,128)(2,1)} %all-gather.17.cloned.1.call-done, bf16[512,8192]{1,0:T(8,128)(2,1)} %get-tuple-element.204, ...), kind=kOutput, calls=%fused_computation.108 | convolution fusion | flops 34399584256 | bytes 92295168 | tf_op jit(solution)/shard_map/dot_general | solution.py:35
  2423.6 146.3 %while.29 = (s32[]{:T(128)}, f32[8,512,4,64]{1,3,2,0:T(8,128)}, bf16[8,1024,64]{1,2,0:T(8,128)(2,1)}, bf16[8,1024,64]{1,2,0:T(8,128)(2,1)}, bf16[8,1024,64]{1,2,...) while((s32[]{:T(128)}, f32[8,512,4,64]{1,3,2,0:T(8,128)}, ...), condition=%wide.region_9.10_spmd.clone, body=%wide.region_7.9_spmd.clone.sunk | while | flops 1374353408 | bytes 67570816 | solution.py:160
  2570.1 25.4 convert_bitcast_fusion
  2604.6 12.3 copy.60
  2627.3 12.0 convolution_convert_fusion.1
  2639.2 79.9 %pad_maximum_fusion = bf16[2048,29696]{1,0:T(8,128)(2,1)} fusion(bf16[2048,8192]{1,0:T(8,128)(2,1)} %convert_bitcast_fusion, bf16[2048,16384]{1,0:T(8,128)(2,1)} %convolution_convert_fusion, bf16[2048,2048]{1,0:T(8,128)(2,1)} %copy.60, bf16[2048,3072]{1,0:T(8,128)(2,1)} %convolution_convert_fusion.1), kind=kLoop, calls=%fused_computation.69 | loop fusion | flops 486539264 | bytes 243269632 | tf_op jit(solution)/shard_map/concatenate | solution.py:189
  2719.2 1843.9 %reduce-scatter.10.cloned.1.call-done = bf16[256,29696]{1,0:T(8,128)(2,1)} async-done(((bf16[2048,29696]{1,0:T(8,128)(2,1)}), bf16[256,29696]{1,0:T(8,128)(2,1)}) %reduce-scatter.10.cloned.1.call-update) | async-done | bytes 15204368
  4565.0 26.1 fusion.83
  4591.1 12.4 fusion.72
  4603.5 27.6 all-reduce.7
  4631.2 12.7 all-reduce.8
  4651.5 176.1 %all-reduce.11.cloned.1.call-done = bf16[256,29696]{1,0:T(8,128)(2,1)} async-done(((bf16[256,29696]{1,0:T(8,128)(2,1)}), bf16[256,29696]{1,0:T(8,128)(2,1)}) %all-reduce.11.cloned.1.call-update) | async-done | bytes 15204368 | tf_op jit(solution)/shard_map/psum | solution.py:207
  4833.9 11.5 slice.64
  (245 shorter events, 318.5 us)
Async XLA Ops:
  7.2 181.2 %all-gather.9.cloned.1.call-start = ((), (), s32[]{:S(2)}) async-start(), calls=%async_computation.3 | async-start | bytes 14155776 | tf_op jit(solution)/shard_map/all_gather | solution.py:78
  7.9 230.0 %all-gather.11.cloned.1.call-start = ((), (), s32[]{:S(2)}) async-start(), calls=%async_computation.4 | async-start | bytes 1572864 | tf_op jit(solution)/shard_map/all_gather | solution.py:89
  26.5 171.9 %copy-start.16 = (f32[8,1,256]{2,1,0:T(1,128)}, f32[8,1,256]{2,1,0:T(1,128)S(1)}, u32[]{:S(2)}) copy-start(f32[8,1,256]{2,1,0:T(1,128)S(1)} %convert_element_type.126) | copy-start | bytes 24580
  29.4 169.0 %copy-start.18 = (f32[512]{0:T(512)}, f32[512]{0:T(512)S(1)}, u32[]{:S(2)}) copy-start(f32[512]{0:T(512)S(1)} %fusion.76) | copy-start | bytes 6148
  29.4 169.0 %copy-start.23 = (f32[512]{0:T(512)}, f32[512]{0:T(512)S(1)}, u32[]{:S(2)}) copy-start(f32[512]{0:T(512)S(1)} %fusion.97) | copy-start | bytes 6148
  202.1 43.7 all-gather.13.cloned.1.call-start
  202.5 34.0 copy-start.7
  202.5 34.0 copy-start.9
  206.5 165.8 %all-gather.15.cloned.1.call-start = ((), (), s32[]{:S(2)}) async-start(), calls=%async_computation.6 | async-start | bytes 9437184 | tf_op jit(solution)/shard_map/all_gather | solution.py:109
  207.1 1432.1 %all-gather.17.cloned.1.call-start = ((), (), s32[]{:S(2)}) async-start(), calls=%async_computation.7 | async-start | bytes 75497472 | tf_op jit(solution)/shard_map/all_gather | solution.py:115
  207.7 2070.6 %all-gather.19.cloned.1.call-start = ((), (), s32[]{:S(2)}) async-start(), calls=%async_computation.8 | async-start | bytes 37748736 | tf_op jit(solution)/shard_map/all_gather | solution.py:122
  208.3 2416.2 %reduce-scatter.6.cloned.1.call-start = ((), (), s32[]{:S(2)}) async-start(), calls=%async_computation.9 | async-start | bytes 1572864 | tf_op jit(solution)/shard_map/reduce_scatter | solution.py:166
  314.8 68.9 %copy-start.1 = (bf16[8,512,4,64]{1,3,2,0:T(8,128)(2,1)}, bf16[8,512,4,64]{1,3,2,0:T(8,128)(2,1)S(1)}, u32[]{:S(2)}) copy-start(bf16[8,512,4,64]{1,3,2,0:T(8,128)(2,1)S(1)} %get-tuple-element.420) | copy-start | bytes 6291460
  314.8 68.9 %copy-start.4 = (bf16[8,1024,64]{1,2,0:T(8,128)(2,1)}, bf16[8,1024,64]{1,2,0:T(8,128)(2,1)S(1)}, u32[]{:S(2)}) copy-start(bf16[8,1024,64]{1,2,0:T(8,128)(2,1)S(1)} %get-tuple-element.424) | copy-start | bytes 3145732
  314.8 68.9 %copy-start.12 = (s32[1024]{0:T(1024)}, s32[1024]{0:T(1024)S(1)}, u32[]{:S(2)}) copy-start(s32[1024]{0:T(1024)S(1)} %get-tuple-element.445) | copy-start | bytes 12292
  314.8 68.9 %copy-start.14 = (s32[512]{0:T(512)}, s32[512]{0:T(512)S(1)}, u32[]{:S(2)}) copy-start(s32[512]{0:T(512)S(1)} %get-tuple-element.446) | copy-start | bytes 6148
  383.7 1301.6 %copy-start.20 = (f32[512]{0:T(512)}, f32[512]{0:T(512)S(1)}, u32[]{:S(2)}) copy-start(f32[512]{0:T(512)S(1)} %get-tuple-element.216) | copy-start | bytes 6148
  1639.2 639.1 %copy-start.11 = (bf16[1,512,2048]{2,1,0:T(8,128)(2,1)S(1)}, bf16[1,512,2048]{2,1,0:T(8,128)(2,1)}, u32[]{:S(2)}) copy-start(bf16[1,512,2048]{2,1,0:T(8,128)(2,1)} %param.21) | copy-start | bytes 6291460
  2359.3 48.8 %copy-start.21 = (f32[512]{0:T(512)S(1)}, f32[512]{0:T(512)}, u32[]{:S(2)}) copy-start(f32[512]{0:T(512)} %copy-done.20) | copy-start | bytes 6148
  2570.0 57.2 %reduce-scatter.8.cloned.1.call-start = ((), (), s32[]{:S(2)}) async-start(), calls=%async_computation.10 | async-start | bytes 1572864 | tf_op jit(solution)/shard_map/reduce_scatter | solution.py:169
  2595.5 1967.6 %reduce-scatter.10.cloned.1.call-start = ((), (), s32[]{:S(2)}) async-start(), calls=%async_computation.12 | async-start | bytes 136839168
  2719.2 2108.5 %all-reduce.11.cloned.1.call-start = ((), (), s32[]{:S(2)}) async-start(), calls=%async_computation.11 | async-start | bytes 30408704 | tf_op jit(solution)/shard_map/psum | solution.py:207
  4565.0 26.1 copy-start.26
  4591.1 53.9 %copy-start.19 = (f32[512]{0:T(512)S(1)}, f32[512]{0:T(512)}, u32[]{:S(2)}) copy-start(f32[512]{0:T(512)} %copy-done.18) | copy-start | bytes 6148
  (17 other events, 86.1 us)
Sparse Core Ops, SparseCore 0:
  10.2 178.1 all-gather.8
  202.2 20.0 all-gather.10
  224.4 21.3 all-gather.12
  247.7 124.5 all-gather.14
  373.7 1265.4 all-gather.16
  1640.6 637.6 all-gather.18
  2570.1 20.2 reduce-scatter.5
  2595.6 20.2 reduce-scatter.7
  2719.3 1843.8 reduce-scatter.9
  4565.6 261.9 all-reduce.10
where the time goes:
time: 4870 us; the launch traced here: 4860 us
  waiting for transfers between devices  4090 us (84%)
  matrix products  450 us (9%)
  other arithmetic  157 us (3%)
  blocking collectives  72.8 us (1%)
  local copies, waits for them, and re-layouts  69.9 us (1%)
    unnamed x11, waiting for transfers between devices  1850 us
    all_gather x1, waiting for transfers between devices, shards(): lax.all_gather(w_gate_up, ('fsdp', 'ctx'), axis=0, tiled=True)  1260 us
    all_gather x1, waiting for transfers between devices, shards(): lax.all_gather(w_down, ('fsdp', 'ctx'), axis=0, tiled=True)  593 us
    psum x1, waiting for transfers between devices, shards(): lax.psum(shard_grads.astype(jnp.bfloat16), 'dp').astype(jnp.float32)  176 us
    all_gather x1, waiting for transfers between devices, shards(): lax.all_gather(w_qkv, ('fsdp', 'ctx'), axis=0, tiled=True)  159 us
    dot_general x4, matrix products, matmul(): return jnp.dot(left, right, preferred_element_type=jnp.float32)  104 us
  transfers between devices with their start and end apart: 10, of which 7 were waited for; matrix products, arithmetic and copies ran while one was open for 5% of the time, Pallas kernels for 0%

commit v1 on v0

v1 whole, which is shorter than its diff:
```python
import math

import jax
import jax.numpy as jnp
from jax import lax
from jax.experimental import pallas as pl
from jax.experimental.pallas import tpu as pltpu
from jax.sharding import PartitionSpec as P

HEADS = 32
KV_HEADS = 8
HD = 64
EPS = 1e-05
SUBS = 4

BF = jnp.bfloat16
F32 = jnp.float32
GRID = ("fsdp", "ctx")


def matmul(left, right):
    return jnp.dot(left, right, preferred_element_type=F32)


def matmul_rows(left, right):
    return lax.dot_general(left, right, (((1,), (1,)), ((), ())), preferred_element_type=F32)


def matmul_tokens(left, right):
    return lax.dot_general(left, right, (((0,), (0,)), ((), ())), preferred_element_type=F32)


def rope_tables(positions):
    half = HD // 2
    freq = jnp.exp(jnp.arange(half, dtype=F32) * (-math.log(500000.0) / half))
    angle = positions[:, None] * freq[None, :]
    cosine, sine = jnp.cos(angle), jnp.sin(angle)
    zero = jnp.zeros_like(sine)
    return (
        jnp.concatenate([cosine] * 4, -1),
        jnp.concatenate([-sine, zero] * 2, -1),
        jnp.concatenate([zero, sine] * 2, -1),
    )


def inv_rms(rows):
    return lax.rsqrt(jnp.mean(rows * rows, -1, keepdims=True) + EPS)


def norm_back(rows, scale, gain, grad):
    unit = rows * scale
    pulled = grad * gain[None, :]
    inner = jnp.mean(pulled * unit, -1, keepdims=True)
    return scale * (pulled - unit * inner), jnp.sum(grad * unit, 0)


MIB = 1 << 20
ANY = pl.BlockSpec(memory_space=pl.ANY)
WHOLE = pl.BlockSpec(memory_space=pltpu.VMEM)


def cost(flops, moved, exps=0):
    return pl.CostEstimate(flops=int(flops), bytes_accessed=int(moved), transcendentals=int(exps))


def params(mib):
    return pltpu.CompilerParams(vmem_limit_bytes=mib * MIB)


def dot_nn(a, b):
    return lax.dot_general(a, b, (((1,), (0,)), ((), ())), preferred_element_type=F32)


def dot_nt(a, b):
    return lax.dot_general(a, b, (((1,), (1,)), ((), ())), preferred_element_type=F32)


def dot_tn(a, b):
    return lax.dot_general(a, b, (((0,), (0,)), ((), ())), preferred_element_type=F32)


def reorder(array, places, axis=1, deps=()):
    count = places.shape[0]
    if axis == 1 and (array.shape[1] // count) % 128 != 0:
        size = array.shape[1] // count
        blocks = [lax.dynamic_slice_in_dim(array, places[s] * size, size, 1) for s in range(count)]
        return jnp.concatenate(blocks, 1)
    if axis == 1:
        shape = (array.shape[0], array.shape[1] // count)
        took = lambda s, where: (0, where[s])
        gave = lambda s, where: (0, s)
    else:
        shape = (array.shape[0] // count, array.shape[1])
        took = lambda s, where: (where[s], 0)
        gave = lambda s, where: (s, 0)

    def kernel(where, source, *rest):
        rest[-1][...] = source[...]

    return pl.pallas_call(
        kernel,
        grid_spec=pltpu.PrefetchScalarGridSpec(
            num_scalar_prefetch=1,
            grid=(count,),
            in_specs=[pl.BlockSpec(shape, took)] + [ANY] * len(deps),
            out_specs=pl.BlockSpec(shape, gave),
        ),
        out_shape=jax.ShapeDtypeStruct(array.shape, array.dtype),
        compiler_params=params(16),
        cost_estimate=cost(0, 2 * array.size * array.dtype.itemsize),
    )(places, array, *deps)


def turn(piece, cosine, sine_low, sine_high):
    return (
        piece * cosine
        + pltpu.roll(piece, 128 - HD // 2, axis=1) * sine_low
        + pltpu.roll(piece, HD // 2, axis=1) * sine_high
    )


def head_of(block, group):
    odd = (group // 2) % 2 == 1
    return jnp.where(odd, block[:, HD:], block[:, :HD])


def causal_tile(size):
    key = lax.broadcasted_iota(jnp.int32, (size, size), 0)
    query = lax.broadcasted_iota(jnp.int32, (size, size), 1)
    return key <= query


def scores_of(key, key_far, query, seen, mask, span):
    tile = query.shape[0]
    own = dot_nt(key, query)
    if key.shape[0] > tile:
        last = key.shape[0] - tile
        own = jnp.concatenate([own[:last], jnp.where(mask, own[last:], -1e30)], 0)
    else:
        own = jnp.where(mask, own, -1e30)
    far = dot_nt(key_far, query)
    far = [jnp.where(seen[k], far[k * span : (k + 1) * span], -1e30) for k in range(len(seen))]
    return own, (far[0] if len(far) == 1 else jnp.concatenate(far, 0))


def place_grads(pieces, columns, sub, ffwidth):
    rows = pieces[0].shape[0]
    count = len(pieces)

    def kernel(*refs):
        where = refs[0]
        sources = refs[1 : 1 + count]
        gu_ref, down_ref, took, gave, in_sems, out_sems = refs[1 + count :]

        def read(k):
            return pltpu.make_async_copy(sources[k], took.at[k % 2], in_sems.at[k % 2])

        def writes(k):
            at = pl.multiple_of(where[k], 128)
            here = gave.at[k % 2]
            return (
                pltpu.make_async_copy(
                    here.at[:, pl.ds(0, sub)], gu_ref.at[:, pl.ds(at, sub)], out_sems.at[k % 2, 0]
                ),
                pltpu.make_async_copy(
                    here.at[:, pl.ds(sub, sub)], gu_ref.at[:, pl.ds(at + ffwidth, sub)], out_sems.at[k % 2, 1]
                ),
                pltpu.make_async_copy(
                    here.at[:, pl.ds(2 * sub, sub)], down_ref.at[:, pl.ds(at, sub)], out_sems.at[k % 2, 2]
                ),
            )

        read(0).start()
        for k in range(count):
            if k + 1 < count:
                read(k + 1).start()
            read(k).wait()
            if k >= 2:
                for copy in writes(k - 2):
                    copy.wait()
            gave[k % 2] = took[k % 2].astype(F32)
            for copy in writes(k):
                copy.start()
        for k in range(max(0, count - 2), count):
            for copy in writes(k):
                copy.wait()

    return pl.pallas_call(
        kernel,
        in_specs=[pl.BlockSpec(memory_space=pltpu.SMEM)] + [ANY] * count,
        out_specs=[ANY, ANY],
        out_shape=[
            jax.ShapeDtypeStruct((rows, 2 * ffwidth), F32),
            jax.ShapeDtypeStruct((rows, ffwidth), F32),
        ],
        scratch_shapes=[
            pltpu.VMEM((2, rows, 3 * sub), BF),
            pltpu.VMEM((2, rows, 3 * sub), F32),
            pltpu.SemaphoreType.DMA((2,)),
            pltpu.SemaphoreType.DMA((2, 3)),
        ],
        compiler_params=params(32),
        cost_estimate=cost(0, rows * ffwidth * 18),
    )(columns, *pieces)


MESH = pl.DeviceIdType.MESH


def ring_place(n_fsdp):
    f, c = lax.axis_index("fsdp"), lax.axis_index("ctx")

    def device(place):
        row, k = place // n_fsdp, place % n_fsdp
        return {"fsdp": k + (row % 2) * (n_fsdp - 1 - 2 * k), "ctx": row}

    return c * n_fsdp + f + (c % 2) * (n_fsdp - 1 - 2 * f), device


def slot_lanes(ref, block, rows):
    if rows % 128 == 0:
        return ref[:, pl.ds(pl.multiple_of(block * rows, 128), rows)].astype(F32)
    share = 128 // rows
    wide = ref[:, pl.ds(pl.multiple_of(block // share * 128, 128), 128)].astype(F32)
    part = wide[:, :rows]
    for k in range(1, share):
        part = jnp.where(block % share == k, wide[:, k * rows : (k + 1) * rows], part)
    return part


def team_place(size, me, bit):
    return me + bit - 2 * bit * ((me // bit) % 2)


def greet(partners):
    barrier = pltpu.get_barrier_semaphore()
    for partner in partners:
        pl.semaphore_signal(barrier, inc=1, device_id=partner, device_id_type=MESH)
    pl.semaphore_wait(barrier, len(partners))


def own_columns(size, w_gate_up, w_down, first):
    ffwidth = w_down.shape[1]
    ffq = ffwidth // size
    sub = ffq // SUBS
    out = []
    for way in range(2):
        at = lax.axis_index("dp") * ffq + (first + way) * sub
        out.append(
            [
                (w_gate_up.at[:, pl.ds(pl.multiple_of(at, 128), sub)], 0),
                (w_gate_up.at[:, pl.ds(pl.multiple_of(at + ffwidth, 128), sub)], sub),
                (w_down.at[:, pl.ds(pl.multiple_of(at, 128), sub)], 2 * sub),
            ]
        )
    return out


class RingGather:
    def __init__(self, sizes, own, out, own_v, own_sem, store_sem, send, recv):
        self.n = sizes[1] * sizes[2]
        self.rows = own_v.shape[1]
        self.own, self.out, self.own_v = own, out, own_v
        self.own_sem, self.store_sem, self.send, self.recv = own_sem, store_sem, send, recv
        place, device = ring_place(sizes[1])
        self.partners = [device((place + 1) % self.n), device((place + self.n - 1) % self.n)]

    def rows_of(self, way, t):
        slot = t if way == 0 else (self.n - t) % self.n
        return pl.ds(slot * self.rows, self.rows)

    def loads(self, way):
        width = self.own_v.shape[2] // 3
        return [
            pltpu.make_async_copy(
                source, self.own_v.at[way, :, pl.ds(place, width)], self.own_sem.at[way, place // width]
            )
            for source, place in self.own[way]
        ]

    def store(self, way):
        return pltpu.make_async_copy(
            self.own_v.at[way], self.out[way].at[pl.ds(0, self.rows)], self.store_sem.at[way]
        )

    def ring(self, way, t, first=False):
        source = self.own_v.at[way] if first else self.out[way].at[self.rows_of(way, t - 1)]
        return pltpu.make_async_remote_copy(
            src_ref=source,
            dst_ref=self.out[way].at[self.rows_of(way, t)],
            send_sem=self.send.at[way, t],
            recv_sem=self.recv.at[way, t],
            device_id=self.partners[way],
            device_id_type=MESH,
        )

    def arrived(self, way, t):
        target = self.out[way].at[self.rows_of(way, t)]
        return pltpu.make_async_remote_copy(
            src_ref=target,
            dst_ref=target,
            send_sem=self.send.at[way, t],
            recv_sem=self.recv.at[way, t],
            device_id=self.partners[way],
            device_id_type=MESH,
        )

    def first(self):
        for way in range(2):
            for copy in self.loads(way):
                copy.start()
        for way in range(2):
            for copy in self.loads(way):
                copy.wait()
            self.ring(way, 1, True).start()
            self.store(way).start()

    def tick(self, t):
        for way in range(2):
            self.arrived(way, t - 1).wait_recv()
            self.ring(way, t).start()

    def last(self):
        for way in range(2):
            self.arrived(way, self.n - 1).wait_recv()
            self.store(way).wait()
            self.ring(way, 1, True).wait_send()
            for t in range(2, self.n):
                self.ring(way, t).wait_send()


def gather_scratch(n, rows, wide):
    dma = pltpu.SemaphoreType.DMA
    return [pltpu.VMEM((2, rows, wide), BF), dma((2, 3)), dma((2,)), dma((2, n)), dma((2, n))]


class RingReduce:
    def __init__(self, sizes, parts, out, land, own_v, land_v, send_v, own_sem, land_sem, out_sem, send, recv):
        self.n = sizes[1] * sizes[2]
        self.rows = out[0].shape[0]
        self.parts, self.out, self.land = parts, out, land
        self.own_v, self.land_v, self.send_v = own_v, land_v, send_v
        self.own_sem, self.land_sem, self.out_sem = own_sem, land_sem, out_sem
        self.send, self.recv = send, recv
        place, device = ring_place(sizes[1])
        self.partners = [device((place + 1) % self.n), device((place + self.n - 1) % self.n)]

    def load_own(self, way, t):
        slot = t % self.n if way == 0 else self.n - t
        return pltpu.make_async_copy(
            self.parts[way].at[pl.ds(slot * self.rows, self.rows)],
            self.own_v.at[way, t % 2],
            self.own_sem.at[way, t % 2],
        )

    def load_land(self, way, t):
        return pltpu.make_async_copy(self.land.at[way, t - 1], self.land_v.at[way], self.land_sem.at[way])

    def ring(self, way, t):
        return pltpu.make_async_remote_copy(
            src_ref=self.send_v.at[way, t % 2],
            dst_ref=self.land.at[way, t - 1],
            send_sem=self.send.at[way, t],
            recv_sem=self.recv.at[way, t],
            device_id=self.partners[way],
            device_id_type=MESH,
        )

    def save(self, way):
        return pltpu.make_async_copy(self.own_v.at[way, self.n % 2], self.out[way], self.out_sem.at[way])

    def first(self):
        for way in range(2):
            self.load_own(way, 1).start()
            self.load_own(way, 2).start()
        for way in range(2):
            self.load_own(way, 1).wait()
            self.send_v[way, 1] = self.own_v[way, 1]
            self.ring(way, 1).start()

    def tick(self, t):
        for way in range(2):
            self.ring(way, t - 1).wait_recv()
            self.load_land(way, t - 1).start()
            self.load_own(way, t + 1).start()
        for way in range(2):
            self.load_own(way, t).wait()
            self.load_land(way, t - 1).wait()

            @pl.when(t >= 3)
            def _():
                self.ring(way, t - 2).wait_send()

            total = self.own_v[way, t % 2].astype(F32) + self.land_v[way].astype(F32)
            self.send_v[way, t % 2] = total.astype(BF)
            self.ring(way, t).start()

    def last(self):
        n = self.n
        for way in range(2):
            self.ring(way, n - 1).wait_recv()
            self.load_land(way, n - 1).start()
        for way in range(2):
            self.load_own(way, n).wait()
            self.load_land(way, n - 1).wait()
            total = self.own_v[way, n % 2].astype(F32) + self.land_v[way].astype(F32)
            self.own_v[way, n % 2] = total.astype(BF)
            self.save(way).start()
        for way in range(2):
            self.ring(way, n - 2).wait_send()
            self.ring(way, n - 1).wait_send()
            self.save(way).wait()


class RingReduceNear(RingReduce):
    def __init__(self, sizes, parts, out, land, own_v, own_sem, out_sem, send, recv):
        RingReduce.__init__(self, sizes, parts, out, land, own_v, None, None, own_sem, None, out_sem, send, recv)

    def ring(self, way, t, first=False):
        return pltpu.make_async_remote_copy(
            src_ref=self.own_v.at[way, 1] if first else self.land.at[way, t - 2],
            dst_ref=self.land.at[way, t - 1],
            send_sem=self.send.at[way, t],
            recv_sem=self.recv.at[way, t],
            device_id=self.partners[way],
            device_id_type=MESH,
        )

    def arrived(self, way, t):
        target = self.land.at[way, t - 1]
        return pltpu.make_async_remote_copy(
            src_ref=target,
            dst_ref=target,
            send_sem=self.send.at[way, t],
            recv_sem=self.recv.at[way, t],
            device_id=self.partners[way],
            device_id_type=MESH,
        )

    def first(self):
        for way in range(2):
            self.load_own(way, 1).start()
            self.load_own(way, 2).start()
        for way in range(2):
            self.load_own(way, 1).wait()
            self.ring(way, 1, True).start()

    def tick(self, t):
        for way in range(2):
            self.arrived(way, t - 1).wait_recv()
            self.load_own(way, t).wait()
            total = self.own_v[way, t % 2].astype(F32) + self.land[way, t - 2].astype(F32)
            self.land[way, t - 2] = total.astype(BF)
            self.ring(way, t).start()

            @pl.when(t == 2)
            def _():
                self.ring(way, 1, True).wait_send()

            self.load_own(way, t + 1).start()

    def last(self):
        n = self.n
        for way in range(2):
            self.arrived(way, n - 1).wait_recv()
            self.load_own(way, n).wait()
            total = self.own_v[way, n % 2].astype(F32) + self.land[way, n - 2].astype(F32)
            self.own_v[way, n % 2] = total.astype(BF)
            self.save(way).start()
        for way in range(2):
            for t in range(2, n):
                self.ring(way, t).wait_send()
            self.save(way).wait()


def near_scratch(n, rows, wide):
    dma = pltpu.SemaphoreType.DMA
    return [
        pltpu.VMEM((2, n - 1, rows, wide), BF),
        pltpu.VMEM((2, 2, rows, wide), BF),
        dma((2, 2)),
        dma((2,)),
        dma((2, n)),
        dma((2, n)),
    ]


class TeamSpread:
    def __init__(self, size, own, others, send, recv):
        self.own, self.others, self.send, self.recv = own, others, send, recv
        self.count = len(own)
        me = lax.axis_index("dp")
        self.stages = []
        held, bit = 1, size // 2
        while bit:
            partner = {"dp": me + bit - 2 * bit * ((me // bit) % 2)}
            self.stages.append((held, partner))
            held, bit = 2 * held, bit // 2

    def partners(self):
        return [partner for _, partner in self.stages]

    def copies(self, stage):
        held, partner = self.stages[stage]
        for k in range(self.count):
            for b in range(held):
                yield pltpu.make_async_remote_copy(
                    src_ref=self.own[k] if b == 0 else self.others[k][b - 1],
                    dst_ref=self.others[k][held + b - 1],
                    send_sem=self.send.at[k, held + b - 1],
                    recv_sem=self.recv.at[k, held + b - 1],
                    device_id=partner,
                    device_id_type=MESH,
                )

    def start(self, stage):
        if stage < len(self.stages):
            for copy in self.copies(stage):
                copy.start()

    def arrive(self, stage):
        if stage < len(self.stages):
            for copy in self.copies(stage):
                copy.wait_recv()

    def last(self):
        for stage in range(len(self.stages)):
            for copy in self.copies(stage):
                copy.wait_send()


def spread_scratch(count, size):
    return [pltpu.SemaphoreType.DMA((count, size)), pltpu.SemaphoreType.DMA((count, size))]


def reduce_scratch(n, rows, wide):
    dma = pltpu.SemaphoreType.DMA
    return [
        pltpu.VMEM((2, 2, rows, wide), BF),
        pltpu.VMEM((2, rows, wide), BF),
        pltpu.VMEM((2, 2, rows, wide), BF),
        dma((2, 2)),
        dma((2,)),
        dma((2,)),
        dma((2, n)),
        dma((2, n)),
    ]


def feed_forward(sizes, xs, dys, weights, before, ring_parts, reducing, ident):
    n_dp, n_fsdp, n_ctx = sizes
    n = n_fsdp * n_ctx
    team, (span, width) = len(xs), xs[0].shape
    rows, wide = width // n, weights[0][0].shape[1]
    sub = wide // 3
    pieces = [piece for group in weights for piece in group]
    counts = [len(group) for group in weights]
    tile = min(span, 256)
    per = span // tile
    steps = team * per
    part = max(rows, 128)
    half = width // 2
    gsteps = width // part
    total = 2 * steps + gsteps
    inside = team // 2 if reducing and team > 2 else 0
    carried = [] if before is None else [b[0] for b in before] + [b[1] for b in before]
    backwards = reducing

    def kernel(*refs):
        refs = list(refs)

        def take(count):
            out = refs[:count]
            del refs[:count]
            return out

        x_refs, dy_refs, piece_refs = take(team), take(team), take(len(pieces))
        old_y, old_dn = take(len(carried) // 2), take(len(carried) // 2)
        part_refs = take(2)
        y_refs, dn_refs, grad_refs, ring_outs = take(team), take(team), take(2), take(2)
        if reducing:
            (land,) = take(1)
            near = take(max(1, inside))
            (far,) = take(1)
        wgu, wd, xb, dyb, yb, dnb, dgu, inner, xg, dyg, gout = take(11)
        w_sems, x_sems, y_sems, g_sems, gout_sems = take(5)
        if carried:
            cb, c_sems = take(2)
        if reducing:
            swap_send, swap_recv, face_send, face_recv = take(4)
            ring = RingReduce(sizes, part_refs, ring_outs, land, *refs)
        else:
            ring = RingGather(sizes, own_columns(n_dp, *part_refs, SUBS // 2), ring_outs, *refs)
        me = lax.axis_index("dp")
        sibling = {"dp": me + 1 - 2 * (me % 2)}
        bit = team // 2
        facing = {"dp": me + bit - 2 * bit * ((me // bit) % 2)}

        k = 0
        w_copies = []
        for b, count in enumerate(counts):
            at = 0
            for ref in piece_refs[k : k + count]:
                high = ref.shape[0]
                w_copies += [
                    pltpu.make_async_copy(
                        ref.at[:, pl.ds(0, 2 * sub)],
                        wgu.at[pl.ds(at, high), pl.ds(b * 2 * sub, 2 * sub)],
                        w_sems.at[2 * k],
                    ),
                    pltpu.make_async_copy(
                        ref.at[:, pl.ds(2 * sub, sub)],
                        wd.at[pl.ds(at, high), pl.ds(b * sub, sub)],
                        w_sems.at[2 * k + 1],
                    ),
                ]
                at += high
                k += 1
        for copy in w_copies:
            copy.start()

        def block_of(i):
            return team - 1 - i // per if backwards else i // per

        def loads(m, i):
            rows_here = pl.ds((i % per) * tile, tile)
            return [
                pltpu.make_async_copy(x_refs[m].at[rows_here], xb.at[i % 2], x_sems.at[0, i % 2]),
                pltpu.make_async_copy(dy_refs[m].at[rows_here], dyb.at[i % 2], x_sems.at[1, i % 2]),
            ]

        def more(m, i):
            if not carried:
                return []
            rows_here = pl.ds((i % per) * tile, tile)
            out = [
                pltpu.make_async_copy(old_y[m].at[rows_here], cb.at[0], c_sems.at[0]),
                pltpu.make_async_copy(old_dn[m].at[rows_here], cb.at[1], c_sems.at[1]),
            ]
            if m < inside:
                out.append(pltpu.make_async_copy(near[m].at[rows_here], cb.at[2], c_sems.at[2]))
            return out

        def writes(m, i):
            rows_here = pl.ds((i % per) * tile, tile)
            return [
                pltpu.make_async_copy(yb, y_refs[m].at[rows_here], y_sems.at[0]),
                pltpu.make_async_copy(dnb, dn_refs[m].at[rows_here], y_sems.at[1]),
            ]

        def on_block(i, act):
            for m in range(team):

                @pl.when(block_of(i) == m)
                def _():
                    act(m)

        def swap(m):
            return pltpu.make_async_remote_copy(
                src_ref=dn_refs[m],
                dst_ref=near[m - inside],
                send_sem=swap_send.at[m - inside],
                recv_sem=swap_recv.at[m - inside],
                device_id=sibling,
                device_id_type=MESH,
            )

        def face():
            return pltpu.make_async_remote_copy(
                src_ref=dn_refs[1],
                dst_ref=far,
                send_sem=face_send,
                recv_sem=face_recv,
                device_id=facing,
                device_id_type=MESH,
            )

        def go(copies):
            for copy in copies:
                copy.start()

        def end(copies):
            for copy in copies:
                copy.wait()

        def ticks(lo, hi):
            lax.fori_loop(2 + lo * (n - 2) // total, 2 + hi * (n - 2) // total, lambda t, c: (ring.tick(t), c)[1], 0)

        on_block(0, lambda m: go(loads(m, 0)))
        partners = list(ring.partners)
        if inside:
            partners.append(sibling)
        if reducing and team > 1:
            partners.append(facing)
        greet(partners)
        ring.first()
        for copy in w_copies:
            copy.wait()

        def forward(i, carry):
            @pl.when(i + 1 < steps)
            def _():
                on_block(i + 1, lambda m: go(loads(m, i + 1)))

            @pl.when(i == steps - 1)
            def _():
                go(sides(0))

            if inside:
                @pl.when(i % per == 0)
                def _():
                    on_block(i, lambda m: swap(m + inside).wait_recv() if m < inside else None)

            on_block(i, lambda m: go(more(m, i)))
            ticks(2 * i, 2 * i + 2)
            end(loads(0, i))
            here = pl.ds(pl.multiple_of(i * tile, tile), tile)
            for b in range(2):
                gate_up = dot_nn(xb[i % 2], wgu[:, b * 2 * sub : (b + 1) * 2 * sub])
                d_inner = dot_nn(dyb[i % 2], wd[:, b * sub : (b + 1) * sub])
                gate, up = gate_up[:, :sub], gate_up[:, sub:]
                sig = 1.0 / (1.0 + jnp.exp(-gate))
                act = gate * sig
                inner[here, b * sub : (b + 1) * sub] = (act * up).astype(BF)
                dgu[here, b * 2 * sub : b * 2 * sub + sub] = (
                    d_inner * up * (sig + act * (1.0 - sig))
                ).astype(BF)
                dgu[here, b * 2 * sub + sub : (b + 1) * 2 * sub] = (d_inner * act).astype(BF)
            drained = (i > 0) & (i % per != 0) if reducing else i > 0

            @pl.when(drained)
            def _():
                end(writes(0, i))

            if carried:
                on_block(i, lambda m: end(more(m, i)))
            for at in range(0, width, half):
                lanes = slice(at, at + half)
                y = dot_nt(inner[here, :], wd[lanes, :])
                if carried:
                    y = y + cb[0, :, lanes].astype(F32)
                yb[:, lanes] = y.astype(BF)
                dn = dot_nt(dgu[here, :], wgu[lanes, :])
                if carried:
                    dn = dn + cb[1, :, lanes].astype(F32)
                if inside:
                    dn = dn + jnp.where(block_of(i) < inside, cb[2, :, lanes].astype(F32), 0.0)
                dnb[:, lanes] = dn.astype(BF)
            on_block(i, lambda m: go(writes(m, i)))
            if reducing and team > 1:

                @pl.when(i % per == per - 1)
                def _():
                    def sent(m):
                        if m >= 1:
                            end(writes(m, i))
                            go([swap(m)] if inside and m >= inside else [face()])

                    on_block(i, sent)

            return carry

        def sides(g):
            cols = pl.ds(g * part, part) if isinstance(g, int) else pl.ds(pl.multiple_of(g * part, part), part)
            out = []
            for k in range(team):
                m = team - 1 - k if backwards else k
                at = pl.ds(k * span, span)
                out += [
                    pltpu.make_async_copy(x_refs[m].at[:, cols], xg.at[g % 2, at], g_sems.at[0, g % 2, k]),
                    pltpu.make_async_copy(dy_refs[m].at[:, cols], dyg.at[g % 2, at], g_sems.at[1, g % 2, k]),
                ]
            return out

        def keep(g):
            at = pl.ds(pl.multiple_of(g * part, part), part)
            return [pltpu.make_async_copy(gout.at[b], grad_refs[b].at[at], gout_sems.at[b]) for b in range(2)]

        def outer(g, carry):
            @pl.when(g + 1 < gsteps)
            def _():
                go(sides(g + 1))

            ticks(2 * steps + g, 2 * steps + g + 1)
            end(sides(g))

            @pl.when(g > 0)
            def _():
                end(keep(g))

            for b in range(2):
                up_down = dot_tn(xg[g % 2], dgu[:, b * 2 * sub : (b + 1) * 2 * sub])
                gout[b, :, : 2 * sub] = up_down.astype(BF)
                down = dot_tn(dyg[g % 2], inner[:, b * sub : (b + 1) * sub])
                gout[b, :, 2 * sub :] = down.astype(BF)
            go(keep(g))
            return carry

        lax.fori_loop(0, steps, forward, 0)
        lax.fori_loop(0, gsteps, outer, 0)
        end(writes(0, 0))
        end(keep(0))
        ring.last()
        if reducing and team > 1:
            for m in range(inside, team) if inside else []:
                swap(m).wait_send()
            face().wait_recv()
            face().wait_send()

    shape = lambda a, b: jax.ShapeDtypeStruct((a, b), BF)
    outs = [shape(span, width)] * (2 * team) + [shape(width, wide)] * 2
    if reducing:
        outs += [shape(rows, wide)] * 2 + [jax.ShapeDtypeStruct((2, n - 1, rows, wide), BF)]
        outs += [shape(span, width)] * (max(1, inside) + 1)
    else:
        outs += [shape(width, wide)] * 2
    dma = pltpu.SemaphoreType.DMA
    scratch = [
        pltpu.VMEM((width, 4 * sub), BF),
        pltpu.VMEM((width, 2 * sub), BF),
        pltpu.VMEM((2, tile, width), BF),
        pltpu.VMEM((2, tile, width), BF),
        pltpu.VMEM((tile, width), BF),
        pltpu.VMEM((tile, width), BF),
        pltpu.VMEM((team * span, 4 * sub), BF),
        pltpu.VMEM((team * span, 2 * sub), BF),
        pltpu.VMEM((2, team * span, part), BF),
        pltpu.VMEM((2, team * span, part), BF),
        pltpu.VMEM((2, part, wide), BF),
        dma((2 * len(pieces),)),
        dma((2, 2)),
        dma((2,)),
        dma((2, 2, team)),
        dma((2,)),
    ]
    if carried:
        scratch += [pltpu.VMEM((3 if inside else 2, tile, width), BF), dma((3,))]
    if reducing:
        scratch += [dma((max(1, inside),)), dma((max(1, inside),)), dma(()), dma(())]
        scratch += reduce_scratch(n, rows, wide)
    else:
        scratch += gather_scratch(n, rows, wide)
    operands = list(xs) + list(dys) + pieces + carried + list(ring_parts)
    out = pl.pallas_call(
        kernel,
        in_specs=[ANY] * len(operands),
        out_specs=[ANY] * len(outs),
        out_shape=outs,
        scratch_shapes=scratch,
        compiler_params=pltpu.CompilerParams(
            collective_id=ident, has_side_effects=True, vmem_limit_bytes=56 * MIB
        ),
        cost_estimate=cost(18 * team * span * width * 2 * sub, 40 * MIB),
    )(*operands)
    y, dn, grads, ringed = out[:team], out[team : 2 * team], out[2 * team : 2 * team + 2], out[2 * team + 2 :]
    if reducing:
        return y, (dn[0], ringed[-1]) if team > 1 else (dn[0],), grads, ringed[:2]
    return y, dn, grads, ringed[:2]


def attend_forward(sizes, x, qkv, kv_far, seen, w_out, gains, dy, w_gate_up, w_down):
    n_dp, n_fsdp, n_ctx = sizes
    n = n_fsdp * n_ctx
    span, width = x.shape
    rows = width // n
    far = kv_far.shape[0]
    blocks = far // span
    qwidth, kvwidth = HEADS * HD, KV_HEADS * HD
    near, kvpairs = qwidth // 128, kvwidth // 128
    pairs = HEADS // 2
    tile = min(span, 256)
    wide = 3 * (w_down.shape[1] // n_dp // SUBS)
    early = max(0, 3 * (n - 2) // 7)
    others = n_dp - 1
    chunk = min(512, width)

    def kernel(seen_ref, q_ref, k_ref, v_ref, kf_ref, vf_ref, x_ref, gains_ref, *refs):
        refs = list(refs)

        def take(count):
            out = refs[:count]
            del refs[:count]
            return out

        wo_ref, dy_ref, gu_ref, down_ref = take(4)
        lse_ref, attn_out, hidden_out, normed_out = take(4)
        x_blocks, dy_blocks, ring_outs = take(others), take(others), take(2)
        attn_v, wo_v, hidden_v, normed_v, load_sem, save_sems = take(6)
        dy_send, dy_recv, x_send, x_recv = take(4)
        ring = RingGather(sizes, own_columns(n_dp, gu_ref, down_ref, 0), ring_outs, *refs)
        dy_spread = TeamSpread(n_dp, [dy_ref], [dy_blocks], dy_send, dy_recv)
        x_spread = TeamSpread(n_dp, [normed_v], [x_blocks], x_send, x_recv)
        group = pl.program_id(0)
        mask = causal_tile(tile)
        flags = [seen_ref[k] == 1 for k in range(blocks)]
        load = pltpu.make_async_copy(wo_ref, wo_v, load_sem)

        @pl.when(group == 0)
        def _():
            greet(ring.partners + dy_spread.partners())
            ring.first()
            dy_spread.start(0)
            load.start()

        lax.fori_loop(
            2 + group * early // pairs,
            2 + (group + 1) * early // pairs,
            lambda t, c: (ring.tick(t), c)[1],
            0,
        )
        key, value = head_of(k_ref[...], group), head_of(v_ref[...], group)
        key_far, value_far = head_of(kf_ref[...], group), head_of(vf_ref[...], group)
        value_t = value.astype(F32).T.astype(BF)
        value_far_t = value_far.astype(F32).T.astype(BF)
        for head in range(2):
            down = pl.ds(pl.multiple_of(group * 128 + head * HD, HD), HD)
            for at in range(0, span, tile):
                end = at + tile
                q = q_ref[at:end, head * HD : (head + 1) * HD]
                own, other = scores_of(key[:end], key_far, q, flags, mask, span)
                peak = jnp.maximum(jnp.max(own, 0, keepdims=True), jnp.max(other, 0, keepdims=True))
                own = jnp.exp(own - peak)
                other = jnp.exp(other - peak)
                total = jnp.sum(own, 0, keepdims=True) + jnp.sum(other, 0, keepdims=True)
                scale = 1.0 / total
                result = dot_nn(value_t[:, :end], (own * scale).astype(BF)) + dot_nn(
                    value_far_t, (other * scale).astype(BF)
                )
                attn_v[down, at:end] = result.astype(BF)
                lse_ref[0, head : head + 1, at:end] = peak + jnp.log(total)

        @pl.when(group == pairs - 1)
        def _():
            saves = [
                pltpu.make_async_copy(a, b, save_sems.at[k])
                for k, (a, b) in enumerate([(attn_v, attn_out), (hidden_v, hidden_out), (normed_v, normed_out)])
            ]
            saves[0].start()
            load.wait()
            square = jnp.zeros((span, 1), F32)
            for at in range(0, width, chunk):
                lanes = slice(at, at + chunk)
                hidden = x_ref[:, lanes].astype(F32) + dot_tn(attn_v[...], wo_v[:, lanes])
                hidden_v[:, lanes] = hidden
                square = square + jnp.sum(hidden * hidden, -1, keepdims=True)
            scale = lax.rsqrt(square / width + EPS)
            place, device = ring_place(n_fsdp)
            for slot in range(n):
                there = device((place + n - slot) % n)
                part = slot_lanes(hidden_v, there["fsdp"] * n_ctx + there["ctx"], rows)
                normed = part * scale * gains_ref[slot, 1:2, :].astype(F32)
                normed_v[:, slot * rows : (slot + 1) * rows] = normed.astype(BF)
            x_spread.start(0)
            saves[1].start()
            saves[2].start()
            dy_spread.arrive(0)
            dy_spread.start(1)
            middle = max(2 + early, n - 2)
            for t in range(2 + early, middle):
                ring.tick(t)
            x_spread.arrive(0)
            x_spread.start(1)
            for t in range(middle, n):
                ring.tick(t)
            dy_spread.arrive(1)
            x_spread.arrive(1)
            ring.last()
            dy_spread.last()
            x_spread.last()
            for copy in saves:
                copy.wait()

    pair = lambda high, shift: pl.BlockSpec((high, 128), lambda i: (0, i // 4 + shift))
    dma = pltpu.SemaphoreType.DMA
    block = jax.ShapeDtypeStruct((span, width), BF)
    out = pl.pallas_call(
        kernel,
        grid=(pairs,),
        in_specs=[
            pl.BlockSpec(memory_space=pltpu.SMEM),
            pl.BlockSpec((span, 128), lambda i: (0, i)),
            pair(span, near),
            pair(span, near + kvpairs),
            pair(far, 0),
            pair(far, kvpairs),
            pl.BlockSpec((span, width), lambda i: (0, 0)),
            pl.BlockSpec(gains.shape, lambda i: (0, 0, 0)),
        ]
        + [ANY] * 4,
        out_specs=[pl.BlockSpec((1, 8, span), lambda i: (i, 0, 0))] + [ANY] * (5 + 2 * others),
        out_shape=[
            jax.ShapeDtypeStruct((pairs, 8, span), F32),
            jax.ShapeDtypeStruct((qwidth, span), BF),
            jax.ShapeDtypeStruct((span, width), F32),
        ]
        + [block] * (1 + 2 * others)
        + [jax.ShapeDtypeStruct((width, wide), BF)] * 2,
        scratch_shapes=[
            pltpu.VMEM((qwidth, span), BF),
            pltpu.VMEM((qwidth, width), BF),
            pltpu.VMEM((span, width), F32),
            pltpu.VMEM((span, width), BF),
            dma(()),
            dma((3,)),
        ]
        + spread_scratch(1, n_dp)
        + spread_scratch(1, n_dp)
        + gather_scratch(n, rows, wide),
        compiler_params=pltpu.CompilerParams(
            collective_id=5, has_side_effects=True, vmem_limit_bytes=48 * MIB
        ),
        cost_estimate=cost(pairs * 2 * span * (span + far) * 128 * 4, 30 * MIB),
    )(seen, qkv, qkv, qkv, kv_far, kv_far, x, gains, w_out, dy, w_gate_up, w_down)
    lse, attn, hidden, normed = out[:4]
    return attn, lse, hidden, normed, out[4 : 4 + others], out[4 + others : 4 + 2 * others], out[4 + 2 * others :]


def attend_backward(sizes, qkv, kv_far, d_attn, lse, seen, tables, attn_t, d_proj, normed, ring_parts, sums, ident):
    n_dp, n_fsdp, n_ctx = sizes
    n = n_fsdp * n_ctx
    span, far = qkv.shape[0], kv_far.shape[0]
    blocks = far // span
    qwidth, kvwidth = HEADS * HD, KV_HEADS * HD
    near, kvpairs = qwidth // 128, kvwidth // 128
    pairs = HEADS // 2
    tile = min(span, 256)
    rows, wide = ring_parts[0].shape[0] // n, ring_parts[0].shape[1]
    early = 4 * (n - 2) // 7
    width = normed.shape[1]
    qkvwidth = qwidth + 2 * kvwidth
    part = max(rows, 128)
    others = n_dp - 1

    def kernel(seen_ref, q_ref, k_ref, v_ref, kf_ref, vf_ref, d_ref, lse_ref, cos_ref, low_ref, high_ref, *refs):
        refs = list(refs)

        def take(count):
            out = refs[:count]
            del refs[:count]
            return out

        attn_ref, proj_ref, normed_ref = take(3)
        parts, own_sums = take(2), take(2)
        dqkv_out, go_out, gq_out = take(3)
        ring_outs, blocks_out = take(2), take(2 * others)
        dqkv_v, dkv, dkv_far, give, got, save_sem, kv_send, kv_recv = take(8)
        attn_v, proj_v, normed_v, stage, load_sems, stage_sems = take(6)
        spread_send, spread_recv = take(2)
        ring = RingReduceNear(sizes, parts, ring_outs, *refs)
        spread = TeamSpread(
            n_dp, own_sums, [blocks_out[k * others : (k + 1) * others] for k in range(2)], spread_send, spread_recv
        )
        loads = [
            pltpu.make_async_copy(a, b, load_sems.at[k])
            for k, (a, b) in enumerate([(attn_ref, attn_v), (proj_ref, proj_v), (normed_ref, normed_v)])
        ]

        def product(out, cols, make):
            def write(g):
                return pltpu.make_async_copy(
                    stage.at[g % 2, :, pl.ds(0, cols)],
                    out.at[pl.ds(pl.multiple_of(g * part, part), part)],
                    stage_sems.at[g % 2],
                )

            def body(g, carry):
                @pl.when(g >= 2)
                def _():
                    write(g - 2).wait()

                stage[g % 2, :, :cols] = make(pl.ds(pl.multiple_of(g * part, part), part)).astype(BF)
                write(g).start()
                return carry

            count = width // part
            lax.fori_loop(0, count, body, 0)
            for g in range(max(0, count - 2), count):
                write(g).wait()

        ctx = lax.axis_index("ctx")
        group = pl.program_id(0)
        mask = causal_tile(tile)
        flags = [seen_ref[k] == 1 for k in range(blocks)]
        key, value = head_of(k_ref[...], group), head_of(v_ref[...], group)
        key_far, value_far = head_of(kf_ref[...], group), head_of(vf_ref[...], group)
        key_t = key.astype(F32).T.astype(BF)
        key_far_t = key_far.astype(F32).T.astype(BF)
        odd = (group // 2) % 2 == 1
        cosine, low, high = cos_ref[...], -low_ref[...], -high_ref[...]

        @pl.when(group == 0)
        def _():
            greet(ring.partners + [{"ctx": (ctx + k) % n_ctx} for k in range(1, n_ctx)] + spread.partners())
            ring.first()
            spread.start(0)
            for copy in loads:
                copy.start()
            dkv[...] = jnp.zeros_like(dkv)
            dkv_far[...] = jnp.zeros_like(dkv_far)

        @pl.when(group == pairs - 4)
        def _():
            spread.arrive(0)
            spread.start(1)

        lax.fori_loop(
            2 + group * early // pairs,
            2 + (group + 1) * early // pairs,
            lambda t, c: (ring.tick(t), c)[1],
            0,
        )

        def put(ref, size, shift, add):
            zero = jnp.zeros_like(add)
            lanes = pl.ds(pl.multiple_of(group // 4 * 128 + shift, 128), 128)
            ref[0:size, lanes] += jnp.concatenate([jnp.where(odd, zero, add), jnp.where(odd, add, zero)], 1)

        for at in range(0, span, tile):
            end = at + tile
            turned = []
            for head in range(2):
                lanes = slice(head * HD, (head + 1) * HD)
                q = q_ref[at:end, lanes]
                d = d_ref[at:end, lanes]
                own, other = scores_of(key[:end], key_far, q, flags, mask, span)
                base = lse_ref[0, head : head + 1, at:end]
                own = jnp.exp(own - base)
                other = jnp.exp(other - base)
                d_own = dot_nt(value[:end], d)
                d_other = dot_nt(value_far, d)
                delta = jnp.sum(own * d_own, 0, keepdims=True) + jnp.sum(other * d_other, 0, keepdims=True)
                ds_own = (own * (d_own - delta)).astype(BF)
                ds_other = (other * (d_other - delta)).astype(BF)
                put(dkv, end, kvwidth, dot_nn(own.astype(BF), d))
                put(dkv_far, far, kvwidth, dot_nn(other.astype(BF), d))
                put(dkv, end, 0, dot_nn(ds_own, q))
                put(dkv_far, far, 0, dot_nn(ds_other, q))
                turned.append(dot_nn(key_t[:, :end], ds_own) + dot_nn(key_far_t, ds_other))
            d_query = jnp.concatenate(turned, 0).T * HD**-0.5
            dqkv_v[at:end, pl.ds(pl.multiple_of(group * 128, 128), 128)] = turn(
                d_query, cosine[at:end], low[at:end], high[at:end]
            ).astype(BF)

        @pl.when(group == pairs - 1)
        def _():
            give[...] = dkv_far[...].astype(BF)

            def back(k):
                return pltpu.make_async_remote_copy(
                    src_ref=give.at[pl.ds((k - 1) * span, span)],
                    dst_ref=got.at[k - 1],
                    send_sem=kv_send.at[k],
                    recv_sem=kv_recv.at[k],
                    device_id={"ctx": (ctx + k) % n_ctx},
                    device_id_type=MESH,
                )

            for k in range(1, n_ctx):
                back(k).start()
            middle = (2 + early + n) // 2
            for t in range(2 + early, middle):
                ring.tick(t)
            for copy in loads:
                copy.wait()
            product(go_out, qwidth, lambda at: dot_nn(attn_v[at, :], proj_v[...]))
            for k in range(1, n_ctx):
                back(k).wait_recv()
            for at in range(0, 2 * kvwidth, 128):
                piece = dkv[:, at : at + 128]
                for k in range(1, n_ctx):
                    piece = piece + got[k - 1, :, at : at + 128].astype(F32)
                if at < kvwidth:
                    piece = turn(piece, cosine, low, high)
                dqkv_v[:, qwidth + at : qwidth + at + 128] = piece.astype(BF)
            save = pltpu.make_async_copy(dqkv_v, dqkv_out, save_sem)
            save.start()
            for t in range(middle, n - 1):
                ring.tick(t)
            product(gq_out, qkvwidth, lambda at: dot_tn(normed_v[:, at], dqkv_v[...]))
            ring.tick(n - 1)
            spread.arrive(1)
            ring.last()
            spread.last()
            for k in range(1, n_ctx):
                back(k).wait_send()
            save.wait()

    pair = lambda high, shift: pl.BlockSpec((high, 128), lambda i: (0, i // 4 + shift))
    wide_block = pl.BlockSpec((span, 128), lambda i: (0, i))
    table = pl.BlockSpec((span, 128), lambda i: (0, 0))
    dma = pltpu.SemaphoreType.DMA
    out = pl.pallas_call(
        kernel,
        grid=(pairs,),
        in_specs=[
            pl.BlockSpec(memory_space=pltpu.SMEM),
            wide_block,
            pair(span, near),
            pair(span, near + kvpairs),
            pair(far, 0),
            pair(far, kvpairs),
            wide_block,
            pl.BlockSpec((1, 8, span), lambda i: (i, 0, 0)),
            table,
            table,
            table,
        ]
        + [ANY] * 7,
        out_specs=[ANY] * (5 + 2 * others),
        out_shape=[
            jax.ShapeDtypeStruct((span, qkvwidth), BF),
            jax.ShapeDtypeStruct((width, qwidth), BF),
            jax.ShapeDtypeStruct((width, qkvwidth), BF),
        ]
        + [jax.ShapeDtypeStruct((rows, wide), BF)] * (2 + 2 * others),
        scratch_shapes=[
            pltpu.VMEM((span, qwidth + 2 * kvwidth), BF),
            pltpu.VMEM((span, 2 * kvwidth), F32),
            pltpu.VMEM((far, 2 * kvwidth), F32),
            pltpu.VMEM((far, 2 * kvwidth), BF),
            pltpu.VMEM((n_ctx - 1, span, 2 * kvwidth), BF),
            dma(()),
            dma((n_ctx,)),
            dma((n_ctx,)),
            pltpu.VMEM(attn_t.shape, BF),
            pltpu.VMEM(d_proj.shape, BF),
            pltpu.VMEM(normed.shape, BF),
            pltpu.VMEM((2, part, max(qwidth, qkvwidth)), BF),
            dma((3,)),
            dma((2,)),
        ]
        + spread_scratch(2, n_dp)
        + near_scratch(n, rows, wide),
        compiler_params=pltpu.CompilerParams(
            collective_id=ident, has_side_effects=True, vmem_limit_bytes=40 * MIB
        ),
        cost_estimate=cost(pairs * 2 * span * (span + far) * 128 * 10, 30 * MIB),
    )(seen, qkv, qkv, qkv, kv_far, kv_far, d_attn, lse, *tables, attn_t, d_proj, normed, *ring_parts, *sums)
    return out[0], out[1], out[2], out[3:5], [out[5 + k * others : 5 + (k + 1) * others] for k in range(2)]


def opening(sizes, x, w_qkv, w_out, gains, tables):
    n_dp, n_fsdp, n_ctx = sizes
    n = n_fsdp * n_ctx
    span, width = x.shape
    rows = width // n
    share, half = w_qkv.shape[1] // n_dp, w_out.shape[1] // 2
    qwidth, kvwidth = HEADS * HD, KV_HEADS * HD
    qkvwidth = qwidth + 2 * kvwidth
    chunk = share // 2 if share % 256 == 0 else share
    across_x = n_dp > 2

    def kernel(x_ref, wq_ref, wo_ref, g_ref, cos_ref, low_ref, high_ref, *refs):
        refs = list(refs)

        def take(count):
            out = refs[:count]
            del refs[:count]
            return out

        qkv_out, far_out, xs_out, wq_out, wo_out, gains_out = take(6)
        qkv_v, far_v, xs_v = take(3)
        wq_v = take(n_dp)
        om_v, oo_v, gains_v = take(3)
        load_sems, save_sems, wq_sems, wo_sems = take(4)
        send, recv, x_send, x_recv, c_send, c_recv, o_send, o_recv = take(8)
        gain_send, gain_recv, kv_send, kv_recv = take(4)
        me = lax.axis_index("dp")
        core = me % 2
        sibling = {"dp": team_place(n_dp, me, 1)}
        facing = {"dp": team_place(n_dp, me, n_dp // 2)}
        bases = [me, team_place(n_dp, me, n_dp // 2)] if across_x else [me]
        bases = [b * share for b in bases + [team_place(n_dp, b, 1) for b in bases]]
        held = n_dp // 2
        place, device = ring_place(n_fsdp)
        ahead, behind = device((place + 1) % n), device((place + n - 1) % n)
        mine = (wq_v[0], om_v)
        widths = (share, half)

        def block_of(slot):
            there = device((place + n - slot) % n)
            return there["fsdp"] * n_ctx + there["ctx"]

        loads = [
            pltpu.make_async_copy(
                ref.at[:, pl.ds(pl.multiple_of(at, 128), w)], mine[k].at[pl.ds(0, rows)], load_sems.at[k]
            )
            for k, (ref, at, w) in enumerate(((wq_ref, me * share, share), (wo_ref, core * half, half)))
        ] + [pltpu.make_async_copy(g_ref, gains_v.at[0], load_sems.at[2])]
        for copy in loads:
            copy.start()
        ctx = lax.axis_index("ctx")
        greet(
            [ahead, behind, sibling]
            + ([facing] if across_x else [])
            + [{"ctx": (ctx + k) % n_ctx} for k in range(1, n_ctx)]
        )

        def lanes(k, way):
            return pl.ds(way * (widths[k] // 2), widths[k] // 2)

        def remote(source, target, send_sem, recv_sem, partner):
            return pltpu.make_async_remote_copy(
                src_ref=source,
                dst_ref=target,
                send_sem=send_sem,
                recv_sem=recv_sem,
                device_id=partner,
                device_id_type=MESH,
            )

        def step(k, way, t):
            here = t - 1 if way == 0 else (n - t + 1) % n
            there = t if way == 0 else n - t
            return remote(
                mine[k].at[pl.ds(here * rows, rows), lanes(k, way)],
                mine[k].at[pl.ds(there * rows, rows), lanes(k, way)],
                send.at[k, way, t],
                recv.at[k, way, t],
                ahead if way == 0 else behind,
            )

        def over_x(way, slot):
            at = (pl.ds(slot * rows, rows), lanes(0, way))
            return remote(wq_v[0].at[at], wq_v[1].at[at], x_send.at[way, slot], x_recv.at[way, slot], facing)

        def over_core(b, way, slot):
            at = (pl.ds(slot * rows, rows), lanes(0, way))
            return remote(
                wq_v[b].at[at], wq_v[held + b].at[at], c_send.at[b, way, slot], c_recv.at[b, way, slot], sibling
            )

        def out_over(way, slot):
            at = (pl.ds(slot * rows, rows), lanes(1, way))
            return remote(om_v.at[at], oo_v.at[at], o_send.at[way, slot], o_recv.at[way, slot], sibling)

        def gain_step(t):
            return remote(gains_v.at[t - 1], gains_v.at[t], gain_send.at[t], gain_recv.at[t], ahead)

        def kv_step(k):
            return remote(
                qkv_v.at[:, pl.ds(qwidth, 2 * kvwidth)],
                far_v.at[pl.ds((k - 1) * span, span)],
                kv_send.at[k],
                kv_recv.at[k],
                {"ctx": (ctx + n_ctx - k) % n_ctx},
            )

        def give(way, slot):
            if across_x:
                over_x(way, slot).start()
            over_core(0, way, slot).start()

        f32 = x_ref[...].astype(F32)
        scale = lax.rsqrt(jnp.mean(f32 * f32, -1, keepdims=True) + EPS)

        def normalize(slot):
            part = slot_lanes(x_ref, block_of(slot), rows)
            xs_v[:, slot * rows : (slot + 1) * rows] = (
                part * scale * gains_v[slot, 0:1, :].astype(F32)
            ).astype(BF)

        loads[0].wait()
        loads[2].wait()
        gain_step(1).start()
        for way in range(2):
            step(0, way, 1).start()
        loads[1].wait()
        for way in range(2):
            give(way, 0)
        normalize(0)
        for t in range(1, n):
            gain_step(t).wait_recv()
            if t < n - 1:
                gain_step(t + 1).start()
            for way in range(2):
                step(0, way, t).wait_recv()
                if t < n - 1:
                    step(0, way, t + 1).start()
                give(way, t if way == 0 else n - t)
            normalize(t)

        for way in range(2):
            step(1, way, 1).start()
            out_over(way, 0).start()

        def out_tick(t):
            for way in range(2):
                step(1, way, t).wait_recv()
                if t < n - 1:
                    step(1, way, t + 1).start()
                out_over(way, t if way == 0 else n - t).start()

        order = [(way, 0) for way in range(2)]
        for t in range(1, n):
            order += [(0, t), (1, n - t)]
        cosine, low, high = cos_ref[...], low_ref[...], high_ref[...]

        def form(b, at):
            value = dot_nn(xs_v[...], wq_v[b][:, at : at + chunk])
            for part in range(0, chunk, 128):
                piece = value[:, part : part + 128]
                here = bases[b] + at + part
                piece = jnp.where(here >= qwidth + kvwidth, piece, turn(piece, cosine, low, high))
                piece = piece * jnp.where(here < qwidth, HD**-0.5, 1.0)
                qkv_v[:, pl.ds(pl.multiple_of(here, 128), 128)] = piece.astype(BF)

        def save_share(b):
            return [
                pltpu.make_async_copy(
                    wq_v[b].at[pl.ds(slot * rows, rows)],
                    wq_out.at[
                        pl.ds(pl.multiple_of(block_of(slot) * rows, rows), rows),
                        pl.ds(pl.multiple_of(bases[b], 128), share),
                    ],
                    wq_sems.at[b, slot],
                )
                for slot in range(n)
            ]

        def save_half(k):
            whose = core if k == 0 else 1 - core
            return [
                pltpu.make_async_copy(
                    (om_v, oo_v)[k].at[pl.ds(slot * rows, rows)],
                    wo_out.at[
                        pl.ds(pl.multiple_of(block_of(slot) * rows, rows), rows),
                        pl.ds(pl.multiple_of(whose * half, 128), half),
                    ],
                    wo_sems.at[k, slot],
                )
                for slot in range(n)
            ]

        def go(copies):
            for copy in copies:
                copy.start()

        jobs = [lambda at=at: form(0, at) for at in range(0, share, chunk)]
        jobs.append(lambda: go(save_share(0)))

        def core_shares(b):
            for way, slot in order:
                over_core(b, way, slot).wait_recv()
            go(save_share(held + b))

        jobs.append(lambda: core_shares(0))
        jobs += [lambda at=at: form(held, at) for at in range(0, share, chunk)]
        if across_x:

            def relay(way, slot):
                over_x(way, slot).wait_recv()
                over_core(1, way, slot).start()

            jobs += [lambda w=way, k=slot: relay(w, k) for way, slot in order]
            jobs.append(lambda: go(save_share(1)))
            jobs += [lambda at=at: form(1, at) for at in range(0, share, chunk)]
            jobs.append(lambda: core_shares(1))
            jobs += [lambda at=at: form(held + 1, at) for at in range(0, share, chunk)]
        for k, job in enumerate(jobs):
            job()
            for t in range(1 + k * (n - 1) // len(jobs), 1 + (k + 1) * (n - 1) // len(jobs)):
                out_tick(t)
        for j in range(1, n_ctx):
            kv_step(j).start()
        saves = [
            pltpu.make_async_copy(a, b, save_sems.at[k])
            for k, (a, b) in enumerate([(qkv_v, qkv_out), (far_v, far_out), (xs_v, xs_out), (gains_v, gains_out)])
        ]
        for k in (0, 2, 3):
            saves[k].start()
        go(save_half(0))
        for way, slot in order:
            out_over(way, slot).wait_recv()
        go(save_half(1))
        for j in range(1, n_ctx):
            kv_step(j).wait_recv()
        saves[1].start()
        for t in range(1, n):
            gain_step(t).wait_send()
            for way in range(2):
                for k in range(2):
                    step(k, way, t).wait_send()
        for way, slot in order:
            out_over(way, slot).wait_send()
            for b in range(held):
                over_core(b, way, slot).wait_send()
            if across_x:
                over_x(way, slot).wait_send()
        for j in range(1, n_ctx):
            kv_step(j).wait_send()
        for copies in [save_share(b) for b in range(n_dp)] + [save_half(k) for k in range(2)] + [saves]:
            for copy in copies:
                copy.wait()

    dma = pltpu.SemaphoreType.DMA
    shapes = [
        (span, qkvwidth),
        ((n_ctx - 1) * span, 2 * kvwidth),
        (span, width),
        (width, qkvwidth),
        (width, 2 * half),
        (n, 16, rows),
    ]
    return pl.pallas_call(
        kernel,
        in_specs=[WHOLE, ANY, ANY, ANY, WHOLE, WHOLE, WHOLE],
        out_specs=[ANY] * 6,
        out_shape=[jax.ShapeDtypeStruct(shape, BF) for shape in shapes],
        scratch_shapes=[pltpu.VMEM(shape, BF) for shape in shapes[:3]]
        + [pltpu.VMEM((width, share), BF)] * n_dp
        + [pltpu.VMEM((width, half), BF)] * 2
        + [pltpu.VMEM((n, 16, rows), BF)]
        + [
            dma((3,)),
            dma((4,)),
            dma((n_dp, n)),
            dma((2, n)),
            dma((2, 2, n)),
            dma((2, 2, n)),
            dma((2, n)),
            dma((2, n)),
            dma((n_dp // 2, 2, n)),
            dma((n_dp // 2, 2, n)),
            dma((2, n)),
            dma((2, n)),
            dma((n,)),
            dma((n,)),
            dma((n_ctx,)),
            dma((n_ctx,)),
        ],
        compiler_params=pltpu.CompilerParams(
            collective_id=0, has_side_effects=True, vmem_limit_bytes=56 * MIB
        ),
        cost_estimate=cost(2 * span * width * qkvwidth, 4 * width * qkvwidth),
    )(x, w_qkv, w_out, gains, *tables)


def closing(sizes, fulls, slotted, sums):
    n_dp, n_fsdp, n_ctx = sizes
    n = n_fsdp * n_ctx
    rows = [f.shape[0] // n for f in fulls]
    widths = [f.shape[1] // 2 for f in fulls]
    kinds = [f.dtype for f in fulls]
    count = len(fulls)
    bits = [1 << k for k in range(1, n_dp.bit_length() - 1)]
    others = n_dp - 1

    def kernel(*refs):
        refs = list(refs)

        def take(size):
            out = refs[:size]
            del refs[:size]
            return out

        full, own_sums = take(count), take(len(sums))
        outs, blocks_out = take(count), take(len(sums) * others)
        near, land, done, extra, back = take(count), take(count), take(count), take(count), take(count)
        send, recv, pair_send, pair_recv, x_send, x_recv, end_send, end_recv = take(8)
        spread = TeamSpread(
            n_dp, own_sums, [blocks_out[k * others : (k + 1) * others] for k in range(len(sums))], *refs
        )
        me = lax.axis_index("dp")
        core = me % 2
        sibling = {"dp": me + 1 - 2 * core}
        place, device = ring_place(n_fsdp)
        ahead, behind = device((place + 1) % n), device((place + n - 1) % n)
        facing = [{"dp": me + bit - 2 * bit * ((me // bit) % 2)} for bit in bits]
        greet([ahead, behind, sibling] + facing)

        def half(g, way):
            return pl.ds(way * (widths[g] // 2), widths[g] // 2)

        def half_of(g, way, whose):
            base = whose * widths[g] + way * (widths[g] // 2)
            return pl.ds(pl.multiple_of(base, 128), widths[g] // 2)

        def at(g, slot):
            return pl.ds(slot * rows[g], rows[g])

        def source_at(g, slot):
            if slotted[g]:
                return at(g, slot)
            there = device((place + n - slot) % n)
            block = there["fsdp"] * n_ctx + there["ctx"]
            return pl.ds(pl.multiple_of(block * rows[g], rows[g]), rows[g])

        def swap(g, way, slot):
            return pltpu.make_async_remote_copy(
                src_ref=full[g].at[source_at(g, slot), half_of(g, way, 1 - core)],
                dst_ref=near[g].at[at(g, slot), half(g, way)],
                send_sem=pair_send.at[g, way, slot],
                recv_sem=pair_recv.at[g, way, slot],
                device_id=sibling,
                device_id_type=MESH,
            )

        def step(g, way, t):
            slot = t if way == 0 else n - t
            source = near[g].at[at(g, slot), half(g, way)] if t == 1 else land[g].at[way, t - 2]
            return pltpu.make_async_remote_copy(
                src_ref=source,
                dst_ref=land[g].at[way, t - 1],
                send_sem=send.at[g, way, t],
                recv_sem=recv.at[g, way, t],
                device_id=ahead if way == 0 else behind,
                device_id_type=MESH,
            )

        def face(g, k):
            return pltpu.make_async_remote_copy(
                src_ref=done[g].at[k],
                dst_ref=extra[g].at[k],
                send_sem=x_send.at[g, k],
                recv_sem=x_recv.at[g, k],
                device_id=facing[k],
                device_id_type=MESH,
            )

        def end(g):
            return pltpu.make_async_remote_copy(
                src_ref=done[g].at[len(bits)],
                dst_ref=back[g],
                send_sem=end_send.at[g],
                recv_sem=end_recv.at[g],
                device_id=sibling,
                device_id_type=MESH,
            )

        for t in list(range(1, n)) + [0]:
            for g in range(count):
                swap(g, 0, t).start()
                swap(g, 1, (n - t) % n).start()
        spread.start(0)
        for t in range(1, n):
            for g in range(count):
                for way in range(2):
                    slot = t if way == 0 else n - t
                    swap(g, way, slot).wait_recv()
                    cols = half(g, way)
                    value = full[g][source_at(g, slot), half_of(g, way, core)].astype(F32)
                    value = value + near[g][at(g, slot), cols].astype(F32)
                    if t == 1:
                        near[g][at(g, slot), cols] = value.astype(kinds[g])
                    else:
                        step(g, way, t - 1).wait_recv()
                        land[g][way, t - 2] = (value + land[g][way, t - 2].astype(F32)).astype(kinds[g])
                    step(g, way, t).start()
            if t == n - 2:
                spread.arrive(0)
                spread.start(1)
        for g in range(count):
            for way in range(2):
                swap(g, way, 0).wait_recv()
                step(g, way, n - 1).wait_recv()
                cols = half(g, way)
                value = full[g][source_at(g, 0), half_of(g, way, core)].astype(F32)
                value = value + near[g][at(g, 0), cols].astype(F32)
                done[g][0, :, cols] = (value + land[g][way, n - 2].astype(F32)).astype(kinds[g])
            if bits:
                face(g, 0).start()
        for k in range(len(bits)):
            for g in range(count):
                face(g, k).wait_recv()
                done[g][k + 1] = (done[g][k].astype(F32) + extra[g][k].astype(F32)).astype(kinds[g])
                if k + 1 < len(bits):
                    face(g, k + 1).start()
        for g in range(count):
            end(g).start()
            here = pl.ds(pl.multiple_of(core * widths[g], 128), widths[g])
            outs[g][:, here] = done[g][len(bits)].astype(F32)
        for g in range(count):
            end(g).wait_recv()
            here = pl.ds(pl.multiple_of((1 - core) * widths[g], 128), widths[g])
            outs[g][:, here] = back[g][...].astype(F32)
        spread.arrive(1)
        spread.last()
        for g in range(count):
            end(g).wait_send()
            for k in range(len(bits)):
                face(g, k).wait_send()
            for way in range(2):
                for t in range(1, n):
                    step(g, way, t).wait_send()
                for slot in range(n):
                    swap(g, way, slot).wait_send()

    dma = pltpu.SemaphoreType.DMA
    groups = list(zip(rows, widths, kinds))
    out = pl.pallas_call(
        kernel,
        in_specs=[WHOLE] * count + [ANY] * len(sums),
        out_specs=[WHOLE] * count + [ANY] * (len(sums) * others),
        out_shape=[jax.ShapeDtypeStruct((r, 2 * w), F32) for r, w, _ in groups]
        + [jax.ShapeDtypeStruct(a.shape, BF) for a in sums for _ in range(others)],
        scratch_shapes=[pltpu.VMEM((n * r, w), kind) for r, w, kind in groups]
        + [pltpu.VMEM((2, n - 1, r, w // 2), kind) for r, w, kind in groups]
        + [pltpu.VMEM((len(bits) + 1, r, w), kind) for r, w, kind in groups]
        + [pltpu.VMEM((max(1, len(bits)), r, w), kind) for r, w, kind in groups]
        + [pltpu.VMEM((r, w), kind) for r, w, kind in groups]
        + [
            dma((count, 2, n)),
            dma((count, 2, n)),
            dma((count, 2, n)),
            dma((count, 2, n)),
            dma((count, max(1, len(bits)))),
            dma((count, max(1, len(bits)))),
            dma((count,)),
            dma((count,)),
        ]
        + spread_scratch(len(sums), n_dp),
        compiler_params=pltpu.CompilerParams(
            collective_id=1, has_side_effects=True, vmem_limit_bytes=60 * MIB
        ),
        cost_estimate=cost(0, sum(12 * n * r * w for r, w, _ in groups)),
    )(*fulls, *sums)
    return out[:count], [out[count + k * others : count + (k + 1) * others] for k in range(len(sums))]


class Ring:
    def __init__(self, n_fsdp, n_ctx):
        order = []
        for c in range(n_ctx):
            rows = range(n_fsdp) if c % 2 == 0 else reversed(range(n_fsdp))
            order += [f * n_ctx + c for f in rows]
        self.order = order
        self.size = n = len(order)
        place = [0] * n
        for k, block in enumerate(order):
            place[block] = k
        self.place = place
        self.block = lax.axis_index(GRID)
        self.rank = jnp.array(place, jnp.int32)[self.block]

    def slot_blocks(self):
        slots = jnp.arange(self.size, dtype=jnp.int32)
        return jnp.array(self.order, jnp.int32)[(self.rank - slots) % self.size]

    def to_slots(self, array, axis=1, deps=()):
        return reorder(array, self.slot_blocks(), axis, deps)

    def from_slots(self, array, axis=1):
        return reorder(array, (self.rank - jnp.array(self.place, jnp.int32)) % self.size, axis)


class Team:
    def __init__(self, size):
        self.size = size
        self.rank = lax.axis_index("dp")
        self.bits = [1 << k for k in range(size.bit_length() - 1)]
        self.order = [0]
        for bit in reversed(self.bits):
            self.order = self.order + [m ^ bit for m in self.order]

    def swap(self, value, bit):
        return lax.ppermute(value, "dp", [(k, k ^ bit) for k in range(self.size)])

    def scatter(self, parts):
        for bit in self.bits:
            half = len(parts) // 2
            got = [self.swap(part.astype(BF), bit) for part in parts[half:]]
            parts = [kept + part.astype(F32) for kept, part in zip(parts[:half], got)]
        return parts[0]


def shards(sizes, x_in, span_order, attn_gain, w_qkv, w_out, ffn_gain, w_gate_up, w_down, cotangent):
    n_dp, n_fsdp, n_ctx = sizes
    ring = Ring(n_fsdp, n_ctx)
    team = Team(n_dp)
    n = ring.size
    width = x_in.shape[-1]
    rows = width // n
    tokens = x_in.reshape(-1, width)
    span = tokens.shape[0]
    rank = lax.axis_index("ctx")
    qwidth = HEADS * HD
    kvwidth = KV_HEADS * HD
    ffwidth = w_down.shape[1]
    order = span_order.reshape(-1)
    near = [(rank + k) % n_ctx for k in range(n_ctx)]
    offsets = jnp.arange(span, dtype=jnp.int32)
    query_pos = order[rank] * span + offsets
    seen = jnp.stack([order[c] < order[rank] for c in near[1:]]).astype(jnp.int32)
    tables = rope_tables(query_pos.astype(F32))

    ffq = ffwidth // n_dp
    sub = ffq // SUBS
    grad_y = cotangent.reshape(span, width)
    dy = ring.to_slots(grad_y)
    gains = jnp.concatenate([attn_gain[None], ffn_gain[None], jnp.zeros((14, rows), BF)], 0)
    qkv, kv_far, normed_one, wqkv, wout, gains = opening(sizes, tokens, w_qkv, w_out, gains, tables)
    attn_t, lse, hidden_one, normed_two, x_others, dy_others, weights_a = attend_forward(
        sizes, tokens, qkv, kv_far, seen, wout, gains, dy, w_gate_up, w_down
    )
    xs = [normed_two] + list(x_others)
    dys = [dy] + list(dy_others)
    gains = gains[:, :2][(ring.rank - jnp.array(ring.place, jnp.int32)) % n]
    gain_one = gains[:, 0].reshape(-1).astype(F32)
    gain_two = gains[:, 1].reshape(-1).astype(F32)
    inputs = tokens.astype(F32)
    scale_one = inv_rms(inputs)
    scale_two = inv_rms(hidden_one)

    y, dn, grads_a, weights_b = feed_forward(
        sizes, xs, dys, [[w] for w in weights_a], None, (w_gate_up, w_down), False, 2
    )
    y, dn, grads_b, sums_a = feed_forward(
        sizes, xs, dys, [[w] for w in weights_b], list(zip(y, dn)), grads_a, True, 3
    )

    d_normed_two = ring.from_slots(sum(part.astype(F32) for part in dn))
    d_hidden_norm, d_gain_two = norm_back(hidden_one, scale_two, gain_two, d_normed_two)
    d_hidden = grad_y.astype(F32) + d_hidden_norm
    d_proj = d_hidden.astype(BF)

    d_attn = matmul_rows(d_proj, wout).astype(BF)
    d_qkv, part_out, part_qkv, sums_b, others_a = attend_backward(
        sizes, qkv, kv_far, d_attn, lse, seen, tables, attn_t, d_proj, normed_one, grads_b, sums_a, 4
    )
    d_normed_one = matmul_rows(d_qkv, wqkv)
    d_input_norm, d_gain_one = norm_back(inputs, scale_one, gain_one, d_normed_one)
    grad_input = d_hidden + d_input_norm

    room = max(rows, 256)

    def by_slot(gain):
        blocks = gain.reshape(n, 1, rows)[ring.slot_blocks()]
        return jnp.pad(blocks, ((0, 0), (0, 7), (0, room - rows))).reshape(n * 8, room)

    part_gain = jnp.concatenate([by_slot(d_gain_one), by_slot(d_gain_two)], 1)
    (grad_qkv, grad_out, grad_gain), others_b = closing(
        sizes, (part_qkv, part_out, part_gain), (True, False, True), sums_b
    )

    placed, columns = [], []
    for q in range(SUBS):
        blocks = [sums_a[q]] + list(others_a[q]) if q < 2 else [sums_b[q - 2]] + list(others_b[q - 2])
        for m, block in zip(team.order, blocks):
            placed.append(block)
            columns.append((team.rank ^ m) * ffq + q * sub)
    grad_gate_up, grad_down = place_grads(placed, jnp.stack(columns).astype(jnp.int32), sub, ffwidth)

    y_out = hidden_one + ring.from_slots(team.scatter(y))
    return (
        y_out.astype(BF).reshape(x_in.shape),
        grad_input.reshape(x_in.shape),
        grad_gain[0, :rows],
        grad_qkv,
        grad_out,
        grad_gain[0, room : room + rows],
        grad_gate_up,
        grad_down,
    )


def solution(mesh):
    sizes = (mesh.shape["dp"], mesh.shape["fsdp"], mesh.shape["ctx"])
    tokens = P(("dp", "fsdp"), "ctx", None)
    weight = P(("fsdp", "ctx"), None)
    gain = P(("fsdp", "ctx"))

    def body(*args):
        return shards(sizes, *args)

    return jax.shard_map(
        body,
        mesh=mesh,
        in_specs=(tokens, P(("dp", "fsdp"), None), gain, weight, weight, gain, weight, weight, tokens),
        out_specs=(tokens, tokens, gain, weight, weight, gain, weight, weight),
        check_vma=False,
    )
```

time: 4870 us -> 959 us (0.20)
  waiting for transfers between devices: 4090 us -> 0.01 us
  Pallas kernels: 0 us -> 840 us
  matrix products: 450 us -> 17.7 us
  other arithmetic: 157 us -> 25.4 us
  blocking collectives: 72.8 us -> 0 us
    all_gather x6 -> x0, waiting for transfers between devices: 2070 us -> none  [the longest x1 1260 us: shards(): lax.all_gather(w_gate_up, ('fsdp', 'ctx'), axis=0, tiled=True)]
    unnamed x11 -> x0, waiting for transfers between devices: 1850 us -> none
    pallas_call x0 -> x10, Pallas kernels: none -> 840 us  [the longest x2 263 us: feed_forward(): pl.pallas_call(kernel, in_specs=[ANY] * len(operands), out_specs=[ANY] *...]
    dot_general x64 -> x0, matrix products: 357 us -> none  [the longest x4 104 us: matmul(): return jnp.dot(left, right, preferred_element_type=jnp.float32)]
    psum x1 -> x0, waiting for transfers between devices: 176 us -> none  [shards(): lax.psum(shard_grads.astype(jnp.bfloat16), 'dp').astype(jnp.float32)]
    concatenate x2 -> x3, other arithmetic: 79.9 us -> 2.88 us  [the longest x1 1.55 us: rope_tables(): jnp.concatenate([zero, sine] * 2, -1)]
    dot_general x4 -> x2, matrix products: 93.2 us -> 17.7 us  [matmul_rows(): lax.dot_general(left, right, (((1,), (1,)), ((), ())), preferred_element_...]
  transfers between devices with their start and end apart: 10 -> 3, of which waited for: 7 -> 0; matrix products, arithmetic and copies ran while one was open for 5% -> 4% of each run, Pallas kernels for 0% -> 34%
where the time goes in v1:
time: 959 us; the launch traced here: 948 us
  Pallas kernels  840 us (88%)
  local copies, waits for them, and re-layouts  53.2 us (6%)
  other arithmetic  25.4 us (3%)
  matrix products  17.7 us (2%)
    pallas_call x2, Pallas kernels, feed_forward(): pl.pallas_call(kernel, in_specs=[ANY] * len(operands), out_specs=[ANY] *...  263 us
    pallas_call x1, Pallas kernels, attend_backward(): pl.pallas_call(kernel, grid=(pairs,), in_specs=[pl.BlockSpec(memory_space...  160 us
    pallas_call x1, Pallas kernels, closing(): pl.pallas_call(kernel, in_specs=[WHOLE] * count + [ANY] * len(sums), out_...  147 us
    pallas_call x1, Pallas kernels, attend_forward(): pl.pallas_call(kernel, grid=(pairs,), in_specs=[pl.BlockSpec(memory_space...  139 us
    pallas_call x1, Pallas kernels, opening(): pl.pallas_call(kernel, in_specs=[WHOLE, ANY, ANY, ANY, WHOLE, WHOLE, WHOL...  116 us
    unnamed x124, local copies, waits for them, and re-layouts  44 us
  transfers between devices with their start and end apart: 3, of which 0 were waited for; matrix products, arithmetic and copies ran while one was open for 4% of the time, Pallas kernels for 34%

profile of v1, /device:TPU:1, one launch (start us, length us, event | category | flops | bytes accessed | tf_op | source)
XLA Modules:
  0.0 948.2 jit_solution(12125412761847584514)
XLA Ops:
  9.6 1.6 copy-done.2
  11.2 1.3 shard_map.216.refs_1_.refs_4_
  14.5 1.5 pad_maximum_fusion.2
  16.1 115.6 %shard_map.215 = (bf16[512,3072]{1,0:T(8,128)(2,1)}, bf16[512,1024]{1,0:T(8,128)(2,1)}, bf16[512,2048]{1,0:T(8,128)(2,1)}, bf16[2048,3072]{1,0:T(8,128)(2,1)}, b...) custom-call(bf16[512,2048]{1,0:T(8,128)(2,1)} %bitcast.55, bf16[256,3072]{1,0:T(8,128)(2,1)} %wq_ref.1, ...), custom_call_target="tpu_custom_call" | custom-call | flops 6442450944 | bytes 25165824 | tf_op jit(solution)/shard_map/pallas_call | solution.py:1505
  133.7 138.8 %shard_map.217 = (f32[16,8,512]{2,1,0:T(8,128)S(1)}, bf16[2048,512]{1,0:T(8,128)(2,1)S(1)}, f32[512,2048]{1,0:T(8,128)}, bf16[512,2048]{1,0:T(8,128)(2,1)S(1)}, ...) custom-call(s32[1]{0:T(128)} %bitcast.seen_ref, ...), custom_call_target="tpu_custom_call" | custom-call | flops 8589934592 | bytes 31457280 | tf_op jit(solution)/shard_map/pallas_call | solution.py:976
  275.9 123.6 %shard_map.218 = (bf16[512,2048]{1,0:T(8,128)(2,1)}, bf16[512,2048]{1,0:T(8,128)(2,1)}, bf16[512,2048]{1,0:T(8,128)(2,1)}, bf16[512,2048]{1,0:T(8,128)(2,1)}, bf...) custom-call(bf16[512,2048]{1,0:T(8,128)(2,1)} %copy-done.39, ...), custom_call_target="tpu_custom_call" | custom-call | flops 77309411328 | bytes 41943040 | tf_op jit(solution)/shard_map/pallas_call | solution.py:844
  399.5 139.5 %shard_map.219 = (bf16[512,2048]{1,0:T(8,128)(2,1)}, bf16[512,2048]{1,0:T(8,128)(2,1)}, bf16[512,2048]{1,0:T(8,128)(2,1)}, bf16[512,2048]{1,0:T(8,128)(2,1)}, bf...) custom-call(bf16[512,2048]{1,0:T(8,128)(2,1)} %copy-done.39, ...), custom_call_target="tpu_custom_call" | custom-call | flops 77309411328 | bytes 41943040 | tf_op jit(solution)/shard_map/pallas_call | solution.py:844
  539.1 8.3 collective-permute-start.1
  550.0 2.7 multiply_reduce_fusion.2
  553.6 2.0 shard_map.221
  558.7 1.3 fusion.16.refs_1_
  560.0 1.3 slice-done.1
  561.4 5.7 convolution_convert_fusion.d_ref
  571.9 1.6 copy-done.38
  574.4 1.6 copy-done.42
  576.0 160.2 %shard_map.222 = (bf16[512,3072]{1,0:T(8,128)(2,1)}, bf16[2048,2048]{1,0:T(8,128)(2,1)}, bf16[2048,3072]{1,0:T(8,128)(2,1)}, bf16[256,1536]{1,0:T(8,128)(2,1)S(1...) custom-call(s32[1]{0:T(128)} %bitcast.seen_ref, ...), custom_call_target="tpu_custom_call" | custom-call | flops 21474836480 | bytes 31457280 | tf_op jit(solution)/shard_map/pallas_call | solution.py:1192
  737.3 5.6 add_convert_fusion.1
  742.9 12.0 %fusion.8 = (f32[2048]{0:T(1024)S(1)}, f32[512]{0:T(512)S(1)}, f32[512,2048]{1,0:T(8,128)}) fusion(f32[512]{0:T(512)S(1)} %add_rsqrt_fusion, bf16[1,512,2048]{2,1,0:T(8,128)(2,1)S(1)} %copy-done.46, f32[2048]{0:T(1024)S(1)} %bitcast.62, bf16[512,3072]{1,0:T(8,128)(2,1)S(1)} %copy-done.57, bf16[2048,3072]{1,0:T(8,128)(2,1)} %get-tuple-element.110), kind=kOutput, calls=%fused_computation.14 | convolution fusion | flops 6449788416 | bytes 22040576 | tf_op jit(solution)/shard_map/dot_general | solution.py:26
  756.2 146.5 %shard_map.223 = (f32[256,3072]{1,0:T(8,128)}, f32[256,2048]{1,0:T(8,128)}, f32[8,512]{1,0:T(8,128)}, bf16[256,1536]{1,0:T(8,128)(2,1)}, bf16[256,1536]{1,0:T(8,...) custom-call(bf16[2048,3072]{1,0:T(8,128)(2,1)} %get-tuple-element.11, ...), custom_call_target="tpu_custom_call" | custom-call | bytes 63111168 | tf_op jit(solution)/shard_map/pallas_call | solution.py:1691
  919.9 10.9 %shard_map.224 = (f32[256,16384]{1,0:T(8,128)}, f32[256,8192]{1,0:T(8,128)}) custom-call(s32[16]{0:T(128)S(1)} %stack.68.refs_0_, bf16[256,1536]{1,0:T(8,128)(2,1)S(1)} %copy-done.12, bf16[256,1536]{1,0:T(8,128)(2,1)S(1)} %copy-done.16, bf16[256,1536]{1,0:T(8,128)(2,1)S(1)} %copy-done.18, bf16[256,1536]{1,0:T(8,128)(2,1)S(1)} %copy-done.20, ...), custom_call_target="tpu_custom_call" | custom-call | bytes 37748736 | tf_op jit(solution)/shard_map/pallas_call | solution.py:188
  932.1 3.6 convert_add_fusion.1.source
  935.8 1.6 shard_map.220
  939.3 4.7 fusion.7
  944.0 1.7 copy.32
  (162 shorter events, 51.5 us)
Async XLA Ops:
  399.5 147.9 %copy-start.45 = (bf16[1,512,2048]{2,1,0:T(8,128)(2,1)S(1)}, bf16[1,512,2048]{2,1,0:T(8,128)(2,1)}, u32[]{:S(2)}) copy-start(bf16[1,512,2048]{2,1,0:T(8,128)(2,1)} %param.16) | copy-start | bytes 6291460
  399.5 149.2 %copy-start.56 = (s32[8]{0:T(128)S(1)}, s32[8]{0:T(128)}, u32[]{:S(2)}) copy-start(s32[8]{0:T(128)} %constant.106) | copy-start | bytes 100
  539.1 13.6 %copy-start.54 = (bf16[512,2048]{1,0:T(8,128)(2,1)S(1)}, bf16[512,2048]{1,0:T(8,128)(2,1)}, u32[]{:S(2)}) copy-start(bf16[512,2048]{1,0:T(8,128)(2,1)} %get-tuple-element.100) | copy-start | bytes 6291460
  539.1 198.2 %collective-permute-start.1 = (bf16[512,2048]{1,0:T(8,128)(2,1)}, bf16[512,2048]{1,0:T(8,128)(2,1)}, u32[]{:S(2)}, u32[]{:S(2)}) collective-permute-start(bf16[512,2048]{1,0:T(8,128)(2,1)} %get-tuple-element.99), channel_id=1, source_target_pairs={{0,8},{8,0},{16,24},{24,16},{1,9},{9,1},{17,25},{25,17},{2,10},{10... | collective-permute-start | bytes 6291464 | tf_op jit(solution)/shard_map/ppermute | solution.py:1757
  547.3 384.8 %collective-permute-start = (bf16[512,2048]{1,0:T(8,128)(2,1)}, bf16[512,2048]{1,0:T(8,128)(2,1)}, u32[]{:S(2)}, u32[]{:S(2)}) collective-permute-start(bf16[512,2048]{1,0:T(8,128)(2,1)} %get-tuple-element.97), channel_id=1, source_target_pairs={{0,8},{8,0},{16,24},{24,16},{1,9},{9,1},{17,25},{25,17},{2,10},{10... | collective-permute-start | bytes 6291464 | tf_op jit(solution)/shard_map/ppermute | solution.py:1757
  561.4 5.7 copy-start.52
  561.4 6.3 copy-start.6
  561.4 6.3 copy-start.33
  576.0 161.2 %copy-start.51 = (bf16[512,2048]{1,0:T(8,128)(2,1)S(1)}, bf16[512,2048]{1,0:T(8,128)(2,1)}, u32[]{:S(2)}) copy-start(bf16[512,2048]{1,0:T(8,128)(2,1)} %get-tuple-element.98) | copy-start | bytes 6291460
  737.2 17.7 %copy-start.7 = (bf16[256,1536]{1,0:T(8,128)(2,1)}, bf16[256,1536]{1,0:T(8,128)(2,1)S(1)}, u32[]{:S(2)}) copy-start(bf16[256,1536]{1,0:T(8,128)(2,1)S(1)} %get-tuple-element.113.refs_3_.refs_9_) | copy-start | bytes 2359300
  737.2 17.7 %copy-start.9 = (bf16[256,1536]{1,0:T(8,128)(2,1)}, bf16[256,1536]{1,0:T(8,128)(2,1)S(1)}, u32[]{:S(2)}) copy-start(bf16[256,1536]{1,0:T(8,128)(2,1)S(1)} %get-tuple-element.114.refs_4_.refs_13_) | copy-start | bytes 2359300
  737.2 17.7 %copy-start.15 = (bf16[256,1536]{1,0:T(8,128)(2,1)}, bf16[256,1536]{1,0:T(8,128)(2,1)S(1)}, u32[]{:S(2)}) copy-start(bf16[256,1536]{1,0:T(8,128)(2,1)S(1)} %get-tuple-element.118.refs_2_) | copy-start | bytes 2359300
  737.2 17.7 %copy-start.17 = (bf16[256,1536]{1,0:T(8,128)(2,1)}, bf16[256,1536]{1,0:T(8,128)(2,1)S(1)}, u32[]{:S(2)}) copy-start(bf16[256,1536]{1,0:T(8,128)(2,1)S(1)} %get-tuple-element.119.refs_3_) | copy-start | bytes 2359300
  737.2 17.7 %copy-start.19 = (bf16[256,1536]{1,0:T(8,128)(2,1)}, bf16[256,1536]{1,0:T(8,128)(2,1)S(1)}, u32[]{:S(2)}) copy-start(bf16[256,1536]{1,0:T(8,128)(2,1)S(1)} %get-tuple-element.120.refs_4_) | copy-start | bytes 2359300
  737.2 17.7 %copy-start.21 = (bf16[256,1536]{1,0:T(8,128)(2,1)}, bf16[256,1536]{1,0:T(8,128)(2,1)S(1)}, u32[]{:S(2)}) copy-start(bf16[256,1536]{1,0:T(8,128)(2,1)S(1)} %get-tuple-element.121.refs_6_) | copy-start | bytes 2359300
  737.2 17.7 %copy-start.23 = (bf16[256,1536]{1,0:T(8,128)(2,1)}, bf16[256,1536]{1,0:T(8,128)(2,1)S(1)}, u32[]{:S(2)}) copy-start(bf16[256,1536]{1,0:T(8,128)(2,1)S(1)} %get-tuple-element.122.refs_7_) | copy-start | bytes 2359300
  737.2 5.6 copy-start.46
  737.2 5.6 copy-start.57
  742.8 189.3 %collective-permute-start.2 = (bf16[512,2048]{1,0:T(8,128)(2,1)}, bf16[512,2048]{1,0:T(8,128)(2,1)}, u32[]{:S(2)}, u32[]{:S(2)}) collective-permute-start(bf16[512,2048]{1,0:T(8,128)(2,1)} %add_convert_fusion.1), channel_id=1, source_target_pairs={{0,16},{8,24},{16,0},{24,8},{1,17},{9,25},{17,1},{25,9},{2,18},{10... | collective-permute-start | bytes 6291464 | tf_op jit(solution)/shard_map/ppermute | solution.py:1757
  756.2 146.6 %copy-start.8 = (bf16[256,1536]{1,0:T(8,128)(2,1)S(1)}, bf16[256,1536]{1,0:T(8,128)(2,1)}, u32[]{:S(2)}) copy-start(bf16[256,1536]{1,0:T(8,128)(2,1)} %copy-done.7) | copy-start | bytes 2359300
  919.9 12.2 %copy-start.50 = (bf16[512,2048]{1,0:T(8,128)(2,1)S(1)}, bf16[512,2048]{1,0:T(8,128)(2,1)}, u32[]{:S(2)}) copy-start(bf16[512,2048]{1,0:T(8,128)(2,1)} %get-tuple-element.96) | copy-start | bytes 6291460
  932.1 5.3 copy-start.47
  932.1 5.2 copy-start.48
  939.2 4.7 copy-start.49
  (39 other events, 60.0 us)

commit v2 on v1

--- a/solution.py
+++ b/solution.py
@@ -199,7 +199,7 @@
             pltpu.SemaphoreType.DMA((2,)),
             pltpu.SemaphoreType.DMA((2, 3)),
         ],
-        compiler_params=params(32),
+        compiler_params=params(60),
         cost_estimate=cost(0, rows * ffwidth * 18),
     )(columns, *pieces)
 
@@ -335,39 +335,54 @@
 
 
 class RingReduce:
-    def __init__(self, sizes, parts, out, land, own_v, land_v, send_v, own_sem, land_sem, out_sem, send, recv):
+    def __init__(self, sizes, parts, out, land, own_v, own_sem, out_sem, send, recv, staged=None):
         self.n = sizes[1] * sizes[2]
-        self.rows = out[0].shape[0]
-        self.parts, self.out, self.land = parts, out, land
-        self.own_v, self.land_v, self.send_v = own_v, land_v, send_v
-        self.own_sem, self.land_sem, self.out_sem = own_sem, land_sem, out_sem
-        self.send, self.recv = send, recv
+        self.rows, self.wide = out[0].shape
+        self.parts, self.out, self.land, self.own_v = parts, out, land, own_v
+        self.own_sem, self.out_sem, self.send, self.recv = own_sem, out_sem, send, recv
+        self.staged = staged
         place, device = ring_place(sizes[1])
         self.partners = [device((place + 1) % self.n), device((place + self.n - 1) % self.n)]
+
+    def lanes(self, h):
+        return pl.ds(pl.multiple_of(h * (self.wide // 2), 128), self.wide // 2)
 
     def load_own(self, way, t):
         slot = t % self.n if way == 0 else self.n - t
         return pltpu.make_async_copy(
             self.parts[way].at[pl.ds(slot * self.rows, self.rows)],
-            self.own_v.at[way, t % 2],
-            self.own_sem.at[way, t % 2],
+            self.own_v.at[way, t % 3],
+            self.own_sem.at[way, t % 3],
         )
 
-    def load_land(self, way, t):
-        return pltpu.make_async_copy(self.land.at[way, t - 1], self.land_v.at[way], self.land_sem.at[way])
-
-    def ring(self, way, t):
+    def ring(self, source, way, t, h):
         return pltpu.make_async_remote_copy(
-            src_ref=self.send_v.at[way, t % 2],
-            dst_ref=self.land.at[way, t - 1],
-            send_sem=self.send.at[way, t],
-            recv_sem=self.recv.at[way, t],
+            src_ref=source,
+            dst_ref=self.land.at[way, h, t - 1],
+            send_sem=self.send.at[way, h, t],
+            recv_sem=self.recv.at[way, h, t],
             device_id=self.partners[way],
             device_id_type=MESH,
         )
 
+    def arrived(self, way, t, h):
+        return self.ring(self.land.at[way, h, t - 1], way, t, h)
+
+    def start(self, way, h):
+        return self.ring(self.own_v.at[way, 1, :, self.lanes(h)], way, 1, h)
+
+    def source(self, way, t, h):
+        if self.staged:
+            return self.staged[1].at[way, h]
+        return self.land.at[way, h, t - 2]
+
+    def fetch(self, way, t, h):
+        return pltpu.make_async_copy(
+            self.land.at[way, h, t - 1], self.staged[0].at[way], self.staged[2].at[way]
+        )
+
     def save(self, way):
-        return pltpu.make_async_copy(self.own_v.at[way, self.n % 2], self.out[way], self.out_sem.at[way])
+        return pltpu.make_async_copy(self.own_v.at[way, self.n % 3], self.out[way], self.out_sem.at[way])
 
     def first(self):
         for way in range(2):
@@ -375,114 +390,73 @@
             self.load_own(way, 2).start()
         for way in range(2):
             self.load_own(way, 1).wait()
-            self.send_v[way, 1] = self.own_v[way, 1]
-            self.ring(way, 1).start()
-
-    def tick(self, t):
+            for h in range(2):
+                self.start(way, h).start()
+
+    def total(self, way, t, h):
+        brought = self.staged[0][way] if self.staged else self.land[way, h, t - 2]
+        return self.own_v[way, t % 3, :, self.lanes(h)].astype(F32) + brought.astype(F32)
+
+    def step(self, u):
+        t, h = u // 2, u % 2
         for way in range(2):
-            self.ring(way, t - 1).wait_recv()
-            self.load_land(way, t - 1).start()
-            self.load_own(way, t + 1).start()
+            self.arrived(way, t - 1, h).wait_recv()
+            if self.staged:
+                self.fetch(way, t - 1, h).start()
+
+            @pl.when(h == 0)
+            def _():
+                self.load_own(way, t).wait()
+
+                @pl.when(t == 3)
+                def _():
+                    for half in range(2):
+                        self.start(way, half).wait_send()
+
+                self.load_own(way, t + 1).start()
+
         for way in range(2):
-            self.load_own(way, t).wait()
-            self.load_land(way, t - 1).wait()
-
-            @pl.when(t >= 3)
-            def _():
-                self.ring(way, t - 2).wait_send()
-
-            total = self.own_v[way, t % 2].astype(F32) + self.land_v[way].astype(F32)
-            self.send_v[way, t % 2] = total.astype(BF)
-            self.ring(way, t).start()
+            if self.staged:
+                self.fetch(way, t - 1, h).wait()
+
+                @pl.when(t >= 3)
+                def _():
+                    self.ring(self.source(way, t - 1, h), way, t - 1, h).wait_send()
+
+                self.staged[1][way, h] = self.total(way, t, h).astype(BF)
+            else:
+                self.land[way, h, t - 2] = self.total(way, t, h).astype(BF)
+            self.ring(self.source(way, t, h), way, t, h).start()
 
     def last(self):
         n = self.n
         for way in range(2):
-            self.ring(way, n - 1).wait_recv()
-            self.load_land(way, n - 1).start()
-        for way in range(2):
             self.load_own(way, n).wait()
-            self.load_land(way, n - 1).wait()
-            total = self.own_v[way, n % 2].astype(F32) + self.land_v[way].astype(F32)
-            self.own_v[way, n % 2] = total.astype(BF)
+            for h in range(2):
+                self.arrived(way, n - 1, h).wait_recv()
+                if self.staged:
+                    self.fetch(way, n - 1, h).start()
+                    self.fetch(way, n - 1, h).wait()
+                half = self.wide // 2
+                total = self.total(way, n, h).astype(BF)
+                self.own_v[way, n % 3, :, h * half : (h + 1) * half] = total
             self.save(way).start()
         for way in range(2):
-            self.ring(way, n - 2).wait_send()
-            self.ring(way, n - 1).wait_send()
+            for h in range(2):
+                for t in range(n - 1 if self.staged else 2, n):
+                    self.ring(self.source(way, t, h), way, t, h).wait_send()
             self.save(way).wait()
 
 
-class RingReduceNear(RingReduce):
-    def __init__(self, sizes, parts, out, land, own_v, own_sem, out_sem, send, recv):
-        RingReduce.__init__(self, sizes, parts, out, land, own_v, None, None, own_sem, None, out_sem, send, recv)
-
-    def ring(self, way, t, first=False):
-        return pltpu.make_async_remote_copy(
-            src_ref=self.own_v.at[way, 1] if first else self.land.at[way, t - 2],
-            dst_ref=self.land.at[way, t - 1],
-            send_sem=self.send.at[way, t],
-            recv_sem=self.recv.at[way, t],
-            device_id=self.partners[way],
-            device_id_type=MESH,
-        )
-
-    def arrived(self, way, t):
-        target = self.land.at[way, t - 1]
-        return pltpu.make_async_remote_copy(
-            src_ref=target,
-            dst_ref=target,
-            send_sem=self.send.at[way, t],
-            recv_sem=self.recv.at[way, t],
-            device_id=self.partners[way],
-            device_id_type=MESH,
-        )
-
-    def first(self):
-        for way in range(2):
-            self.load_own(way, 1).start()
-            self.load_own(way, 2).start()
-        for way in range(2):
-            self.load_own(way, 1).wait()
-            self.ring(way, 1, True).start()
-
-    def tick(self, t):
-        for way in range(2):
-            self.arrived(way, t - 1).wait_recv()
-            self.load_own(way, t).wait()
-            total = self.own_v[way, t % 2].astype(F32) + self.land[way, t - 2].astype(F32)
-            self.land[way, t - 2] = total.astype(BF)
-            self.ring(way, t).start()
-
-            @pl.when(t == 2)
-            def _():
-                self.ring(way, 1, True).wait_send()
-
-            self.load_own(way, t + 1).start()
-
-    def last(self):
-        n = self.n
-        for way in range(2):
-            self.arrived(way, n - 1).wait_recv()
-            self.load_own(way, n).wait()
-            total = self.own_v[way, n % 2].astype(F32) + self.land[way, n - 2].astype(F32)
-            self.own_v[way, n % 2] = total.astype(BF)
-            self.save(way).start()
-        for way in range(2):
-            for t in range(2, n):
-                self.ring(way, t).wait_send()
-            self.save(way).wait()
-
-
-def near_scratch(n, rows, wide):
+def reduce_scratch(n, rows, wide, near):
     dma = pltpu.SemaphoreType.DMA
-    return [
-        pltpu.VMEM((2, n - 1, rows, wide), BF),
-        pltpu.VMEM((2, 2, rows, wide), BF),
-        dma((2, 2)),
-        dma((2,)),
-        dma((2, n)),
-        dma((2, n)),
-    ]
+    land = [pltpu.VMEM((2, 2, n - 1, rows, wide // 2), BF)] if near else []
+    stage = [pltpu.VMEM((2, rows, wide // 2), BF), pltpu.VMEM((2, 2, rows, wide // 2), BF), dma((2,))]
+    return (
+        land
+        + [pltpu.VMEM((2, 3, rows, wide), BF), dma((2, 3)), dma((2,)), dma((2, 2, n)), dma((2, 2, n))]
+        + ([] if near else stage)
+    )
 
 
 class TeamSpread:
@@ -531,20 +505,6 @@
 
 def spread_scratch(count, size):
     return [pltpu.SemaphoreType.DMA((count, size)), pltpu.SemaphoreType.DMA((count, size))]
-
-
-def reduce_scratch(n, rows, wide):
-    dma = pltpu.SemaphoreType.DMA
-    return [
-        pltpu.VMEM((2, 2, rows, wide), BF),
-        pltpu.VMEM((2, rows, wide), BF),
-        pltpu.VMEM((2, 2, rows, wide), BF),
-        dma((2, 2)),
-        dma((2,)),
-        dma((2,)),
-        dma((2, n)),
-        dma((2, n)),
-    ]
 
 
 def feed_forward(sizes, xs, dys, weights, before, ring_parts, reducing, ident):
@@ -588,7 +548,7 @@
             cb, c_sems = take(2)
         if reducing:
             swap_send, swap_recv, face_send, face_recv = take(4)
-            ring = RingReduce(sizes, part_refs, ring_outs, land, *refs)
+            ring = RingReduce(sizes, part_refs, ring_outs, land, *refs[:5], staged=refs[5:])
         else:
             ring = RingGather(sizes, own_columns(n_dp, *part_refs, SUBS // 2), ring_outs, *refs)
         me = lax.axis_index("dp")
@@ -684,7 +644,13 @@
                 copy.wait()
 
         def ticks(lo, hi):
-            lax.fori_loop(2 + lo * (n - 2) // total, 2 + hi * (n - 2) // total, lambda t, c: (ring.tick(t), c)[1], 0)
+            if reducing:
+                count, base, act = 2 * (n - 2), 4, ring.step
+            else:
+                count, base, act = n - 2, 2, ring.tick
+            lax.fori_loop(
+                base + lo * count // total, base + hi * count // total, lambda t, c: (act(t), c)[1], 0
+            )
 
         on_block(0, lambda m: go(loads(m, 0)))
         partners = list(ring.partners)
@@ -810,7 +776,7 @@
     shape = lambda a, b: jax.ShapeDtypeStruct((a, b), BF)
     outs = [shape(span, width)] * (2 * team) + [shape(width, wide)] * 2
     if reducing:
-        outs += [shape(rows, wide)] * 2 + [jax.ShapeDtypeStruct((2, n - 1, rows, wide), BF)]
+        outs += [shape(rows, wide)] * 2 + [jax.ShapeDtypeStruct((2, 2, n - 1, rows, wide // 2), BF)]
         outs += [shape(span, width)] * (max(1, inside) + 1)
     else:
         outs += [shape(width, wide)] * 2
@@ -837,7 +803,7 @@
         scratch += [pltpu.VMEM((3 if inside else 2, tile, width), BF), dma((3,))]
     if reducing:
         scratch += [dma((max(1, inside),)), dma((max(1, inside),)), dma(()), dma(())]
-        scratch += reduce_scratch(n, rows, wide)
+        scratch += reduce_scratch(n, rows, wide, False)
     else:
         scratch += gather_scratch(n, rows, wide)
     operands = list(xs) + list(dys) + pieces + carried + list(ring_parts)
@@ -1007,7 +973,7 @@
         + spread_scratch(1, n_dp)
         + gather_scratch(n, rows, wide),
         compiler_params=pltpu.CompilerParams(
-            collective_id=5, has_side_effects=True, vmem_limit_bytes=48 * MIB
+            collective_id=5, has_side_effects=True, vmem_limit_bytes=58 * MIB
         ),
         cost_estimate=cost(pairs * 2 * span * (span + far) * 128 * 4, 30 * MIB),
     )(seen, qkv, qkv, qkv, kv_far, kv_far, x, gains, w_out, dy, w_gate_up, w_down)
@@ -1025,7 +991,7 @@
     pairs = HEADS // 2
     tile = min(span, 256)
     rows, wide = ring_parts[0].shape[0] // n, ring_parts[0].shape[1]
-    early = 4 * (n - 2) // 7
+    early = 4 + 8 * (n - 2) // 6
     width = normed.shape[1]
     qkvwidth = qwidth + 2 * kvwidth
     part = max(rows, 128)
@@ -1046,7 +1012,7 @@
         dqkv_v, dkv, dkv_far, give, got, save_sem, kv_send, kv_recv = take(8)
         attn_v, proj_v, normed_v, stage, load_sems, stage_sems = take(6)
         spread_send, spread_recv = take(2)
-        ring = RingReduceNear(sizes, parts, ring_outs, *refs)
+        ring = RingReduce(sizes, parts, ring_outs, *refs)
         spread = TeamSpread(
             n_dp, own_sums, [blocks_out[k * others : (k + 1) * others] for k in range(2)], spread_send, spread_recv
         )
@@ -1104,9 +1070,9 @@
             spread.start(1)
 
         lax.fori_loop(
-            2 + group * early // pairs,
-            2 + (group + 1) * early // pairs,
-            lambda t, c: (ring.tick(t), c)[1],
+            4 + group * (early - 4) // pairs,
+            4 + (group + 1) * (early - 4) // pairs,
+            lambda u, c: (ring.step(u), c)[1],
             0,
         )
 
@@ -1157,12 +1123,11 @@
 
             for k in range(1, n_ctx):
                 back(k).start()
-            middle = (2 + early + n) // 2
-            for t in range(2 + early, middle):
-                ring.tick(t)
             for copy in loads:
                 copy.wait()
+            ring.step(early)
             product(go_out, qwidth, lambda at: dot_nn(attn_v[at, :], proj_v[...]))
+            ring.step(early + 1)
             for k in range(1, n_ctx):
                 back(k).wait_recv()
             for at in range(0, 2 * kvwidth, 128):
@@ -1174,10 +1139,10 @@
                 dqkv_v[:, qwidth + at : qwidth + at + 128] = piece.astype(BF)
             save = pltpu.make_async_copy(dqkv_v, dqkv_out, save_sem)
             save.start()
-            for t in range(middle, n - 1):
-                ring.tick(t)
+            lax.fori_loop(early + 2, 2 * n - 1, lambda u, c: (ring.step(u), c)[1], 0)
             product(gq_out, qkvwidth, lambda at: dot_tn(normed_v[:, at], dqkv_v[...]))
-            ring.tick(n - 1)
+            if early + 2 < 2 * n:
+                ring.step(2 * n - 1)
             spread.arrive(1)
             ring.last()
             spread.last()
@@ -1230,9 +1195,9 @@
             dma((2,)),
         ]
         + spread_scratch(2, n_dp)
-        + near_scratch(n, rows, wide),
+        + reduce_scratch(n, rows, wide, True),
         compiler_params=pltpu.CompilerParams(
-            collective_id=ident, has_side_effects=True, vmem_limit_bytes=40 * MIB
+            collective_id=ident, has_side_effects=True, vmem_limit_bytes=58 * MIB
         ),
         cost_estimate=cost(pairs * 2 * span * (span + far) * 128 * 10, 30 * MIB),
     )(seen, qkv, qkv, qkv, kv_far, kv_far, d_attn, lse, *tables, attn_t, d_proj, normed, *ring_parts, *sums)
@@ -1557,6 +1522,8 @@
         full, own_sums = take(count), take(len(sums))
         outs, blocks_out = take(count), take(len(sums) * others)
         near, land, done, extra, back = take(count), take(count), take(count), take(count), take(count)
+        own = take(count)
+        (own_sems,) = take(1)
         send, recv, pair_send, pair_recv, x_send, x_recv, end_send, end_recv = take(8)
         spread = TeamSpread(
             n_dp, own_sums, [blocks_out[k * others : (k + 1) * others] for k in range(len(sums))], *refs
@@ -1628,38 +1595,59 @@
                 device_id_type=MESH,
             )
 
-        for t in list(range(1, n)) + [0]:
-            for g in range(count):
-                swap(g, 0, t).start()
-                swap(g, 1, (n - t) % n).start()
+        def own_load(g, way, t):
+            slot = t % n if way == 0 else n - t
+            return pltpu.make_async_copy(
+                full[g].at[source_at(g, slot), half_of(g, way, core)],
+                own[g].at[way, t % 2],
+                own_sems.at[g, way, t % 2],
+            )
+
+        def both(g, way, t, slot):
+            own_load(g, way, t).wait()
+            swap(g, way, slot).wait_recv()
+            return own[g][way, t % 2].astype(F32) + near[g][at(g, slot), half(g, way)].astype(F32)
+
+        def forward(g, t):
+            for way in range(2):
+                slot = t if way == 0 else n - t
+                value = both(g, way, t, slot)
+                if t == 1:
+                    near[g][at(g, slot), half(g, way)] = value.astype(kinds[g])
+                else:
+                    step(g, way, t - 1).wait_recv()
+                    land[g][way, t - 2] = (value + land[g][way, t - 2].astype(F32)).astype(kinds[g])
+                step(g, way, t).start()
+                own_load(g, way, t + 1).start()
+
+        def finish(g):
+            for way in range(2):
+                value = both(g, way, n, 0)
+                step(g, way, n - 1).wait_recv()
+                done[g][0, :, half(g, way)] = (value + land[g][way, n - 2].astype(F32)).astype(kinds[g])
+            if bits:
+                face(g, 0).start()
+
+        rest = list(range(1, count))
+        for g in range(count):
+            for way in range(2):
+                own_load(g, way, 1).start()
+        for t in range(1, n + 1):
+            for g in rest + [0]:
+                swap(g, 0, t % n).start()
+                swap(g, 1, n - t).start()
         spread.start(0)
         for t in range(1, n):
-            for g in range(count):
-                for way in range(2):
-                    slot = t if way == 0 else n - t
-                    swap(g, way, slot).wait_recv()
-                    cols = half(g, way)
-                    value = full[g][source_at(g, slot), half_of(g, way, core)].astype(F32)
-                    value = value + near[g][at(g, slot), cols].astype(F32)
-                    if t == 1:
-                        near[g][at(g, slot), cols] = value.astype(kinds[g])
-                    else:
-                        step(g, way, t - 1).wait_recv()
-                        land[g][way, t - 2] = (value + land[g][way, t - 2].astype(F32)).astype(kinds[g])
-                    step(g, way, t).start()
-            if t == n - 2:
-                spread.arrive(0)
-                spread.start(1)
-        for g in range(count):
-            for way in range(2):
-                swap(g, way, 0).wait_recv()
-                step(g, way, n - 1).wait_recv()
-                cols = half(g, way)
-                value = full[g][source_at(g, 0), half_of(g, way, core)].astype(F32)
-                value = value + near[g][at(g, 0), cols].astype(F32)
-                done[g][0, :, cols] = (value + land[g][way, n - 2].astype(F32)).astype(kinds[g])
-            if bits:
-                face(g, 0).start()
+            for g in rest:
+                forward(g, t)
+            if t >= 2:
+                forward(0, t - 1)
+        spread.arrive(0)
+        spread.start(1)
+        for g in rest:
+            finish(g)
+        forward(0, n - 1)
+        finish(0)
         for k in range(len(bits)):
             for g in range(count):
                 face(g, k).wait_recv()
@@ -1690,7 +1678,7 @@
     groups = list(zip(rows, widths, kinds))
     out = pl.pallas_call(
         kernel,
-        in_specs=[WHOLE] * count + [ANY] * len(sums),
+        in_specs=[ANY] * (count + len(sums)),
         out_specs=[WHOLE] * count + [ANY] * (len(sums) * others),
         out_shape=[jax.ShapeDtypeStruct((r, 2 * w), F32) for r, w, _ in groups]
         + [jax.ShapeDtypeStruct(a.shape, BF) for a in sums for _ in range(others)],
@@ -1699,7 +1687,9 @@
         + [pltpu.VMEM((len(bits) + 1, r, w), kind) for r, w, kind in groups]
         + [pltpu.VMEM((max(1, len(bits)), r, w), kind) for r, w, kind in groups]
         + [pltpu.VMEM((r, w), kind) for r, w, kind in groups]
+        + [pltpu.VMEM((2, 2, r, w // 2), kind) for r, w, kind in groups]
         + [
+            dma((count, 2, 2)),
             dma((count, 2, n)),
             dma((count, 2, n)),
             dma((count, 2, n)),

time: 959 us -> 918 us (0.957)
  local copies, waits for them, and re-layouts: 53.2 us -> 22.1 us
    unnamed x124 -> x46, local copies, waits for them, and re-layouts: 44 us -> 12.4 us
    pallas_call x1, Pallas kernels: 160 us -> 148 us  [attend_backward(): pl.pallas_call(kernel, grid=(pairs,), in_specs=[pl.BlockSpec(memory_space...]
    pallas_call x2, Pallas kernels: 263 us -> 275 us  [feed_forward(): pl.pallas_call(kernel, in_specs=[ANY] * len(operands), out_specs=[ANY] *...]
    pallas_call x1, Pallas kernels: 147 us -> 135 us  [closing(): pl.pallas_call(kernel, in_specs=[ANY] * (count + len(sums)), out_specs=[W...]
  transfers between devices with their start and end apart: 3 -> 3, of which waited for: 0 -> 0; matrix products, arithmetic and copies ran while one was open for 4% -> 4% of each run, Pallas kernels for 34% -> 33%
where the time goes in v2:
time: 918 us; the launch traced here: 908 us
  Pallas kernels  834 us (91%)
  other arithmetic  24.4 us (3%)
  local copies, waits for them, and re-layouts  22.1 us (2%)
  matrix products  17.7 us (2%)
    pallas_call x2, Pallas kernels, feed_forward(): pl.pallas_call(kernel, in_specs=[ANY] * len(operands), out_specs=[ANY] *...  275 us
    pallas_call x1, Pallas kernels, attend_backward(): pl.pallas_call(kernel, grid=(pairs,), in_specs=[pl.BlockSpec(memory_space...  148 us
    pallas_call x1, Pallas kernels, attend_forward(): pl.pallas_call(kernel, grid=(pairs,), in_specs=[pl.BlockSpec(memory_space...  139 us
    pallas_call x1, Pallas kernels, closing(): pl.pallas_call(kernel, in_specs=[ANY] * (count + len(sums)), out_specs=[W...  135 us
    pallas_call x1, Pallas kernels, opening(): pl.pallas_call(kernel, in_specs=[WHOLE, ANY, ANY, ANY, WHOLE, WHOLE, WHOL...  116 us
  transfers between devices with their start and end apart: 3, of which 0 were waited for; matrix products, arithmetic and copies ran while one was open for 4% of the time, Pallas kernels for 33%

profile of v2, /device:TPU:1, one launch (start us, length us, event | category | flops | bytes accessed | tf_op | source)
XLA Modules:
  0.0 907.6 jit_solution(1382897498393797966)
XLA Ops:
  2.0 1.3 constant_dynamic-slice_fusion
  9.6 1.6 copy-done.2
  11.2 1.3 shard_map.216.refs_1_.refs_4_
  14.5 1.5 pad_maximum_fusion.2
  16.1 115.6 %shard_map.215 = (bf16[512,3072]{1,0:T(8,128)(2,1)}, bf16[512,1024]{1,0:T(8,128)(2,1)}, bf16[512,2048]{1,0:T(8,128)(2,1)}, bf16[2048,3072]{1,0:T(8,128)(2,1)}, b...) custom-call(bf16[512,2048]{1,0:T(8,128)(2,1)} %bitcast.55, bf16[256,3072]{1,0:T(8,128)(2,1)} %wq_ref.1, ...), custom_call_target="tpu_custom_call" | custom-call | flops 6442450944 | bytes 25165824 | tf_op jit(solution)/shard_map/pallas_call | solution.py:1470
  131.6 139.5 %shard_map.217 = (f32[16,8,512]{2,1,0:T(8,128)}, bf16[2048,512]{1,0:T(8,128)(2,1)}, f32[512,2048]{1,0:T(8,128)}, bf16[512,2048]{1,0:T(8,128)(2,1)}, bf16[512,204...) custom-call(s32[1]{0:T(128)} %bitcast.seen_ref, ...), custom_call_target="tpu_custom_call" | custom-call | flops 8589934592 | bytes 31457280 | tf_op jit(solution)/shard_map/pallas_call | solution.py:942
  271.1 123.7 %shard_map.218 = (bf16[512,2048]{1,0:T(8,128)(2,1)}, bf16[512,2048]{1,0:T(8,128)(2,1)}, bf16[512,2048]{1,0:T(8,128)(2,1)}, bf16[512,2048]{1,0:T(8,128)(2,1)}, bf...) custom-call(bf16[512,2048]{1,0:T(8,128)(2,1)} %get-tuple-element.75., ...), custom_call_target="tpu_custom_call" | custom-call | flops 77309411328 | bytes 41943040 | tf_op jit(solution)/shard_map/pallas_call | solution.py:810
  394.8 151.2 %shard_map.219 = (bf16[512,2048]{1,0:T(8,128)(2,1)}, bf16[512,2048]{1,0:T(8,128)(2,1)}, bf16[512,2048]{1,0:T(8,128)(2,1)}, bf16[512,2048]{1,0:T(8,128)(2,1)}, bf...) custom-call(bf16[512,2048]{1,0:T(8,128)(2,1)} %get-tuple-element.75., ...), custom_call_target="tpu_custom_call" | custom-call | flops 77309411328 | bytes 41943040 | tf_op jit(solution)/shard_map/pallas_call | solution.py:810
  546.0 6.1 collective-permute-start.1
  554.8 2.7 multiply_reduce_fusion.2
  558.4 2.0 shard_map.221
  563.5 1.3 fusion.16.refs_1_
  564.8 1.3 slice-done.1
  566.2 5.7 convolution_convert_fusion.d_ref
  572.5 147.9 %shard_map.222 = (bf16[512,3072]{1,0:T(8,128)(2,1)}, bf16[2048,2048]{1,0:T(8,128)(2,1)}, bf16[2048,3072]{1,0:T(8,128)(2,1)}, bf16[256,1536]{1,0:T(8,128)(2,1)}, ...) custom-call(s32[1]{0:T(128)} %bitcast.seen_ref, ...), custom_call_target="tpu_custom_call" | custom-call | flops 21474836480 | bytes 31457280 | tf_op jit(solution)/shard_map/pallas_call | solution.py:1157
  720.5 4.0 add_convert_fusion.1
  724.4 12.0 %fusion.8 = (f32[2048]{0:T(1024)S(1)}, f32[512]{0:T(512)S(1)}, f32[512,2048]{1,0:T(8,128)}) fusion(f32[512]{0:T(512)S(1)} %add_rsqrt_fusion, bf16[1,512,2048]{2,1,0:T(8,128)(2,1)S(1)} %copy-done.8, f32[2048]{0:T(1024)S(1)} %bitcast.62, bf16[512,3072]{1,0:T(8,128)(2,1)S(1)} %copy-done.18, bf16[2048,3072]{1,0:T(8,128)(2,1)} %get-tuple-element.110), kind=kOutput, calls=%fused_computation.14 | convolution fusion | flops 6449788416 | bytes 22040576 | tf_op jit(solution)/shard_map/dot_general | solution.py:26
  737.7 135.5 %shard_map.223 = (f32[256,3072]{1,0:T(8,128)}, f32[256,2048]{1,0:T(8,128)}, f32[8,512]{1,0:T(8,128)}, bf16[256,1536]{1,0:T(8,128)(2,1)}, bf16[256,1536]{1,0:T(8,...) custom-call(bf16[2048,3072]{1,0:T(8,128)(2,1)} %get-tuple-element.11, ...), custom_call_target="tpu_custom_call" | custom-call | bytes 63111168 | tf_op jit(solution)/shard_map/pallas_call | solution.py:1679
  873.8 15.7 %shard_map.224 = (f32[256,16384]{1,0:T(8,128)}, f32[256,8192]{1,0:T(8,128)}) custom-call(s32[16]{0:T(128)} %stack.68.refs_0_, bf16[256,1536]{1,0:T(8,128)(2,1)} %get-tuple-element.107.refs_5_.refs_1_, bf16[256,1536]{1,0:T(8,128)(2,1)} %get-tuple-element.118.refs_2_, bf16[256,1536]{1,0:T(8,128)(2,1)} %get-tuple-element.119.refs_3_, ...), custom_call_target="tpu_custom_call" | custom-call | bytes 37748736 | tf_op jit(solution)/shard_map/pallas_call | solution.py:188
  890.9 4.2 convert_add_fusion.1.source
  895.1 1.6 shard_map.220
  898.6 4.7 fusion.7
  903.3 1.7 copy.32
  906.1 1.3 copy.33
  (84 shorter events, 20.9 us)
Async XLA Ops:
  9.6 1.6 copy-start.2
  12.5 1.3 copy-start.4
  394.8 157.5 %copy-start.7 = (bf16[1,512,2048]{2,1,0:T(8,128)(2,1)S(1)}, bf16[1,512,2048]{2,1,0:T(8,128)(2,1)}, u32[]{:S(2)}) copy-start(bf16[1,512,2048]{2,1,0:T(8,128)(2,1)} %param.16) | copy-start | bytes 6291460
  394.8 158.7 %copy-start.17 = (s32[8]{0:T(128)S(1)}, s32[8]{0:T(128)}, u32[]{:S(2)}) copy-start(s32[8]{0:T(128)} %constant.106) | copy-start | bytes 100
  546.0 11.5 %copy-start.15 = (bf16[512,2048]{1,0:T(8,128)(2,1)S(1)}, bf16[512,2048]{1,0:T(8,128)(2,1)}, u32[]{:S(2)}) copy-start(bf16[512,2048]{1,0:T(8,128)(2,1)} %get-tuple-element.100) | copy-start | bytes 6291460
  546.0 174.4 %collective-permute-start.1 = (bf16[512,2048]{1,0:T(8,128)(2,1)}, bf16[512,2048]{1,0:T(8,128)(2,1)}, u32[]{:S(2)}, u32[]{:S(2)}) collective-permute-start(bf16[512,2048]{1,0:T(8,128)(2,1)} %get-tuple-element.99), channel_id=1, source_target_pairs={{0,8},{8,0},{16,24},{24,16},{1,9},{9,1},{17,25},{25,17},{2,10},{10... | collective-permute-start | bytes 6291464 | tf_op jit(solution)/shard_map/ppermute | solution.py:1747
  552.1 338.7 %collective-permute-start = (bf16[512,2048]{1,0:T(8,128)(2,1)}, bf16[512,2048]{1,0:T(8,128)(2,1)}, u32[]{:S(2)}, u32[]{:S(2)}) collective-permute-start(bf16[512,2048]{1,0:T(8,128)(2,1)} %get-tuple-element.97), channel_id=1, source_target_pairs={{0,8},{8,0},{16,24},{24,16},{1,9},{9,1},{17,25},{25,17},{2,10},{10... | collective-permute-start | bytes 6291464 | tf_op jit(solution)/shard_map/ppermute | solution.py:1747
  554.8 2.9 copy-start.16
  558.4 2.2 copy-start.5
  560.4 2.1 copy-start
  560.6 2.9 copy-start.3
  560.6 4.3 slice-start
  563.5 2.7 slice-start.1
  566.2 5.7 copy-start.13
  572.5 148.0 %copy-start.12 = (bf16[512,2048]{1,0:T(8,128)(2,1)S(1)}, bf16[512,2048]{1,0:T(8,128)(2,1)}, u32[]{:S(2)}) copy-start(bf16[512,2048]{1,0:T(8,128)(2,1)} %get-tuple-element.98) | copy-start | bytes 6291460
  720.4 4.0 copy-start.8
  720.4 4.0 copy-start.18
  724.4 166.5 %collective-permute-start.2 = (bf16[512,2048]{1,0:T(8,128)(2,1)}, bf16[512,2048]{1,0:T(8,128)(2,1)}, u32[]{:S(2)}, u32[]{:S(2)}) collective-permute-start(bf16[512,2048]{1,0:T(8,128)(2,1)} %add_convert_fusion.1), channel_id=1, source_target_pairs={{0,16},{8,24},{16,0},{24,8},{1,17},{9,25},{17,1},{25,9},{2,18},{10... | collective-permute-start | bytes 6291464 | tf_op jit(solution)/shard_map/ppermute | solution.py:1747
  890.9 5.9 copy-start.9
  890.9 5.9 copy-start.10
  895.1 2.3 copy-start.1
  895.1 3.5 copy-start.6
  898.6 4.7 copy-start.11
  903.3 2.7 copy-start.14

commit v3 on v2

--- a/solution.py
+++ b/solution.py
@@ -335,12 +335,11 @@
 
 
 class RingReduce:
-    def __init__(self, sizes, parts, out, land, own_v, own_sem, out_sem, send, recv, staged=None):
+    def __init__(self, sizes, parts, out, land, own_v, own_sem, out_sem, send, recv):
         self.n = sizes[1] * sizes[2]
         self.rows, self.wide = out[0].shape
         self.parts, self.out, self.land, self.own_v = parts, out, land, own_v
         self.own_sem, self.out_sem, self.send, self.recv = own_sem, out_sem, send, recv
-        self.staged = staged
         place, device = ring_place(sizes[1])
         self.partners = [device((place + 1) % self.n), device((place + self.n - 1) % self.n)]
 
@@ -371,15 +370,8 @@
     def start(self, way, h):
         return self.ring(self.own_v.at[way, 1, :, self.lanes(h)], way, 1, h)
 
-    def source(self, way, t, h):
-        if self.staged:
-            return self.staged[1].at[way, h]
-        return self.land.at[way, h, t - 2]
-
-    def fetch(self, way, t, h):
-        return pltpu.make_async_copy(
-            self.land.at[way, h, t - 1], self.staged[0].at[way], self.staged[2].at[way]
-        )
+    def forward(self, way, t, h):
+        return self.ring(self.land.at[way, h, t - 2], way, t, h)
 
     def save(self, way):
         return pltpu.make_async_copy(self.own_v.at[way, self.n % 3], self.out[way], self.out_sem.at[way])
@@ -394,15 +386,12 @@
                 self.start(way, h).start()
 
     def total(self, way, t, h):
-        brought = self.staged[0][way] if self.staged else self.land[way, h, t - 2]
-        return self.own_v[way, t % 3, :, self.lanes(h)].astype(F32) + brought.astype(F32)
+        return self.own_v[way, t % 3, :, self.lanes(h)].astype(F32) + self.land[way, h, t - 2].astype(F32)
 
     def step(self, u):
         t, h = u // 2, u % 2
         for way in range(2):
             self.arrived(way, t - 1, h).wait_recv()
-            if self.staged:
-                self.fetch(way, t - 1, h).start()
 
             @pl.when(h == 0)
             def _():
@@ -415,18 +404,8 @@
 
                 self.load_own(way, t + 1).start()
 
-        for way in range(2):
-            if self.staged:
-                self.fetch(way, t - 1, h).wait()
-
-                @pl.when(t >= 3)
-                def _():
-                    self.ring(self.source(way, t - 1, h), way, t - 1, h).wait_send()
-
-                self.staged[1][way, h] = self.total(way, t, h).astype(BF)
-            else:
-                self.land[way, h, t - 2] = self.total(way, t, h).astype(BF)
-            self.ring(self.source(way, t, h), way, t, h).start()
+            self.land[way, h, t - 2] = self.total(way, t, h).astype(BF)
+            self.forward(way, t, h).start()
 
     def last(self):
         n = self.n
@@ -434,29 +413,27 @@
             self.load_own(way, n).wait()
             for h in range(2):
                 self.arrived(way, n - 1, h).wait_recv()
-                if self.staged:
-                    self.fetch(way, n - 1, h).start()
-                    self.fetch(way, n - 1, h).wait()
                 half = self.wide // 2
                 total = self.total(way, n, h).astype(BF)
                 self.own_v[way, n % 3, :, h * half : (h + 1) * half] = total
             self.save(way).start()
         for way in range(2):
             for h in range(2):
-                for t in range(n - 1 if self.staged else 2, n):
-                    self.ring(self.source(way, t, h), way, t, h).wait_send()
+                for t in range(2, n):
+                    self.forward(way, t, h).wait_send()
             self.save(way).wait()
 
 
-def reduce_scratch(n, rows, wide, near):
+def reduce_scratch(n, rows, wide):
     dma = pltpu.SemaphoreType.DMA
-    land = [pltpu.VMEM((2, 2, n - 1, rows, wide // 2), BF)] if near else []
-    stage = [pltpu.VMEM((2, rows, wide // 2), BF), pltpu.VMEM((2, 2, rows, wide // 2), BF), dma((2,))]
-    return (
-        land
-        + [pltpu.VMEM((2, 3, rows, wide), BF), dma((2, 3)), dma((2,)), dma((2, 2, n)), dma((2, 2, n))]
-        + ([] if near else stage)
-    )
+    return [
+        pltpu.VMEM((2, 2, n - 1, rows, wide // 2), BF),
+        pltpu.VMEM((2, 3, rows, wide), BF),
+        dma((2, 3)),
+        dma((2,)),
+        dma((2, 2, n)),
+        dma((2, 2, n)),
+    ]
 
 
 class TeamSpread:
@@ -539,7 +516,6 @@
         part_refs = take(2)
         y_refs, dn_refs, grad_refs, ring_outs = take(team), take(team), take(2), take(2)
         if reducing:
-            (land,) = take(1)
             near = take(max(1, inside))
             (far,) = take(1)
         wgu, wd, xb, dyb, yb, dnb, dgu, inner, xg, dyg, gout = take(11)
@@ -548,7 +524,7 @@
             cb, c_sems = take(2)
         if reducing:
             swap_send, swap_recv, face_send, face_recv = take(4)
-            ring = RingReduce(sizes, part_refs, ring_outs, land, *refs[:5], staged=refs[5:])
+            ring = RingReduce(sizes, part_refs, ring_outs, *refs)
         else:
             ring = RingGather(sizes, own_columns(n_dp, *part_refs, SUBS // 2), ring_outs, *refs)
         me = lax.axis_index("dp")
@@ -594,11 +570,11 @@
                 return []
             rows_here = pl.ds((i % per) * tile, tile)
             out = [
-                pltpu.make_async_copy(old_y[m].at[rows_here], cb.at[0], c_sems.at[0]),
-                pltpu.make_async_copy(old_dn[m].at[rows_here], cb.at[1], c_sems.at[1]),
+                pltpu.make_async_copy(old_y[m].at[rows_here], yb, c_sems.at[0]),
+                pltpu.make_async_copy(old_dn[m].at[rows_here], dnb, c_sems.at[1]),
             ]
             if m < inside:
-                out.append(pltpu.make_async_copy(near[m].at[rows_here], cb.at[2], c_sems.at[2]))
+                out.append(pltpu.make_async_copy(near[m].at[rows_here], cb, c_sems.at[2]))
             return out
 
         def writes(m, i):
@@ -677,10 +653,17 @@
                 def _():
                     on_block(i, lambda m: swap(m + inside).wait_recv() if m < inside else None)
 
-            on_block(i, lambda m: go(more(m, i)))
             ticks(2 * i, 2 * i + 2)
             end(loads(0, i))
             here = pl.ds(pl.multiple_of(i * tile, tile), tile)
+            if carried:
+                drained = (i > 0) & (i % per != 0) if reducing else i > 0
+
+                @pl.when(drained)
+                def _():
+                    end(writes(0, i))
+
+                on_block(i, lambda m: go(more(m, i)))
             for b in range(2):
                 gate_up = dot_nn(xb[i % 2], wgu[:, b * 2 * sub : (b + 1) * 2 * sub])
                 d_inner = dot_nn(dyb[i % 2], wd[:, b * sub : (b + 1) * sub])
@@ -692,25 +675,25 @@
                     d_inner * up * (sig + act * (1.0 - sig))
                 ).astype(BF)
                 dgu[here, b * 2 * sub + sub : (b + 1) * 2 * sub] = (d_inner * act).astype(BF)
-            drained = (i > 0) & (i % per != 0) if reducing else i > 0
-
-            @pl.when(drained)
-            def _():
-                end(writes(0, i))
-
-            if carried:
+            if not carried:
+
+                @pl.when(i > 0)
+                def _():
+                    end(writes(0, i))
+
+            else:
                 on_block(i, lambda m: end(more(m, i)))
             for at in range(0, width, half):
                 lanes = slice(at, at + half)
                 y = dot_nt(inner[here, :], wd[lanes, :])
                 if carried:
-                    y = y + cb[0, :, lanes].astype(F32)
+                    y = y + yb[:, lanes].astype(F32)
                 yb[:, lanes] = y.astype(BF)
                 dn = dot_nt(dgu[here, :], wgu[lanes, :])
                 if carried:
-                    dn = dn + cb[1, :, lanes].astype(F32)
+                    dn = dn + dnb[:, lanes].astype(F32)
                 if inside:
-                    dn = dn + jnp.where(block_of(i) < inside, cb[2, :, lanes].astype(F32), 0.0)
+                    dn = dn + jnp.where(block_of(i) < inside, cb[:, lanes].astype(F32), 0.0)
                 dnb[:, lanes] = dn.astype(BF)
             on_block(i, lambda m: go(writes(m, i)))
             if reducing and team > 1:
@@ -776,7 +759,7 @@
     shape = lambda a, b: jax.ShapeDtypeStruct((a, b), BF)
     outs = [shape(span, width)] * (2 * team) + [shape(width, wide)] * 2
     if reducing:
-        outs += [shape(rows, wide)] * 2 + [jax.ShapeDtypeStruct((2, 2, n - 1, rows, wide // 2), BF)]
+        outs += [shape(rows, wide)] * 2
         outs += [shape(span, width)] * (max(1, inside) + 1)
     else:
         outs += [shape(width, wide)] * 2
@@ -800,10 +783,10 @@
         dma((2,)),
     ]
     if carried:
-        scratch += [pltpu.VMEM((3 if inside else 2, tile, width), BF), dma((3,))]
+        scratch += [pltpu.VMEM((tile, width) if inside else (16, 128), BF), dma((3,))]
     if reducing:
         scratch += [dma((max(1, inside),)), dma((max(1, inside),)), dma(()), dma(())]
-        scratch += reduce_scratch(n, rows, wide, False)
+        scratch += reduce_scratch(n, rows, wide)
     else:
         scratch += gather_scratch(n, rows, wide)
     operands = list(xs) + list(dys) + pieces + carried + list(ring_parts)
@@ -814,7 +797,7 @@
         out_shape=outs,
         scratch_shapes=scratch,
         compiler_params=pltpu.CompilerParams(
-            collective_id=ident, has_side_effects=True, vmem_limit_bytes=56 * MIB
+            collective_id=ident, has_side_effects=True, vmem_limit_bytes=60 * MIB
         ),
         cost_estimate=cost(18 * team * span * width * 2 * sub, 40 * MIB),
     )(*operands)
@@ -1195,7 +1178,7 @@
             dma((2,)),
         ]
         + spread_scratch(2, n_dp)
-        + reduce_scratch(n, rows, wide, True),
+        + reduce_scratch(n, rows, wide),
         compiler_params=pltpu.CompilerParams(
             collective_id=ident, has_side_effects=True, vmem_limit_bytes=58 * MIB
         ),
@@ -1204,7 +1187,7 @@
     return out[0], out[1], out[2], out[3:5], [out[5 + k * others : 5 + (k + 1) * others] for k in range(2)]
 
 
-def opening(sizes, x, w_qkv, w_out, gains, tables):
+def opening(sizes, x, dy, w_qkv, w_out, gains, tables):
     n_dp, n_fsdp, n_ctx = sizes
     n = n_fsdp * n_ctx
     span, width = x.shape
@@ -1215,7 +1198,7 @@
     chunk = share // 2 if share % 256 == 0 else share
     across_x = n_dp > 2
 
-    def kernel(x_ref, wq_ref, wo_ref, g_ref, cos_ref, low_ref, high_ref, *refs):
+    def kernel(x_ref, dy_ref, wq_ref, wo_ref, g_ref, cos_ref, low_ref, high_ref, *refs):
         refs = list(refs)
 
         def take(count):
@@ -1223,8 +1206,8 @@
             del refs[:count]
             return out
 
-        qkv_out, far_out, xs_out, wq_out, wo_out, gains_out = take(6)
-        qkv_v, far_v, xs_v = take(3)
+        qkv_out, far_out, xs_out, wq_out, wo_out, gains_out, dy_out = take(7)
+        qkv_v, far_v, xs_v, dy_v = take(4)
         wq_v = take(n_dp)
         om_v, oo_v, gains_v = take(3)
         load_sems, save_sems, wq_sems, wo_sems = take(4)
@@ -1324,6 +1307,7 @@
             xs_v[:, slot * rows : (slot + 1) * rows] = (
                 part * scale * gains_v[slot, 0:1, :].astype(F32)
             ).astype(BF)
+            dy_v[:, slot * rows : (slot + 1) * rows] = slot_lanes(dy_ref, block_of(slot), rows).astype(BF)
 
         loads[0].wait()
         loads[2].wait()
@@ -1430,9 +1414,11 @@
             kv_step(j).start()
         saves = [
             pltpu.make_async_copy(a, b, save_sems.at[k])
-            for k, (a, b) in enumerate([(qkv_v, qkv_out), (far_v, far_out), (xs_v, xs_out), (gains_v, gains_out)])
+            for k, (a, b) in enumerate(
+                [(qkv_v, qkv_out), (far_v, far_out), (xs_v, xs_out), (gains_v, gains_out), (dy_v, dy_out)]
+            )
         ]
-        for k in (0, 2, 3):
+        for k in (0, 2, 3, 4):
             saves[k].start()
         go(save_half(0))
         for way, slot in order:
@@ -1466,19 +1452,20 @@
         (width, qkvwidth),
         (width, 2 * half),
         (n, 16, rows),
+        (span, width),
     ]
     return pl.pallas_call(
         kernel,
-        in_specs=[WHOLE, ANY, ANY, ANY, WHOLE, WHOLE, WHOLE],
-        out_specs=[ANY] * 6,
+        in_specs=[WHOLE, WHOLE, ANY, ANY, ANY, WHOLE, WHOLE, WHOLE],
+        out_specs=[ANY] * 7,
         out_shape=[jax.ShapeDtypeStruct(shape, BF) for shape in shapes],
-        scratch_shapes=[pltpu.VMEM(shape, BF) for shape in shapes[:3]]
+        scratch_shapes=[pltpu.VMEM(shape, BF) for shape in shapes[:3] + shapes[6:]]
         + [pltpu.VMEM((width, share), BF)] * n_dp
         + [pltpu.VMEM((width, half), BF)] * 2
         + [pltpu.VMEM((n, 16, rows), BF)]
         + [
             dma((3,)),
-            dma((4,)),
+            dma((5,)),
             dma((n_dp, n)),
             dma((2, n)),
             dma((2, 2, n)),
@@ -1498,16 +1485,20 @@
             collective_id=0, has_side_effects=True, vmem_limit_bytes=56 * MIB
         ),
         cost_estimate=cost(2 * span * width * qkvwidth, 4 * width * qkvwidth),
-    )(x, w_qkv, w_out, gains, *tables)
-
-
-def closing(sizes, fulls, slotted, sums):
+    )(x, dy, w_qkv, w_out, gains, *tables)
+
+
+def closing(sizes, fulls, slotted, sums, d_qkv, w_qkv, x, gain, d_gain):
     n_dp, n_fsdp, n_ctx = sizes
     n = n_fsdp * n_ctx
-    rows = [f.shape[0] // n for f in fulls]
-    widths = [f.shape[1] // 2 for f in fulls]
-    kinds = [f.dtype for f in fulls]
-    count = len(fulls)
+    span, width = x.shape
+    mine = width // n
+    rows = [f.shape[0] // n for f in fulls] + [8]
+    widths = [f.shape[1] // 2 for f in fulls] + [max(mine, 256)]
+    kinds = [f.dtype for f in fulls] + [F32]
+    count = len(fulls) + 1
+    chunk = min(512, width)
+    parts = width // chunk
     bits = [1 << k for k in range(1, n_dp.bit_length() - 1)]
     others = n_dp - 1
 
@@ -1519,8 +1510,11 @@
             del refs[:size]
             return out
 
-        full, own_sums = take(count), take(len(sums))
-        outs, blocks_out = take(count), take(len(sums) * others)
+        full, own_sums = take(count - 1), take(len(sums))
+        dq_ref, w_ref, x_ref, gain_ref, d_gain_ref = take(5)
+        outs, blocks_out, (input_out,) = take(count), take(len(sums) * others), take(1)
+        gain_v, both_v, d_v, w_v, dn_v, w_sem, d_sem, dn_sem = take(8)
+        full = full + [gain_v]
         near, land, done, extra, back = take(count), take(count), take(count), take(count), take(count)
         own = take(count)
         (own_sems,) = take(1)
@@ -1628,26 +1622,82 @@
             if bits:
                 face(g, 0).start()
 
-        rest = list(range(1, count))
-        for g in range(count):
+        w_load = pltpu.make_async_copy(w_ref, w_v, w_sem)
+        d_load = pltpu.make_async_copy(dq_ref, d_v, d_sem)
+        dn_save = pltpu.make_async_copy(dn_v, input_out, dn_sem)
+
+        def begin(g):
             for way in range(2):
                 own_load(g, way, 1).start()
+
+        def swaps(g, t):
+            swap(g, 0, t % n).start()
+            swap(g, 1, n - t).start()
+
+        def product(k):
+            lanes = slice(k * chunk, (k + 1) * chunk)
+            dn_v[:, lanes] = dot_nt(d_v[...], w_v[lanes, :])
+
+        def norm():
+            square = jnp.zeros((span, 1), F32)
+            for k in range(parts):
+                value = x_ref[:, k * chunk : (k + 1) * chunk].astype(F32)
+                square = square + jnp.sum(value * value, -1, keepdims=True)
+            scale = lax.rsqrt(square / width + EPS)
+            inner = jnp.zeros((span, 1), F32)
+            for k in range(parts):
+                lanes = slice(k * chunk, (k + 1) * chunk)
+                unit = x_ref[:, lanes].astype(F32) * scale
+                product = dn_v[:, lanes] * unit
+                both_v[1:2, lanes] = jnp.sum(product, 0, keepdims=True)
+                inner = inner + jnp.sum(product * gain_ref[0:1, lanes], -1, keepdims=True)
+            inner = inner / width
+            for k in range(parts):
+                lanes = slice(k * chunk, (k + 1) * chunk)
+                unit = x_ref[:, lanes].astype(F32) * scale
+                dn_v[:, lanes] = scale * (dn_v[:, lanes] * gain_ref[0:1, lanes] - unit * inner)
+            dn_save.start()
+            gain_v[...] = jnp.zeros_like(gain_v)
+            both_v[0:1, :] = d_gain_ref[0:1, :]
+            both_v[2:8, :] = jnp.zeros((6, width), F32)
+            for slot in range(n):
+                there = device((place + n - slot) % n)
+                pair = slot_lanes(both_v, there["fsdp"] * n_ctx + there["ctx"], mine)
+                gain_v[slot * 8 : slot * 8 + 1, :mine] = pair[1:2]
+                gain_v[slot * 8 : slot * 8 + 1, widths[-1] : widths[-1] + mine] = pair[0:1]
+
+        rest, gains = list(range(1, count - 1)), count - 1
+        d_load.start()
+        w_load.start()
+        for g in range(count - 1):
+            begin(g)
         for t in range(1, n + 1):
             for g in rest + [0]:
-                swap(g, 0, t % n).start()
-                swap(g, 1, n - t).start()
+                swaps(g, t)
         spread.start(0)
+        jobs = [(lambda k=k: product(k)) for k in range(parts)] + [norm]
         for t in range(1, n):
             for g in rest:
                 forward(g, t)
             if t >= 2:
                 forward(0, t - 1)
+            if t == 1:
+                d_load.wait()
+                w_load.wait()
+            for k in range((t - 1) * len(jobs) // (n - 1), t * len(jobs) // (n - 1)):
+                jobs[k]()
+        begin(gains)
+        for t in range(1, n + 1):
+            swaps(gains, t)
+        for g in rest:
+            finish(g)
         spread.arrive(0)
         spread.start(1)
-        for g in rest:
-            finish(g)
         forward(0, n - 1)
+        for t in range(1, n):
+            forward(gains, t)
         finish(0)
+        finish(gains)
         for k in range(len(bits)):
             for g in range(count):
                 face(g, k).wait_recv()
@@ -1664,6 +1714,7 @@
             outs[g][:, here] = back[g][...].astype(F32)
         spread.arrive(1)
         spread.last()
+        dn_save.wait()
         for g in range(count):
             end(g).wait_send()
             for k in range(len(bits)):
@@ -1678,11 +1729,22 @@
     groups = list(zip(rows, widths, kinds))
     out = pl.pallas_call(
         kernel,
-        in_specs=[ANY] * (count + len(sums)),
-        out_specs=[WHOLE] * count + [ANY] * (len(sums) * others),
+        in_specs=[ANY] * (count - 1 + len(sums) + 2) + [WHOLE] * 3,
+        out_specs=[WHOLE] * count + [ANY] * (len(sums) * others + 1),
         out_shape=[jax.ShapeDtypeStruct((r, 2 * w), F32) for r, w, _ in groups]
-        + [jax.ShapeDtypeStruct(a.shape, BF) for a in sums for _ in range(others)],
-        scratch_shapes=[pltpu.VMEM((n * r, w), kind) for r, w, kind in groups]
+        + [jax.ShapeDtypeStruct(a.shape, BF) for a in sums for _ in range(others)]
+        + [jax.ShapeDtypeStruct((span, width), F32)],
+        scratch_shapes=[
+            pltpu.VMEM((n * 8, 2 * widths[-1]), F32),
+            pltpu.VMEM((8, width), F32),
+            pltpu.VMEM(d_qkv.shape, BF),
+            pltpu.VMEM(w_qkv.shape, BF),
+            pltpu.VMEM((span, width), F32),
+            dma(()),
+            dma(()),
+            dma(()),
+        ]
+        + [pltpu.VMEM((n * r, w), kind) for r, w, kind in groups]
         + [pltpu.VMEM((2, n - 1, r, w // 2), kind) for r, w, kind in groups]
         + [pltpu.VMEM((len(bits) + 1, r, w), kind) for r, w, kind in groups]
         + [pltpu.VMEM((max(1, len(bits)), r, w), kind) for r, w, kind in groups]
@@ -1701,11 +1763,12 @@
         ]
         + spread_scratch(len(sums), n_dp),
         compiler_params=pltpu.CompilerParams(
-            collective_id=1, has_side_effects=True, vmem_limit_bytes=60 * MIB
+            collective_id=1, has_side_effects=True, vmem_limit_bytes=58 * MIB
         ),
         cost_estimate=cost(0, sum(12 * n * r * w for r, w, _ in groups)),
-    )(*fulls, *sums)
-    return out[:count], [out[count + k * others : count + (k + 1) * others] for k in range(len(sums))]
+    )(*fulls, *sums, d_qkv, w_qkv, x, gain, d_gain)
+    blocks = [out[count + k * others : count + (k + 1) * others] for k in range(len(sums))]
+    return out[:count], blocks, out[-1]
 
 
 class Ring:
@@ -1777,9 +1840,10 @@
     ffq = ffwidth // n_dp
     sub = ffq // SUBS
     grad_y = cotangent.reshape(span, width)
-    dy = ring.to_slots(grad_y)
     gains = jnp.concatenate([attn_gain[None], ffn_gain[None], jnp.zeros((14, rows), BF)], 0)
-    qkv, kv_far, normed_one, wqkv, wout, gains = opening(sizes, tokens, w_qkv, w_out, gains, tables)
+    qkv, kv_far, normed_one, wqkv, wout, gains, dy = opening(
+        sizes, tokens, grad_y, w_qkv, w_out, gains, tables
+    )
     attn_t, lse, hidden_one, normed_two, x_others, dy_others, weights_a = attend_forward(
         sizes, tokens, qkv, kv_far, seen, wout, gains, dy, w_gate_up, w_down
     )
@@ -1788,8 +1852,6 @@
     gains = gains[:, :2][(ring.rank - jnp.array(ring.place, jnp.int32)) % n]
     gain_one = gains[:, 0].reshape(-1).astype(F32)
     gain_two = gains[:, 1].reshape(-1).astype(F32)
-    inputs = tokens.astype(F32)
-    scale_one = inv_rms(inputs)
     scale_two = inv_rms(hidden_one)
 
     y, dn, grads_a, weights_b = feed_forward(
@@ -1808,20 +1870,19 @@
     d_qkv, part_out, part_qkv, sums_b, others_a = attend_backward(
         sizes, qkv, kv_far, d_attn, lse, seen, tables, attn_t, d_proj, normed_one, grads_b, sums_a, 4
     )
-    d_normed_one = matmul_rows(d_qkv, wqkv)
-    d_input_norm, d_gain_one = norm_back(inputs, scale_one, gain_one, d_normed_one)
+    room = max(rows, 256)
+    (grad_qkv, grad_out, grad_gain), others_b, d_input_norm = closing(
+        sizes,
+        (part_qkv, part_out),
+        (True, False, True),
+        sums_b,
+        d_qkv,
+        wqkv,
+        tokens,
+        jnp.broadcast_to(gain_one[None], (8, width)),
+        jnp.broadcast_to(d_gain_two[None], (8, width)),
+    )
     grad_input = d_hidden + d_input_norm
-
-    room = max(rows, 256)
-
-    def by_slot(gain):
-        blocks = gain.reshape(n, 1, rows)[ring.slot_blocks()]
-        return jnp.pad(blocks, ((0, 0), (0, 7), (0, room - rows))).reshape(n * 8, room)
-
-    part_gain = jnp.concatenate([by_slot(d_gain_one), by_slot(d_gain_two)], 1)
-    (grad_qkv, grad_out, grad_gain), others_b = closing(
-        sizes, (part_qkv, part_out, part_gain), (True, False, True), sums_b
-    )
 
     placed, columns = [], []
     for q in range(SUBS):

time: 918 us -> 902 us (0.983)
  matrix products: 17.7 us -> 5.71 us
    pallas_call x2, Pallas kernels: 275 us -> 257 us  [feed_forward(): pl.pallas_call(kernel, in_specs=[ANY] * len(operands), out_specs=[ANY] *...]
    dot_general x2 -> x1, matrix products: 17.7 us -> 5.71 us  [matmul_rows(): lax.dot_general(left, right, (((1,), (1,)), ((), ())), preferred_element_...]
    pallas_call x1, Pallas kernels: 148 us -> 160 us  [attend_backward(): pl.pallas_call(kernel, grid=(pairs,), in_specs=[pl.BlockSpec(memory_space...]
    pallas_call x2, Pallas kernels: 251 us -> 262 us  [the longest x1 146 us: closing(): pl.pallas_call(kernel, in_specs=[ANY] * (count - 1 + len(sums) + 2) + [WH...]
  transfers between devices with their start and end apart: 3 -> 3, of which waited for: 0 -> 0; matrix products, arithmetic and copies ran while one was open for 4% -> 3% of each run, Pallas kernels for 33% -> 36%
where the time goes in v3:
time: 902 us; the launch traced here: 892 us
  Pallas kernels  837 us (93%)
  other arithmetic  23.6 us (3%)
  local copies, waits for them, and re-layouts  17.3 us (2%)
    pallas_call x2, Pallas kernels, feed_forward(): pl.pallas_call(kernel, in_specs=[ANY] * len(operands), out_specs=[ANY] *...  257 us
    pallas_call x1, Pallas kernels, attend_backward(): pl.pallas_call(kernel, grid=(pairs,), in_specs=[pl.BlockSpec(memory_space...  160 us
    pallas_call x1, Pallas kernels, closing(): pl.pallas_call(kernel, in_specs=[ANY] * (count - 1 + len(sums) + 2) + [WH...  146 us
    pallas_call x1, Pallas kernels, attend_forward(): pl.pallas_call(kernel, grid=(pairs,), in_specs=[pl.BlockSpec(memory_space...  139 us
    pallas_call x1, Pallas kernels, opening(): pl.pallas_call(kernel, in_specs=[WHOLE, WHOLE, ANY, ANY, ANY, WHOLE, WHOL...  117 us
  transfers between devices with their start and end apart: 3, of which 0 were waited for; matrix products, arithmetic and copies ran while one was open for 3% of the time, Pallas kernels for 36%

profile of v3, /device:TPU:1, one launch (start us, length us, event | category | flops | bytes accessed | tf_op | source)
XLA Modules:
  0.0 892.3 jit_solution(592262828643216941)
XLA Ops:
  0.7 1.3 constant_dynamic-slice_fusion
  7.1 1.5 pad_maximum_fusion.2
  8.6 116.7 %shard_map.188 = (bf16[512,3072]{1,0:T(8,128)(2,1)}, bf16[512,1024]{1,0:T(8,128)(2,1)}, bf16[512,2048]{1,0:T(8,128)(2,1)}, bf16[2048,3072]{1,0:T(8,128)(2,1)}, b...) custom-call(bf16[512,2048]{1,0:T(8,128)(2,1)} %bitcast.38, ...), custom_call_target="tpu_custom_call" | custom-call | flops 6442450944 | bytes 25165824 | tf_op jit(solution)/shard_map/pallas_call | solution.py:1457
  125.3 139.0 %shard_map.189 = (f32[16,8,512]{2,1,0:T(8,128)}, bf16[2048,512]{1,0:T(8,128)(2,1)}, f32[512,2048]{1,0:T(8,128)}, bf16[512,2048]{1,0:T(8,128)(2,1)}, bf16[512,204...) custom-call(s32[1]{0:T(128)} %bitcast.seen_ref, ...), custom_call_target="tpu_custom_call" | custom-call | flops 8589934592 | bytes 31457280 | tf_op jit(solution)/shard_map/pallas_call | solution.py:925
  264.3 123.9 %shard_map.190 = (bf16[512,2048]{1,0:T(8,128)(2,1)}, bf16[512,2048]{1,0:T(8,128)(2,1)}, bf16[512,2048]{1,0:T(8,128)(2,1)}, bf16[512,2048]{1,0:T(8,128)(2,1)}, bf...) custom-call(bf16[512,2048]{1,0:T(8,128)(2,1)} %get-tuple-element.78., ...), custom_call_target="tpu_custom_call" | custom-call | flops 77309411328 | bytes 41943040 | tf_op jit(solution)/shard_map/pallas_call | solution.py:793
  388.3 132.7 %shard_map.191 = (bf16[512,2048]{1,0:T(8,128)(2,1)}, bf16[512,2048]{1,0:T(8,128)(2,1)}, bf16[512,2048]{1,0:T(8,128)(2,1)}, bf16[512,2048]{1,0:T(8,128)(2,1)}, bf...) custom-call(bf16[512,2048]{1,0:T(8,128)(2,1)} %get-tuple-element.78., ...), custom_call_target="tpu_custom_call" | custom-call | flops 77309411328 | bytes 41943040 | tf_op jit(solution)/shard_map/pallas_call | solution.py:793
  521.0 5.5 collective-permute-start.1
  527.3 2.5 multiply_reduce_fusion.2
  531.8 2.4 convert_add_fusion.source
  534.2 2.0 shard_map.193
  539.3 1.2 fusion.3.refs_1_
  540.6 1.4 slice-done.1
  542.0 5.7 convolution_convert_fusion.d_ref
  547.7 3.7 add_convert_fusion.1
  551.4 159.8 %shard_map.194 = (bf16[512,3072]{1,0:T(8,128)(2,1)}, bf16[2048,2048]{1,0:T(8,128)(2,1)}, bf16[2048,3072]{1,0:T(8,128)(2,1)}, bf16[256,1536]{1,0:T(8,128)(2,1)}, ...) custom-call(s32[1]{0:T(128)} %bitcast.seen_ref, ...), custom_call_target="tpu_custom_call" | custom-call | flops 21474836480 | bytes 31457280 | tf_op jit(solution)/shard_map/pallas_call | solution.py:1140
  712.5 145.6 %shard_map.195 = (f32[256,3072]{1,0:T(8,128)}, f32[256,2048]{1,0:T(8,128)}, f32[8,512]{1,0:T(8,128)}, bf16[256,1536]{1,0:T(8,128)(2,1)}, bf16[256,1536]{1,0:T(8,...) custom-call(bf16[2048,3072]{1,0:T(8,128)(2,1)} %get-tuple-element.11, ...), custom_call_target="tpu_custom_call" | custom-call | bytes 63111168 | tf_op jit(solution)/shard_map/pallas_call | solution.py:1730
  858.6 15.7 %shard_map.196 = (f32[256,16384]{1,0:T(8,128)}, f32[256,8192]{1,0:T(8,128)}) custom-call(s32[16]{0:T(128)} %stack.68.refs_0_, bf16[256,1536]{1,0:T(8,128)(2,1)} %get-tuple-element.110.refs_5_.refs_1_, bf16[256,1536]{1,0:T(8,128)(2,1)} %get-tuple-element.122.refs_2_, bf16[256,1536]{1,0:T(8,128)(2,1)} %get-tuple-element.123.refs_3_, ...), custom_call_target="tpu_custom_call" | custom-call | bytes 37748736 | tf_op jit(solution)/shard_map/pallas_call | solution.py:188
  874.4 1.3 fusion.4
  875.7 4.2 convert_add_fusion.1.source
  879.9 1.6 shard_map.192
  882.1 1.3 copy-done.3
  883.4 4.6 add_bitcast_fusion
  888.0 1.7 copy.23
  890.7 1.3 copy.24
  (55 shorter events, 12.5 us)
Async XLA Ops:
  520.9 8.9 %copy-start.12 = (s32[8]{0:T(128)S(1)}, s32[8]{0:T(128)}, u32[]{:S(2)}) copy-start(s32[8]{0:T(128)} %constant.81.clone) | copy-start | bytes 100
  521.0 9.5 %copy-start.11 = (s32[8]{0:T(128)S(1)}, s32[8]{0:T(128)}, u32[]{:S(2)}) copy-start(s32[8]{0:T(128)} %constant.85) | copy-start | bytes 100
  521.0 10.8 %copy-start.10 = (bf16[512,2048]{1,0:T(8,128)(2,1)S(1)}, bf16[512,2048]{1,0:T(8,128)(2,1)}, u32[]{:S(2)}) copy-start(bf16[512,2048]{1,0:T(8,128)(2,1)} %get-tuple-element.103) | copy-start | bytes 6291460
  521.0 26.7 %collective-permute-start.1 = (bf16[512,2048]{1,0:T(8,128)(2,1)}, bf16[512,2048]{1,0:T(8,128)(2,1)}, u32[]{:S(2)}, u32[]{:S(2)}) collective-permute-start(bf16[512,2048]{1,0:T(8,128)(2,1)} %get-tuple-element.102), channel_id=1, source_target_pairs={{0,8},{8,0},{16,24},{24,16},{1,9},{9,1},{17,25},{25,17},{2,10},{10... | collective-permute-start | bytes 6291464 | tf_op jit(solution)/shard_map/ppermute | solution.py:1810
  526.5 349.2 %collective-permute-start = (bf16[512,2048]{1,0:T(8,128)(2,1)}, bf16[512,2048]{1,0:T(8,128)(2,1)}, u32[]{:S(2)}, u32[]{:S(2)}) collective-permute-start(bf16[512,2048]{1,0:T(8,128)(2,1)} %get-tuple-element.100), channel_id=1, source_target_pairs={{0,8},{8,0},{16,24},{24,16},{1,9},{9,1},{17,25},{25,17},{2,10},{10... | collective-permute-start | bytes 6291464 | tf_op jit(solution)/shard_map/ppermute | solution.py:1810
  534.2 2.2 copy-start.2
  536.2 2.1 copy-start
  536.4 2.9 copy-start.4
  536.4 4.2 slice-start
  539.3 2.7 slice-start.1
  542.0 5.7 copy-start.8
  542.0 5.7 copy-start.7
  551.4 324.3 %collective-permute-start.2 = (bf16[512,2048]{1,0:T(8,128)(2,1)}, bf16[512,2048]{1,0:T(8,128)(2,1)}, u32[]{:S(2)}, u32[]{:S(2)}) collective-permute-start(bf16[512,2048]{1,0:T(8,128)(2,1)} %add_convert_fusion.1), channel_id=1, source_target_pairs={{0,16},{8,24},{16,0},{24,8},{1,17},{9,25},{17,1},{25,9},{2,18},{10... | collective-permute-start | bytes 6291464 | tf_op jit(solution)/shard_map/ppermute | solution.py:1810
  875.7 5.8 copy-start.5
  879.9 2.2 copy-start.1
  879.9 3.5 copy-start.3
  883.4 4.6 copy-start.6
  888.0 2.7 copy-start.9

commit v4 on v3

--- a/solution.py
+++ b/solution.py
@@ -1047,11 +1047,6 @@
             dkv[...] = jnp.zeros_like(dkv)
             dkv_far[...] = jnp.zeros_like(dkv_far)
 
-        @pl.when(group == pairs - 4)
-        def _():
-            spread.arrive(0)
-            spread.start(1)
-
         lax.fori_loop(
             4 + group * (early - 4) // pairs,
             4 + (group + 1) * (early - 4) // pairs,
@@ -1123,6 +1118,8 @@
             save = pltpu.make_async_copy(dqkv_v, dqkv_out, save_sem)
             save.start()
             lax.fori_loop(early + 2, 2 * n - 1, lambda u, c: (ring.step(u), c)[1], 0)
+            spread.arrive(0)
+            spread.start(1)
             product(gq_out, qkvwidth, lambda at: dot_tn(normed_v[:, at], dqkv_v[...]))
             if early + 2 < 2 * n:
                 ring.step(2 * n - 1)
@@ -1488,15 +1485,16 @@
     )(x, dy, w_qkv, w_out, gains, *tables)
 
 
-def closing(sizes, fulls, slotted, sums, d_qkv, w_qkv, x, gain, d_gain):
+def closing(sizes, part_qkv, part_out, sums, d_qkv, w_qkv, x, gain, d_gain):
     n_dp, n_fsdp, n_ctx = sizes
     n = n_fsdp * n_ctx
     span, width = x.shape
     mine = width // n
-    rows = [f.shape[0] // n for f in fulls] + [8]
-    widths = [f.shape[1] // 2 for f in fulls] + [max(mine, 256)]
-    kinds = [f.dtype for f in fulls] + [F32]
-    count = len(fulls) + 1
+    rows, widths, kinds = [mine, 8], [part_qkv.shape[1] // 2, max(mine, 256)], [BF, F32]
+    count = 2
+    outwidth = part_out.shape[1]
+    split = n_dp > 2
+    quarter = outwidth // n_dp
     chunk = min(512, width)
     parts = width // chunk
     bits = [1 << k for k in range(1, n_dp.bit_length() - 1)]
@@ -1510,14 +1508,18 @@
             del refs[:size]
             return out
 
-        full, own_sums = take(count - 1), take(len(sums))
+        full, (out_ref,), own_sums = take(1), take(1), take(len(sums))
         dq_ref, w_ref, x_ref, gain_ref, d_gain_ref = take(5)
-        outs, blocks_out, (input_out,) = take(count), take(len(sums) * others), take(1)
+        outs, (wo_out,) = take(count), take(1)
+        blocks_out, (input_out,) = take(len(sums) * others), take(1)
         gain_v, both_v, d_v, w_v, dn_v, w_sem, d_sem, dn_sem = take(8)
         full = full + [gain_v]
         near, land, done, extra, back = take(count), take(count), take(count), take(count), take(count)
         own = take(count)
         (own_sems,) = take(1)
+        o_own, o_near, o_x, o_land, o_done = take(5)
+        o_blocks = take(others)
+        o_load, o_swap_send, o_swap_recv, o_x_send, o_x_recv, o_send, o_recv, o_end_send, o_end_recv = take(9)
         send, recv, pair_send, pair_recv, x_send, x_recv, end_send, end_recv = take(8)
         spread = TeamSpread(
             n_dp, own_sums, [blocks_out[k * others : (k + 1) * others] for k in range(len(sums))], *refs
@@ -1540,16 +1542,9 @@
         def at(g, slot):
             return pl.ds(slot * rows[g], rows[g])
 
-        def source_at(g, slot):
-            if slotted[g]:
-                return at(g, slot)
-            there = device((place + n - slot) % n)
-            block = there["fsdp"] * n_ctx + there["ctx"]
-            return pl.ds(pl.multiple_of(block * rows[g], rows[g]), rows[g])
-
         def swap(g, way, slot):
             return pltpu.make_async_remote_copy(
-                src_ref=full[g].at[source_at(g, slot), half_of(g, way, 1 - core)],
+                src_ref=full[g].at[at(g, slot), half_of(g, way, 1 - core)],
                 dst_ref=near[g].at[at(g, slot), half(g, way)],
                 send_sem=pair_send.at[g, way, slot],
                 recv_sem=pair_recv.at[g, way, slot],
@@ -1592,7 +1587,7 @@
         def own_load(g, way, t):
             slot = t % n if way == 0 else n - t
             return pltpu.make_async_copy(
-                full[g].at[source_at(g, slot), half_of(g, way, core)],
+                full[g].at[at(g, slot), half_of(g, way, core)],
                 own[g].at[way, t % 2],
                 own_sems.at[g, way, t % 2],
             )
@@ -1666,38 +1661,151 @@
                 gain_v[slot * 8 : slot * 8 + 1, :mine] = pair[1:2]
                 gain_v[slot * 8 : slot * 8 + 1, widths[-1] : widths[-1] + mine] = pair[0:1]
 
-        rest, gains = list(range(1, count - 1)), count - 1
+        side = me // 2 if split else 0
+        across = {"dp": team_place(n_dp, me, n_dp // 2)}
+        ends = TeamSpread(n_dp, [o_done], [o_blocks], o_end_send, o_end_recv)
+
+        def natural(slot):
+            there = device((place + n - slot) % n)
+            return pl.ds(pl.multiple_of((there["fsdp"] * n_ctx + there["ctx"]) * mine, mine), mine)
+
+        def quarter_of(whose, which):
+            return pl.ds(pl.multiple_of(whose * (outwidth // 2) + which * quarter, 128), quarter)
+
+        def piece(which):
+            return pl.ds(pl.multiple_of(which * quarter, 128), quarter)
+
+        def o_half(way):
+            return pl.ds(way * (quarter // 2), quarter // 2)
+
+        def out_load(slot):
+            return pltpu.make_async_copy(
+                out_ref.at[natural(slot), pl.ds(pl.multiple_of(core * (outwidth // 2), 128), outwidth // 2)],
+                o_own.at[slot],
+                o_load.at[slot],
+            )
+
+        def out_swap(slot, which):
+            return pltpu.make_async_remote_copy(
+                src_ref=out_ref.at[natural(slot), quarter_of(1 - core, which)],
+                dst_ref=o_near.at[slot, :, piece(which)],
+                send_sem=o_swap_send.at[slot, which],
+                recv_sem=o_swap_recv.at[slot, which],
+                device_id=sibling,
+                device_id_type=MESH,
+            )
+
+        def out_across(slot):
+            return pltpu.make_async_remote_copy(
+                src_ref=o_near.at[slot, :, piece(1 - side)],
+                dst_ref=o_x.at[slot],
+                send_sem=o_x_send.at[slot],
+                recv_sem=o_x_recv.at[slot],
+                device_id=across,
+                device_id_type=MESH,
+            )
+
+        def out_step(way, t):
+            slot = t if way == 0 else n - t
+            return pltpu.make_async_remote_copy(
+                src_ref=o_x.at[slot, :, o_half(way)] if t == 1 else o_land.at[way, t - 2],
+                dst_ref=o_land.at[way, t - 1],
+                send_sem=o_send.at[way, t],
+                recv_sem=o_recv.at[way, t],
+                device_id=ahead if way == 0 else behind,
+                device_id_type=MESH,
+            )
+
+        def out_pair(slot):
+            out_load(slot).wait()
+            for which in range(2 if split else 1):
+                out_swap(slot, which).wait_recv()
+            total = o_own[slot].astype(F32) + o_near[slot].astype(F32)
+            o_near[slot] = total.astype(BF)
+            if split:
+                out_across(slot).start()
+
+        def out_quarter(slot):
+            here = o_near[slot, :, piece(side)].astype(F32)
+            if split:
+                out_across(slot).wait_recv()
+                here = here + o_x[slot].astype(F32)
+            o_x[slot] = here.astype(BF)
+
+        def out_forward(t):
+            for slot in sorted({t, n - t}):
+                if min(slot, n - slot) == t:
+                    out_quarter(slot)
+            for way in range(2):
+                slot = t if way == 0 else n - t
+                if t > 1:
+                    out_step(way, t - 1).wait_recv()
+                    value = o_x[slot, :, o_half(way)].astype(F32) + o_land[way, t - 2].astype(F32)
+                    o_land[way, t - 2] = value.astype(BF)
+                out_step(way, t).start()
+
+        def out_finish():
+            out_quarter(0)
+            for way in range(2):
+                out_step(way, n - 1).wait_recv()
+                value = o_x[0, :, o_half(way)].astype(F32) + o_land[way, n - 2].astype(F32)
+                o_done[:, o_half(way)] = value.astype(BF)
+            ends.start(0)
+
+        gains = 1
         d_load.start()
         w_load.start()
-        for g in range(count - 1):
-            begin(g)
+        begin(0)
+        slots = []
+        for t in range(1, n // 2 + 1):
+            slots += [t] if 2 * t == n else [t, n - t]
+        slots.append(0)
+        for slot in slots:
+            out_load(slot).start()
         for t in range(1, n + 1):
-            for g in rest + [0]:
-                swaps(g, t)
-        spread.start(0)
-        jobs = [(lambda k=k: product(k)) for k in range(parts)] + [norm]
+            swaps(0, t)
+            for slot in slots[t - 1 : t]:
+                for which in range(2 if split else 1):
+                    out_swap(slot, which).start()
+        jobs = [lambda k=k: product(k) for k in range(parts)] + [norm]
+
+        def open_gains():
+            begin(gains)
+            for t in range(1, n + 1):
+                swaps(gains, t)
+
+        jobs.append(open_gains)
+        half_way = n // 2
+        small = []
         for t in range(1, n):
-            for g in rest:
-                forward(g, t)
-            if t >= 2:
-                forward(0, t - 1)
+            small.append(lambda t=t: forward(gains, t))
+            if t % 2 == 0 or n <= 4:
+                small.append(lambda t=t: out_forward(t // 2 if n > 4 else t))
+        for t in range(1, n):
+            forward(0, t)
             if t == 1:
                 d_load.wait()
                 w_load.wait()
-            for k in range((t - 1) * len(jobs) // (n - 1), t * len(jobs) // (n - 1)):
-                jobs[k]()
-        begin(gains)
-        for t in range(1, n + 1):
-            swaps(gains, t)
-        for g in rest:
-            finish(g)
+            if t <= half_way:
+                for slot in slots[(t - 1) * n // half_way : t * n // half_way]:
+                    out_pair(slot)
+                for job in jobs[(t - 1) * len(jobs) // half_way : t * len(jobs) // half_way]:
+                    job()
+                if t == half_way:
+                    spread.start(0)
+            else:
+                left, k = n - 1 - half_way, t - half_way - 1
+                for job in small[k * len(small) // left : (k + 1) * len(small) // left]:
+                    job()
+        finish(0)
+        for t in range((n - 1) // 2 + 1 if n > 4 else n, n):
+            out_forward(t)
+        finish(gains)
+        out_finish()
         spread.arrive(0)
         spread.start(1)
-        forward(0, n - 1)
-        for t in range(1, n):
-            forward(gains, t)
-        finish(0)
-        finish(gains)
+        ends.arrive(0)
+        ends.start(1)
         for k in range(len(bits)):
             for g in range(count):
                 face(g, k).wait_recv()
@@ -1712,6 +1820,22 @@
             end(g).wait_recv()
             here = pl.ds(pl.multiple_of((1 - core) * widths[g], 128), widths[g])
             outs[g][:, here] = back[g][...].astype(F32)
+        ends.arrive(1)
+        bases = [core * (outwidth // 2) + side * quarter]
+        if split:
+            bases.append(core * (outwidth // 2) + (1 - side) * quarter)
+        bases += [b + (1 - 2 * core) * (outwidth // 2) for b in bases]
+        for base, ref in zip(bases, [o_done] + list(o_blocks)):
+            wo_out[:, pl.ds(pl.multiple_of(base, 128), quarter)] = ref[...].astype(F32)
+        ends.last()
+        for slot in range(n):
+            for which in range(2 if split else 1):
+                out_swap(slot, which).wait_send()
+            if split:
+                out_across(slot).wait_send()
+        for way in range(2):
+            for t in range(1, n):
+                out_step(way, t).wait_send()
         spread.arrive(1)
         spread.last()
         dn_save.wait()
@@ -1729,9 +1853,10 @@
     groups = list(zip(rows, widths, kinds))
     out = pl.pallas_call(
         kernel,
-        in_specs=[ANY] * (count - 1 + len(sums) + 2) + [WHOLE] * 3,
-        out_specs=[WHOLE] * count + [ANY] * (len(sums) * others + 1),
+        in_specs=[ANY] * (2 + len(sums) + 2) + [WHOLE] * 3,
+        out_specs=[WHOLE] * (count + 1) + [ANY] * (len(sums) * others + 1),
         out_shape=[jax.ShapeDtypeStruct((r, 2 * w), F32) for r, w, _ in groups]
+        + [jax.ShapeDtypeStruct((mine, outwidth), F32)]
         + [jax.ShapeDtypeStruct(a.shape, BF) for a in sums for _ in range(others)]
         + [jax.ShapeDtypeStruct((span, width), F32)],
         scratch_shapes=[
@@ -1752,6 +1877,24 @@
         + [pltpu.VMEM((2, 2, r, w // 2), kind) for r, w, kind in groups]
         + [
             dma((count, 2, 2)),
+            pltpu.VMEM((n, mine, outwidth // 2), BF),
+            pltpu.VMEM((n, mine, outwidth // 2), BF),
+            pltpu.VMEM((n, mine, quarter), BF),
+            pltpu.VMEM((2, n - 1, mine, quarter // 2), BF),
+            pltpu.VMEM((mine, quarter), BF),
+        ]
+        + [pltpu.VMEM((mine, quarter), BF)] * others
+        + [
+            dma((n,)),
+            dma((n, 2)),
+            dma((n, 2)),
+            dma((n,)),
+            dma((n,)),
+            dma((2, n)),
+            dma((2, n)),
+        ]
+        + spread_scratch(1, n_dp)
+        + [
             dma((count, 2, n)),
             dma((count, 2, n)),
             dma((count, 2, n)),
@@ -1766,9 +1909,9 @@
             collective_id=1, has_side_effects=True, vmem_limit_bytes=58 * MIB
         ),
         cost_estimate=cost(0, sum(12 * n * r * w for r, w, _ in groups)),
-    )(*fulls, *sums, d_qkv, w_qkv, x, gain, d_gain)
-    blocks = [out[count + k * others : count + (k + 1) * others] for k in range(len(sums))]
-    return out[:count], blocks, out[-1]
+    )(part_qkv, part_out, *sums, d_qkv, w_qkv, x, gain, d_gain)
+    blocks = [out[3 + k * others : 3 + (k + 1) * others] for k in range(len(sums))]
+    return out[0], out[2], out[1], blocks, out[-1]
 
 
 class Ring:
@@ -1871,10 +2014,10 @@
         sizes, qkv, kv_far, d_attn, lse, seen, tables, attn_t, d_proj, normed_one, grads_b, sums_a, 4
     )
     room = max(rows, 256)
-    (grad_qkv, grad_out, grad_gain), others_b, d_input_norm = closing(
+    grad_qkv, grad_out, grad_gain, others_b, d_input_norm = closing(
         sizes,
-        (part_qkv, part_out),
-        (True, False, True),
+        part_qkv,
+        part_out,
         sums_b,
         d_qkv,
         wqkv,

time: 902 us -> 866 us (0.960)
  Pallas kernels: 837 us -> 802 us
    pallas_call x1, Pallas kernels: 146 us -> 122 us  [closing(): pl.pallas_call(kernel, in_specs=[ANY] * (2 + len(sums) + 2) + [WHOLE] * 3...]
    pallas_call x1, Pallas kernels: 160 us -> 148 us  [attend_backward(): pl.pallas_call(kernel, grid=(pairs,), in_specs=[pl.BlockSpec(memory_space...]
  transfers between devices with their start and end apart: 3 -> 3, of which waited for: 0 -> 0; matrix products, arithmetic and copies ran while one was open for 3% -> 3% of each run, Pallas kernels for 36% -> 34%
where the time goes in v4:
time: 866 us; the launch traced here: 857 us
  Pallas kernels  802 us (93%)
  other arithmetic  23.6 us (3%)
  local copies, waits for them, and re-layouts  17.3 us (2%)
    pallas_call x2, Pallas kernels, feed_forward(): pl.pallas_call(kernel, in_specs=[ANY] * len(operands), out_specs=[ANY] *...  257 us
    pallas_call x1, Pallas kernels, attend_backward(): pl.pallas_call(kernel, grid=(pairs,), in_specs=[pl.BlockSpec(memory_space...  148 us
    pallas_call x1, Pallas kernels, attend_forward(): pl.pallas_call(kernel, grid=(pairs,), in_specs=[pl.BlockSpec(memory_space...  139 us
    pallas_call x1, Pallas kernels, closing(): pl.pallas_call(kernel, in_specs=[ANY] * (2 + len(sums) + 2) + [WHOLE] * 3...  122 us
    pallas_call x1, Pallas kernels, opening(): pl.pallas_call(kernel, in_specs=[WHOLE, WHOLE, ANY, ANY, ANY, WHOLE, WHOL...  117 us
  transfers between devices with their start and end apart: 3, of which 0 were waited for; matrix products, arithmetic and copies ran while one was open for 3% of the time, Pallas kernels for 34%

profile of v4, /device:TPU:1, one launch (start us, length us, event | category | flops | bytes accessed | tf_op | source)
XLA Modules:
  0.0 856.8 jit_solution(14334463466257407537)
XLA Ops:
  0.7 1.3 constant_dynamic-slice_fusion
  7.1 1.5 pad_maximum_fusion.2
  8.6 116.7 %shard_map.188 = (bf16[512,3072]{1,0:T(8,128)(2,1)}, bf16[512,1024]{1,0:T(8,128)(2,1)}, bf16[512,2048]{1,0:T(8,128)(2,1)}, bf16[2048,3072]{1,0:T(8,128)(2,1)}, b...) custom-call(bf16[512,2048]{1,0:T(8,128)(2,1)} %bitcast.38, ...), custom_call_target="tpu_custom_call" | custom-call | flops 6442450944 | bytes 25165824 | tf_op jit(solution)/shard_map/pallas_call | solution.py:1454
  125.3 139.0 %shard_map.189 = (f32[16,8,512]{2,1,0:T(8,128)}, bf16[2048,512]{1,0:T(8,128)(2,1)}, f32[512,2048]{1,0:T(8,128)}, bf16[512,2048]{1,0:T(8,128)(2,1)}, bf16[512,204...) custom-call(s32[1]{0:T(128)} %bitcast.seen_ref, ...), custom_call_target="tpu_custom_call" | custom-call | flops 8589934592 | bytes 31457280 | tf_op jit(solution)/shard_map/pallas_call | solution.py:925
  264.3 123.9 %shard_map.190 = (bf16[512,2048]{1,0:T(8,128)(2,1)}, bf16[512,2048]{1,0:T(8,128)(2,1)}, bf16[512,2048]{1,0:T(8,128)(2,1)}, bf16[512,2048]{1,0:T(8,128)(2,1)}, bf...) custom-call(bf16[512,2048]{1,0:T(8,128)(2,1)} %get-tuple-element.78., ...), custom_call_target="tpu_custom_call" | custom-call | flops 77309411328 | bytes 41943040 | tf_op jit(solution)/shard_map/pallas_call | solution.py:793
  388.3 132.7 %shard_map.191 = (bf16[512,2048]{1,0:T(8,128)(2,1)}, bf16[512,2048]{1,0:T(8,128)(2,1)}, bf16[512,2048]{1,0:T(8,128)(2,1)}, bf16[512,2048]{1,0:T(8,128)(2,1)}, bf...) custom-call(bf16[512,2048]{1,0:T(8,128)(2,1)} %get-tuple-element.78., ...), custom_call_target="tpu_custom_call" | custom-call | flops 77309411328 | bytes 41943040 | tf_op jit(solution)/shard_map/pallas_call | solution.py:793
  521.0 5.5 collective-permute-start.1
  527.3 2.5 multiply_reduce_fusion.2
  531.8 2.4 convert_add_fusion.source
  534.2 2.0 shard_map.193
  539.3 1.2 fusion.3.refs_1_
  540.6 1.4 slice-done.1
  542.0 5.7 convolution_convert_fusion.d_ref
  547.7 3.7 add_convert_fusion.1
  551.4 147.8 %shard_map.194 = (bf16[512,3072]{1,0:T(8,128)(2,1)}, bf16[2048,2048]{1,0:T(8,128)(2,1)}, bf16[2048,3072]{1,0:T(8,128)(2,1)}, bf16[256,1536]{1,0:T(8,128)(2,1)}, ...) custom-call(s32[1]{0:T(128)} %bitcast.seen_ref, ...), custom_call_target="tpu_custom_call" | custom-call | flops 21474836480 | bytes 31457280 | tf_op jit(solution)/shard_map/pallas_call | solution.py:1137
  700.5 122.1 %shard_map.195 = (f32[256,3072]{1,0:T(8,128)}, f32[8,512]{1,0:T(8,128)}, f32[256,2048]{1,0:T(8,128)}, bf16[256,1536]{1,0:T(8,128)(2,1)}, bf16[256,1536]{1,0:T(8,...) custom-call(bf16[2048,3072]{1,0:T(8,128)(2,1)} %get-tuple-element.11, ...), custom_call_target="tpu_custom_call" | custom-call | bytes 37945344 | tf_op jit(solution)/shard_map/pallas_call | solution.py:1854
  823.2 15.7 %shard_map.196 = (f32[256,16384]{1,0:T(8,128)}, f32[256,8192]{1,0:T(8,128)}) custom-call(s32[16]{0:T(128)} %stack.68.refs_0_, bf16[256,1536]{1,0:T(8,128)(2,1)} %get-tuple-element.110.refs_5_.refs_1_, bf16[256,1536]{1,0:T(8,128)(2,1)} %get-tuple-element.122.refs_2_, bf16[256,1536]{1,0:T(8,128)(2,1)} %get-tuple-element.123.refs_3_, ...), custom_call_target="tpu_custom_call" | custom-call | bytes 37748736 | tf_op jit(solution)/shard_map/pallas_call | solution.py:188
  838.9 1.3 fusion.4
  840.2 4.2 convert_add_fusion.1.source
  844.5 1.6 shard_map.192
  846.6 1.3 copy-done.3
  847.9 4.6 add_bitcast_fusion
  852.5 1.7 copy.23
  855.3 1.3 copy.24
  (55 shorter events, 12.5 us)
Async XLA Ops:
  520.9 8.9 %copy-start.12 = (s32[8]{0:T(128)S(1)}, s32[8]{0:T(128)}, u32[]{:S(2)}) copy-start(s32[8]{0:T(128)} %constant.81.clone) | copy-start | bytes 100
  521.0 9.5 %copy-start.11 = (s32[8]{0:T(128)S(1)}, s32[8]{0:T(128)}, u32[]{:S(2)}) copy-start(s32[8]{0:T(128)} %constant.85) | copy-start | bytes 100
  521.0 10.8 %copy-start.10 = (bf16[512,2048]{1,0:T(8,128)(2,1)S(1)}, bf16[512,2048]{1,0:T(8,128)(2,1)}, u32[]{:S(2)}) copy-start(bf16[512,2048]{1,0:T(8,128)(2,1)} %get-tuple-element.103) | copy-start | bytes 6291460
  521.0 26.7 %collective-permute-start.1 = (bf16[512,2048]{1,0:T(8,128)(2,1)}, bf16[512,2048]{1,0:T(8,128)(2,1)}, u32[]{:S(2)}, u32[]{:S(2)}) collective-permute-start(bf16[512,2048]{1,0:T(8,128)(2,1)} %get-tuple-element.102), channel_id=1, source_target_pairs={{0,8},{8,0},{16,24},{24,16},{1,9},{9,1},{17,25},{25,17},{2,10},{10... | collective-permute-start | bytes 6291464 | tf_op jit(solution)/shard_map/ppermute | solution.py:1953
  526.5 313.7 %collective-permute-start = (bf16[512,2048]{1,0:T(8,128)(2,1)}, bf16[512,2048]{1,0:T(8,128)(2,1)}, u32[]{:S(2)}, u32[]{:S(2)}) collective-permute-start(bf16[512,2048]{1,0:T(8,128)(2,1)} %get-tuple-element.100), channel_id=1, source_target_pairs={{0,8},{8,0},{16,24},{24,16},{1,9},{9,1},{17,25},{25,17},{2,10},{10... | collective-permute-start | bytes 6291464 | tf_op jit(solution)/shard_map/ppermute | solution.py:1953
  534.2 2.2 copy-start.2
  536.2 2.1 copy-start
  536.4 2.9 copy-start.4
  536.4 4.2 slice-start
  539.3 2.7 slice-start.1
  542.0 5.7 copy-start.8
  542.0 5.7 copy-start.7
  551.4 288.8 %collective-permute-start.2 = (bf16[512,2048]{1,0:T(8,128)(2,1)}, bf16[512,2048]{1,0:T(8,128)(2,1)}, u32[]{:S(2)}, u32[]{:S(2)}) collective-permute-start(bf16[512,2048]{1,0:T(8,128)(2,1)} %add_convert_fusion.1), channel_id=1, source_target_pairs={{0,16},{8,24},{16,0},{24,8},{1,17},{9,25},{17,1},{25,9},{2,18},{10... | collective-permute-start | bytes 6291464 | tf_op jit(solution)/shard_map/ppermute | solution.py:1953
  840.2 5.8 copy-start.5
  844.4 2.2 copy-start.1
  844.5 3.5 copy-start.3
  847.9 4.6 copy-start.6
  852.5 2.7 copy-start.9

commit v5 on v4

--- a/solution.py
+++ b/solution.py
@@ -465,9 +465,11 @@
                 )
 
     def start(self, stage):
-        if stage < len(self.stages):
-            for copy in self.copies(stage):
-                copy.start()
+        for later in range(stage, len(self.stages) if stage == 0 else min(stage + 1, len(self.stages))):
+            held = self.stages[later][0]
+            for k, copy in enumerate(self.copies(later)):
+                if (k % held == 0) == (stage == 0):
+                    copy.start()
 
     def arrive(self, stage):
         if stage < len(self.stages):
@@ -832,7 +834,7 @@
             return out
 
         wo_ref, dy_ref, gu_ref, down_ref = take(4)
-        lse_ref, attn_out, hidden_out, normed_out = take(4)
+        lse_ref, scale_ref, attn_out, hidden_out, normed_out = take(5)
         x_blocks, dy_blocks, ring_outs = take(others), take(others), take(2)
         attn_v, wo_v, hidden_v, normed_v, load_sem, save_sems = take(6)
         dy_send, dy_recv, x_send, x_recv = take(4)
@@ -893,6 +895,7 @@
                 hidden_v[:, lanes] = hidden
                 square = square + jnp.sum(hidden * hidden, -1, keepdims=True)
             scale = lax.rsqrt(square / width + EPS)
+            scale_ref[...] = jnp.broadcast_to(scale, (span, 128))
             place, device = ring_place(n_fsdp)
             for slot in range(n):
                 there = device((place + n - slot) % n)
@@ -936,9 +939,11 @@
             pl.BlockSpec(gains.shape, lambda i: (0, 0, 0)),
         ]
         + [ANY] * 4,
-        out_specs=[pl.BlockSpec((1, 8, span), lambda i: (i, 0, 0))] + [ANY] * (5 + 2 * others),
+        out_specs=[pl.BlockSpec((1, 8, span), lambda i: (i, 0, 0)), pl.BlockSpec((span, 128), lambda i: (0, 0))]
+        + [ANY] * (5 + 2 * others),
         out_shape=[
             jax.ShapeDtypeStruct((pairs, 8, span), F32),
+            jax.ShapeDtypeStruct((span, 128), F32),
             jax.ShapeDtypeStruct((qwidth, span), BF),
             jax.ShapeDtypeStruct((span, width), F32),
         ]
@@ -960,8 +965,9 @@
         ),
         cost_estimate=cost(pairs * 2 * span * (span + far) * 128 * 4, 30 * MIB),
     )(seen, qkv, qkv, qkv, kv_far, kv_far, x, gains, w_out, dy, w_gate_up, w_down)
-    lse, attn, hidden, normed = out[:4]
-    return attn, lse, hidden, normed, out[4 : 4 + others], out[4 + others : 4 + 2 * others], out[4 + 2 * others :]
+    lse, scale, attn, hidden, normed = out[:5]
+    blocks = out[5 : 5 + others], out[5 + others : 5 + 2 * others]
+    return attn, lse, hidden, scale[:, :1], normed, *blocks, out[5 + 2 * others :]
 
 
 def attend_backward(sizes, qkv, kv_far, d_attn, lse, seen, tables, attn_t, d_proj, normed, ring_parts, sums, ident):
@@ -1117,12 +1123,10 @@
                 dqkv_v[:, qwidth + at : qwidth + at + 128] = piece.astype(BF)
             save = pltpu.make_async_copy(dqkv_v, dqkv_out, save_sem)
             save.start()
-            lax.fori_loop(early + 2, 2 * n - 1, lambda u, c: (ring.step(u), c)[1], 0)
+            lax.fori_loop(early + 2, 2 * n, lambda u, c: (ring.step(u), c)[1], 0)
             spread.arrive(0)
             spread.start(1)
             product(gq_out, qkvwidth, lambda at: dot_tn(normed_v[:, at], dqkv_v[...]))
-            if early + 2 < 2 * n:
-                ring.step(2 * n - 1)
             spread.arrive(1)
             ring.last()
             spread.last()
@@ -1987,7 +1991,7 @@
     qkv, kv_far, normed_one, wqkv, wout, gains, dy = opening(
         sizes, tokens, grad_y, w_qkv, w_out, gains, tables
     )
-    attn_t, lse, hidden_one, normed_two, x_others, dy_others, weights_a = attend_forward(
+    attn_t, lse, hidden_one, scale_two, normed_two, x_others, dy_others, weights_a = attend_forward(
         sizes, tokens, qkv, kv_far, seen, wout, gains, dy, w_gate_up, w_down
     )
     xs = [normed_two] + list(x_others)
@@ -1995,7 +1999,6 @@
     gains = gains[:, :2][(ring.rank - jnp.array(ring.place, jnp.int32)) % n]
     gain_one = gains[:, 0].reshape(-1).astype(F32)
     gain_two = gains[:, 1].reshape(-1).astype(F32)
-    scale_two = inv_rms(hidden_one)
 
     y, dn, grads_a, weights_b = feed_forward(
         sizes, xs, dys, [[w] for w in weights_a], None, (w_gate_up, w_down), False, 2

time: 866 us -> 864 us (level)
  transfers between devices with their start and end apart: 3 -> 3, of which waited for: 0 -> 0; matrix products, arithmetic and copies ran while one was open for 3% -> 2% of each run, Pallas kernels for 34% -> 34%
where the time goes in v5:
time: 864 us; the launch traced here: 855 us
  Pallas kernels  801 us (93%)
  other arithmetic  21.8 us (3%)
  local copies, waits for them, and re-layouts  17.3 us (2%)
    pallas_call x2, Pallas kernels, feed_forward(): pl.pallas_call(kernel, in_specs=[ANY] * len(operands), out_specs=[ANY] *...  257 us
    pallas_call x1, Pallas kernels, attend_backward(): pl.pallas_call(kernel, grid=(pairs,), in_specs=[pl.BlockSpec(memory_space...  148 us
    pallas_call x1, Pallas kernels, attend_forward(): pl.pallas_call(kernel, grid=(pairs,), in_specs=[pl.BlockSpec(memory_space...  139 us
    pallas_call x1, Pallas kernels, closing(): pl.pallas_call(kernel, in_specs=[ANY] * (2 + len(sums) + 2) + [WHOLE] * 3...  122 us
    pallas_call x1, Pallas kernels, opening(): pl.pallas_call(kernel, in_specs=[WHOLE, WHOLE, ANY, ANY, ANY, WHOLE, WHOL...  117 us
  transfers between devices with their start and end apart: 3, of which 0 were waited for; matrix products, arithmetic and copies ran while one was open for 2% of the time, Pallas kernels for 34%

profile of v5, /device:TPU:1, one launch (start us, length us, event | category | flops | bytes accessed | tf_op | source)
XLA Modules:
  0.0 854.7 jit_solution(7755921572924903785)
XLA Ops:
  0.7 1.3 constant_dynamic-slice_fusion
  7.0 1.5 pad_maximum_fusion.2
  8.6 116.6 %shard_map.188 = (bf16[512,3072]{1,0:T(8,128)(2,1)}, bf16[512,1024]{1,0:T(8,128)(2,1)}, bf16[512,2048]{1,0:T(8,128)(2,1)}, bf16[2048,3072]{1,0:T(8,128)(2,1)}, b...) custom-call(bf16[512,2048]{1,0:T(8,128)(2,1)} %bitcast.38, ...), custom_call_target="tpu_custom_call" | custom-call | flops 6442450944 | bytes 25165824 | tf_op jit(solution)/shard_map/pallas_call | solution.py:1458
  125.2 139.2 %shard_map.189 = (f32[16,8,512]{2,1,0:T(8,128)}, f32[512,128]{1,0:T(8,128)}, bf16[2048,512]{1,0:T(8,128)(2,1)}, f32[512,2048]{1,0:T(8,128)}, bf16[512,2048]{1,0:...) custom-call(s32[1]{0:T(128)} %bitcast.seen_ref, ...), custom_call_target="tpu_custom_call" | custom-call | flops 8589934592 | bytes 31457280 | tf_op jit(solution)/shard_map/pallas_call | solution.py:928
  264.4 124.0 %shard_map.190 = (bf16[512,2048]{1,0:T(8,128)(2,1)}, bf16[512,2048]{1,0:T(8,128)(2,1)}, bf16[512,2048]{1,0:T(8,128)(2,1)}, bf16[512,2048]{1,0:T(8,128)(2,1)}, bf...) custom-call(bf16[512,2048]{1,0:T(8,128)(2,1)} %get-tuple-element.79., ...), custom_call_target="tpu_custom_call" | custom-call | flops 77309411328 | bytes 41943040 | tf_op jit(solution)/shard_map/pallas_call | solution.py:795
  388.5 132.6 %shard_map.191 = (bf16[512,2048]{1,0:T(8,128)(2,1)}, bf16[512,2048]{1,0:T(8,128)(2,1)}, bf16[512,2048]{1,0:T(8,128)(2,1)}, bf16[512,2048]{1,0:T(8,128)(2,1)}, bf...) custom-call(bf16[512,2048]{1,0:T(8,128)(2,1)} %get-tuple-element.79., ...), custom_call_target="tpu_custom_call" | custom-call | flops 77309411328 | bytes 41943040 | tf_op jit(solution)/shard_map/pallas_call | solution.py:795
  521.1 5.5 collective-permute-start
  529.5 3.0 convert_add_fusion.source
  532.6 1.8 shard_map.193
  536.3 1.1 copy-done.4
  537.4 1.3 fusion.3.refs_1_
  538.8 1.3 slice-done.1
  540.1 5.7 convolution_convert_fusion.d_ref
  545.8 3.7 add_convert_fusion.1
  549.5 147.9 %shard_map.194 = (bf16[512,3072]{1,0:T(8,128)(2,1)}, bf16[2048,2048]{1,0:T(8,128)(2,1)}, bf16[2048,3072]{1,0:T(8,128)(2,1)}, bf16[256,1536]{1,0:T(8,128)(2,1)}, ...) custom-call(s32[1]{0:T(128)} %bitcast.seen_ref, ...), custom_call_target="tpu_custom_call" | custom-call | flops 21474836480 | bytes 31457280 | tf_op jit(solution)/shard_map/pallas_call | solution.py:1141
  698.7 121.6 %shard_map.195 = (f32[256,3072]{1,0:T(8,128)}, f32[8,512]{1,0:T(8,128)}, f32[256,2048]{1,0:T(8,128)}, bf16[256,1536]{1,0:T(8,128)(2,1)}, bf16[256,1536]{1,0:T(8,...) custom-call(bf16[2048,3072]{1,0:T(8,128)(2,1)} %get-tuple-element.11, ...), custom_call_target="tpu_custom_call" | custom-call | bytes 37945344 | tf_op jit(solution)/shard_map/pallas_call | solution.py:1858
  820.9 15.7 %shard_map.196 = (f32[256,16384]{1,0:T(8,128)}, f32[256,8192]{1,0:T(8,128)}) custom-call(s32[16]{0:T(128)} %stack.68.refs_0_, bf16[256,1536]{1,0:T(8,128)(2,1)} %get-tuple-element.112.refs_5_.refs_1_, bf16[256,1536]{1,0:T(8,128)(2,1)} %get-tuple-element.124.refs_2_, bf16[256,1536]{1,0:T(8,128)(2,1)} %get-tuple-element.125.refs_3_, ...), custom_call_target="tpu_custom_call" | custom-call | bytes 37748736 | tf_op jit(solution)/shard_map/pallas_call | solution.py:188
  836.7 1.3 fusion.4
  838.0 4.2 convert_add_fusion.1.source
  842.2 1.6 shard_map.192
  844.4 1.3 copy-done.3
  845.7 4.6 add_bitcast_fusion
  850.3 1.7 copy.23
  853.0 1.3 copy.24
  (54 shorter events, 11.5 us)
Async XLA Ops:
  388.4 139.1 %copy-start.12 = (s32[8]{0:T(128)S(1)}, s32[8]{0:T(128)}, u32[]{:S(2)}) copy-start(s32[8]{0:T(128)} %constant.78.clone) | copy-start | bytes 100
  388.5 139.6 %copy-start.11 = (s32[8]{0:T(128)S(1)}, s32[8]{0:T(128)}, u32[]{:S(2)}) copy-start(s32[8]{0:T(128)} %constant.82) | copy-start | bytes 100
  388.5 140.9 %copy-start.10 = (f32[512,128]{1,0:T(8,128)S(1)}, f32[512,128]{1,0:T(8,128)}, u32[]{:S(2)}) copy-start(f32[512,128]{1,0:T(8,128)} %get-tuple-element.104) | copy-start | bytes 786436
  521.1 316.8 %collective-permute-start = (bf16[512,2048]{1,0:T(8,128)(2,1)}, bf16[512,2048]{1,0:T(8,128)(2,1)}, u32[]{:S(2)}, u32[]{:S(2)}) collective-permute-start(bf16[512,2048]{1,0:T(8,128)(2,1)} %get-tuple-element.101), channel_id=1, source_target_pairs={{0,8},{8,0},{16,24},{24,16},{1,9},{9,1},{17,25},{25,17},{2,10},{10... | collective-permute-start | bytes 6291464 | tf_op jit(solution)/shard_map/ppermute | solution.py:1957
  526.6 19.2 %collective-permute-start.1 = (bf16[512,2048]{1,0:T(8,128)(2,1)}, bf16[512,2048]{1,0:T(8,128)(2,1)}, u32[]{:S(2)}, u32[]{:S(2)}) collective-permute-start(bf16[512,2048]{1,0:T(8,128)(2,1)} %get-tuple-element.103), channel_id=1, source_target_pairs={{0,8},{8,0},{16,24},{24,16},{1,9},{9,1},{17,25},{25,17},{2,10},{10... | collective-permute-start | bytes 6291464 | tf_op jit(solution)/shard_map/ppermute | solution.py:1957
  532.6 2.2 copy-start.2
  534.3 2.0 copy-start
  534.7 2.7 copy-start.4
  534.7 4.0 slice-start
  537.4 2.7 slice-start.1
  540.1 5.7 copy-start.8
  540.1 5.7 copy-start.7
  549.5 288.4 %collective-permute-start.2 = (bf16[512,2048]{1,0:T(8,128)(2,1)}, bf16[512,2048]{1,0:T(8,128)(2,1)}, u32[]{:S(2)}, u32[]{:S(2)}) collective-permute-start(bf16[512,2048]{1,0:T(8,128)(2,1)} %add_convert_fusion.1), channel_id=1, source_target_pairs={{0,16},{8,24},{16,0},{24,8},{1,17},{9,25},{17,1},{25,9},{2,18},{10... | collective-permute-start | bytes 6291464 | tf_op jit(solution)/shard_map/ppermute | solution.py:1957
  838.0 5.8 copy-start.5
  842.2 2.2 copy-start.1
  842.2 3.5 copy-start.3
  845.7 4.6 copy-start.6
  850.3 2.7 copy-start.9

commit v6 on v5

--- a/solution.py
+++ b/solution.py
@@ -146,6 +146,7 @@
 def place_grads(pieces, columns, sub, ffwidth):
     rows = pieces[0].shape[0]
     count = len(pieces)
+    depth = 4
 
     def kernel(*refs):
         where = refs[0]
@@ -153,35 +154,36 @@
         gu_ref, down_ref, took, gave, in_sems, out_sems = refs[1 + count :]
 
         def read(k):
-            return pltpu.make_async_copy(sources[k], took.at[k % 2], in_sems.at[k % 2])
+            return pltpu.make_async_copy(sources[k], took.at[k % depth], in_sems.at[k % depth])
 
         def writes(k):
             at = pl.multiple_of(where[k], 128)
-            here = gave.at[k % 2]
+            here = gave.at[k % depth]
             return (
                 pltpu.make_async_copy(
-                    here.at[:, pl.ds(0, sub)], gu_ref.at[:, pl.ds(at, sub)], out_sems.at[k % 2, 0]
+                    here.at[:, pl.ds(0, sub)], gu_ref.at[:, pl.ds(at, sub)], out_sems.at[k % depth, 0]
                 ),
                 pltpu.make_async_copy(
-                    here.at[:, pl.ds(sub, sub)], gu_ref.at[:, pl.ds(at + ffwidth, sub)], out_sems.at[k % 2, 1]
+                    here.at[:, pl.ds(sub, sub)], gu_ref.at[:, pl.ds(at + ffwidth, sub)], out_sems.at[k % depth, 1]
                 ),
                 pltpu.make_async_copy(
-                    here.at[:, pl.ds(2 * sub, sub)], down_ref.at[:, pl.ds(at, sub)], out_sems.at[k % 2, 2]
+                    here.at[:, pl.ds(2 * sub, sub)], down_ref.at[:, pl.ds(at, sub)], out_sems.at[k % depth, 2]
                 ),
             )
 
-        read(0).start()
+        for k in range(min(depth - 1, count)):
+            read(k).start()
         for k in range(count):
-            if k + 1 < count:
-                read(k + 1).start()
+            if k + depth - 1 < count:
+                read(k + depth - 1).start()
             read(k).wait()
-            if k >= 2:
-                for copy in writes(k - 2):
+            if k >= depth:
+                for copy in writes(k - depth):
                     copy.wait()
-            gave[k % 2] = took[k % 2].astype(F32)
+            gave[k % depth] = took[k % depth].astype(F32)
             for copy in writes(k):
                 copy.start()
-        for k in range(max(0, count - 2), count):
+        for k in range(max(0, count - depth), count):
             for copy in writes(k):
                 copy.wait()
 
@@ -194,10 +196,10 @@
             jax.ShapeDtypeStruct((rows, ffwidth), F32),
         ],
         scratch_shapes=[
-            pltpu.VMEM((2, rows, 3 * sub), BF),
-            pltpu.VMEM((2, rows, 3 * sub), F32),
-            pltpu.SemaphoreType.DMA((2,)),
-            pltpu.SemaphoreType.DMA((2, 3)),
+            pltpu.VMEM((depth, rows, 3 * sub), BF),
+            pltpu.VMEM((depth, rows, 3 * sub), F32),
+            pltpu.SemaphoreType.DMA((depth,)),
+            pltpu.SemaphoreType.DMA((depth, 3)),
         ],
         compiler_params=params(60),
         cost_estimate=cost(0, rows * ffwidth * 18),
@@ -822,6 +824,7 @@
     tile = min(span, 256)
     wide = 3 * (w_down.shape[1] // n_dp // SUBS)
     early = max(0, 3 * (n - 2) // 7)
+    paced = pairs - 2 if pairs * early // max(1, pairs - 2) == early else pairs
     others = n_dp - 1
     chunk = min(512, width)
 
@@ -854,8 +857,8 @@
             load.start()
 
         lax.fori_loop(
-            2 + group * early // pairs,
-            2 + (group + 1) * early // pairs,
+            2 + group * early // paced,
+            2 + (group + 1) * early // paced,
             lambda t, c: (ring.tick(t), c)[1],
             0,
         )

time: 864 us -> 864 us (level)
  transfers between devices with their start and end apart: 3 -> 3, of which waited for: 0 -> 0; matrix products, arithmetic and copies ran while one was open for 2% -> 2% of each run, Pallas kernels for 34% -> 33%
where the time goes in v6:
time: 864 us; the launch traced here: 855 us
  Pallas kernels  801 us (93%)
  other arithmetic  21.8 us (3%)
  local copies, waits for them, and re-layouts  17.3 us (2%)
    pallas_call x2, Pallas kernels, feed_forward(): pl.pallas_call(kernel, in_specs=[ANY] * len(operands), out_specs=[ANY] *...  257 us
    pallas_call x1, Pallas kernels, attend_backward(): pl.pallas_call(kernel, grid=(pairs,), in_specs=[pl.BlockSpec(memory_space...  148 us
    pallas_call x1, Pallas kernels, attend_forward(): pl.pallas_call(kernel, grid=(pairs,), in_specs=[pl.BlockSpec(memory_space...  141 us
    pallas_call x1, Pallas kernels, closing(): pl.pallas_call(kernel, in_specs=[ANY] * (2 + len(sums) + 2) + [WHOLE] * 3...  122 us
    pallas_call x1, Pallas kernels, opening(): pl.pallas_call(kernel, in_specs=[WHOLE, WHOLE, ANY, ANY, ANY, WHOLE, WHOL...  117 us
  transfers between devices with their start and end apart: 3, of which 0 were waited for; matrix products, arithmetic and copies ran while one was open for 2% of the time, Pallas kernels for 33%

profile of v6, /device:TPU:1, one launch (start us, length us, event | category | flops | bytes accessed | tf_op | source)
XLA Modules:
  0.0 854.8 jit_solution(7917513724466830692)
XLA Ops:
  0.7 1.3 constant_dynamic-slice_fusion
  7.0 1.5 pad_maximum_fusion.2
  8.6 116.6 %shard_map.188 = (bf16[512,3072]{1,0:T(8,128)(2,1)}, bf16[512,1024]{1,0:T(8,128)(2,1)}, bf16[512,2048]{1,0:T(8,128)(2,1)}, bf16[2048,3072]{1,0:T(8,128)(2,1)}, b...) custom-call(bf16[512,2048]{1,0:T(8,128)(2,1)} %bitcast.38, ...), custom_call_target="tpu_custom_call" | custom-call | flops 6442450944 | bytes 25165824 | tf_op jit(solution)/shard_map/pallas_call | solution.py:1461
  125.2 141.2 %shard_map.189 = (f32[16,8,512]{2,1,0:T(8,128)}, f32[512,128]{1,0:T(8,128)}, bf16[2048,512]{1,0:T(8,128)(2,1)}, f32[512,2048]{1,0:T(8,128)}, bf16[512,2048]{1,0:...) custom-call(s32[1]{0:T(128)} %bitcast.seen_ref, ...), custom_call_target="tpu_custom_call" | custom-call | flops 8589934592 | bytes 31457280 | tf_op jit(solution)/shard_map/pallas_call | solution.py:931
  266.4 124.6 %shard_map.190 = (bf16[512,2048]{1,0:T(8,128)(2,1)}, bf16[512,2048]{1,0:T(8,128)(2,1)}, bf16[512,2048]{1,0:T(8,128)(2,1)}, bf16[512,2048]{1,0:T(8,128)(2,1)}, bf...) custom-call(bf16[512,2048]{1,0:T(8,128)(2,1)} %get-tuple-element.79., ...), custom_call_target="tpu_custom_call" | custom-call | flops 77309411328 | bytes 41943040 | tf_op jit(solution)/shard_map/pallas_call | solution.py:797
  391.1 132.2 %shard_map.191 = (bf16[512,2048]{1,0:T(8,128)(2,1)}, bf16[512,2048]{1,0:T(8,128)(2,1)}, bf16[512,2048]{1,0:T(8,128)(2,1)}, bf16[512,2048]{1,0:T(8,128)(2,1)}, bf...) custom-call(bf16[512,2048]{1,0:T(8,128)(2,1)} %get-tuple-element.79., ...), custom_call_target="tpu_custom_call" | custom-call | flops 77309411328 | bytes 41943040 | tf_op jit(solution)/shard_map/pallas_call | solution.py:797
  523.3 5.5 collective-permute-start
  531.7 3.0 convert_add_fusion.source
  534.7 1.8 shard_map.193
  538.5 1.1 copy-done.4
  539.6 1.3 fusion.3.refs_1_
  540.9 1.3 slice-done.1
  542.3 5.7 convolution_convert_fusion.d_ref
  548.0 3.7 add_convert_fusion.1
  551.7 147.9 %shard_map.194 = (bf16[512,3072]{1,0:T(8,128)(2,1)}, bf16[2048,2048]{1,0:T(8,128)(2,1)}, bf16[2048,3072]{1,0:T(8,128)(2,1)}, bf16[256,1536]{1,0:T(8,128)(2,1)}, ...) custom-call(s32[1]{0:T(128)} %bitcast.seen_ref, ...), custom_call_target="tpu_custom_call" | custom-call | flops 21474836480 | bytes 31457280 | tf_op jit(solution)/shard_map/pallas_call | solution.py:1144
  700.9 121.6 %shard_map.195 = (f32[256,3072]{1,0:T(8,128)}, f32[8,512]{1,0:T(8,128)}, f32[256,2048]{1,0:T(8,128)}, bf16[256,1536]{1,0:T(8,128)(2,1)}, bf16[256,1536]{1,0:T(8,...) custom-call(bf16[2048,3072]{1,0:T(8,128)(2,1)} %get-tuple-element.11, ...), custom_call_target="tpu_custom_call" | custom-call | bytes 37945344 | tf_op jit(solution)/shard_map/pallas_call | solution.py:1861
  823.1 13.6 %shard_map.196 = (f32[256,16384]{1,0:T(8,128)}, f32[256,8192]{1,0:T(8,128)}) custom-call(s32[16]{0:T(128)} %stack.68.refs_0_, bf16[256,1536]{1,0:T(8,128)(2,1)} %get-tuple-element.112.refs_5_.refs_1_, bf16[256,1536]{1,0:T(8,128)(2,1)} %get-tuple-element.124.refs_2_, bf16[256,1536]{1,0:T(8,128)(2,1)} %get-tuple-element.125.refs_3_, ...), custom_call_target="tpu_custom_call" | custom-call | bytes 37748736 | tf_op jit(solution)/shard_map/pallas_call | solution.py:190
  836.7 1.3 fusion.4
  838.0 4.2 convert_add_fusion.1.source
  842.3 1.6 shard_map.192
  844.4 1.3 copy-done.3
  845.7 4.6 add_bitcast_fusion
  850.3 1.7 copy.23
  853.0 1.3 copy.24
  (54 shorter events, 11.5 us)
Async XLA Ops:
  391.1 138.6 %copy-start.12 = (s32[8]{0:T(128)S(1)}, s32[8]{0:T(128)}, u32[]{:S(2)}) copy-start(s32[8]{0:T(128)} %constant.78.clone) | copy-start | bytes 100
  391.1 139.1 %copy-start.11 = (s32[8]{0:T(128)S(1)}, s32[8]{0:T(128)}, u32[]{:S(2)}) copy-start(s32[8]{0:T(128)} %constant.82) | copy-start | bytes 100
  391.1 140.4 %copy-start.10 = (f32[512,128]{1,0:T(8,128)S(1)}, f32[512,128]{1,0:T(8,128)}, u32[]{:S(2)}) copy-start(f32[512,128]{1,0:T(8,128)} %get-tuple-element.104) | copy-start | bytes 786436
  523.3 314.7 %collective-permute-start = (bf16[512,2048]{1,0:T(8,128)(2,1)}, bf16[512,2048]{1,0:T(8,128)(2,1)}, u32[]{:S(2)}, u32[]{:S(2)}) collective-permute-start(bf16[512,2048]{1,0:T(8,128)(2,1)} %get-tuple-element.101), channel_id=1, source_target_pairs={{0,8},{8,0},{16,24},{24,16},{1,9},{9,1},{17,25},{25,17},{2,10},{10... | collective-permute-start | bytes 6291464 | tf_op jit(solution)/shard_map/ppermute | solution.py:1960
  528.8 19.2 %collective-permute-start.1 = (bf16[512,2048]{1,0:T(8,128)(2,1)}, bf16[512,2048]{1,0:T(8,128)(2,1)}, u32[]{:S(2)}, u32[]{:S(2)}) collective-permute-start(bf16[512,2048]{1,0:T(8,128)(2,1)} %get-tuple-element.103), channel_id=1, source_target_pairs={{0,8},{8,0},{16,24},{24,16},{1,9},{9,1},{17,25},{25,17},{2,10},{10... | collective-permute-start | bytes 6291464 | tf_op jit(solution)/shard_map/ppermute | solution.py:1960
  534.7 2.2 copy-start.2
  536.5 2.0 copy-start
  536.9 2.7 copy-start.4
  536.9 4.0 slice-start
  539.6 2.7 slice-start.1
  542.3 5.7 copy-start.8
  542.3 5.7 copy-start.7
  551.7 286.3 %collective-permute-start.2 = (bf16[512,2048]{1,0:T(8,128)(2,1)}, bf16[512,2048]{1,0:T(8,128)(2,1)}, u32[]{:S(2)}, u32[]{:S(2)}) collective-permute-start(bf16[512,2048]{1,0:T(8,128)(2,1)} %add_convert_fusion.1), channel_id=1, source_target_pairs={{0,16},{8,24},{16,0},{24,8},{1,17},{9,25},{17,1},{25,9},{2,18},{10... | collective-permute-start | bytes 6291464 | tf_op jit(solution)/shard_map/ppermute | solution.py:1960
  838.0 5.8 copy-start.5
  842.2 2.2 copy-start.1
  842.3 3.5 copy-start.3
  845.7 4.6 copy-start.6
  850.3 2.7 copy-start.9
